TPU v7x, 512 devices: a whole 4x4x16 slice. The times are simulated.
512 devices in a mesh: tm: 16 (over z_lo, core), space: 32 (over z_hi, y, x).
Axes of the slice: x: 4, y: 4, z: 16 (z_hi: 2, z_lo: 8; z = z_hi * 8 + z_lo), core: 2. Of those that a mesh axis runs over, the one named last changes fastest.
Arguments:
- forcing: float32 [2, 16, 8, 32, 4096], P(None, 'tm', None, None, 'space'), may hold values from -6 to 6
- wind_x: float32 [16, 2, 8, 32, 4096], P('tm', None, None, None, 'space'), may hold values from -1 to 1
- wind_y: float32 [16, 2, 8, 32, 4096], P('tm', None, None, None, 'space'), may hold values from -1 to 1
Outputs:
- adjoint: float32 [2, 16, 8, 32, 4096], P(None, 'tm', None, None, 'space')
All inputs are finite; a program needn't handle non-finite values.
Results may differ from a plain program's by a relative error of at most 0.00015.
Values sent between devices are 32-bit elements; how exact they have to be, the bound alone decides.
No kernel may reach another device: no remote copies, remote signals or barrier semaphores. Data moves between devices by JAX's collectives and lax.ppermute only.
A program may use at most 64 MiB of HBM per device.

v0:
```python
import jax
import jax.numpy as jnp
import numpy as np
from jax import lax
from jax.sharding import PartitionSpec as P

time_step = 0.01
lobatto_points = [
    -1.0,
    -0.8717401485096066,
    -0.5917001814331423,
    -0.20929921790247888,
    0.20929921790247888,
    0.5917001814331423,
    0.8717401485096066,
    1.0,
]


def with_halo(block, sides, width):
    for axis, dim in sides:
        count = lax.axis_size(axis)
        forward = [(i, i + 1) for i in range(count - 1)]
        forward.append((count - 1, 0))
        backward = [(target, source) for source, target in forward]
        low = lax.ppermute(
            lax.slice_in_dim(block, block.shape[dim] - width, None, axis=dim), axis, forward
        )
        high = lax.ppermute(lax.slice_in_dim(block, 0, width, axis=dim), axis, backward)
        block = jnp.concatenate([low, block, high], axis=dim)
    return block


def shifted(block, axis, distance):
    devices = range(lax.axis_size(axis))
    route = [(i - distance, i) for i in devices if i - distance in devices]
    return lax.ppermute(block, axis, route)


def legendre_seven(point):
    before = 1.0
    current = point
    for order in range(1, 7):
        before, current = (
            current,
            ((2 * order + 1) * point * current - order * before) / (order + 1),
        )
    return current


def lobatto_table():
    values = [legendre_seven(point) for point in lobatto_points]
    table = np.zeros((8, 8))
    for row_index in range(8):
        for col_index in range(8):
            if row_index != col_index:
                table[row_index, col_index] = values[row_index] / (
                    values[col_index] * (lobatto_points[row_index] - lobatto_points[col_index])
                )
    table[0, 0] = -14.0
    table[7, 7] = 14.0
    return table.astype(np.float32)


def average_pairs(values, west_edge, east_edge):
    shaped = values.reshape(values.shape[:-1] + (-1, 8))
    firsts = shaped[..., :, 0]
    lasts = shaped[..., :, 7]
    before = jnp.concatenate([west_edge[..., None], lasts[..., :-1]], -1)
    after = jnp.concatenate([firsts[..., 1:], east_edge[..., None]], -1)
    shaped = shaped.at[..., :, 0].set(0.5 * (firsts + before))
    shaped = shaped.at[..., :, 7].set(0.5 * (lasts + after))
    return shaped.reshape(values.shape)


def block_matrix(count):
    return jnp.asarray(np.kron(np.eye(count // 8, dtype=np.float32), lobatto_table()))


def local_step(field, west_edge, east_edge, winds_x, winds_y, column_matrix, row_matrix):
    field = average_pairs(field, west_edge, east_edge)
    swapped = jnp.swapaxes(field, -1, -2)
    swapped = average_pairs(swapped, swapped[..., 0], swapped[..., -1])
    field = jnp.swapaxes(swapped, -1, -2)
    grad_x = jnp.dot(
        winds_x * field,
        column_matrix,
        precision=lax.Precision.HIGHEST,
        preferred_element_type=jnp.float32,
    )
    grad_y = jnp.einsum(
        "ij,mlix->mljx",
        row_matrix,
        winds_y * field,
        precision=lax.Precision.HIGHEST,
        preferred_element_type=jnp.float32,
    )
    return field - time_step * (grad_x + grad_y)


def on_device(forcing, wind_x, wind_y):
    rows_here = forcing.shape[3]
    width = forcing.shape[4]
    steps_count = wind_x.shape[1]
    row_matrix = block_matrix(rows_here)
    column_matrix = block_matrix(width)

    def apply_window(field, steps_x, steps_y):
        for substep in range(steps_count - 1, -1, -1):
            padded = with_halo(field, (("space", 3),), 1)
            field = local_step(
                padded[..., 1:-1],
                padded[..., 0],
                padded[..., -1],
                steps_x[substep],
                steps_y[substep],
                column_matrix,
                row_matrix,
            )
        return field

    local = forcing[:, 0]
    winds_both = (wind_x[0], wind_y[0])

    def one_turn(turn_index, current):
        moved = shifted(apply_window(current, winds_both[0], winds_both[1]), "tm", -1)
        return local + moved

    result = lax.fori_loop(0, lax.axis_size("tm") - 1, one_turn, local)
    return result[:, None]


def solution(mesh):
    placed = (
        P(None, "tm", None, None, "space"),
        P("tm", None, None, None, "space"),
        P("tm", None, None, None, "space"),
    )
    return jax.shard_map(
        on_device,
        mesh=mesh,
        in_specs=placed,
        out_specs=P(None, "tm", None, None, "space"),
        check_vma=False,
    )
```

profile of v0, /device:TPU:1, one launch (start us, length us, event | category | flops | bytes accessed | tf_op | source)
XLA Modules:
  0.0 1212.6 jit_solution(13332328593615884828)
XLA Ops:
  1.1 1210.8 %while.21 = (s32[]{:T(128)}, f32[2,8,32,128]{3,2,1,0:T(8,128)S(1)}, f32[2,8,32,128]{3,2,1,0:T(8,128)S(1)}, f32[2,8,32,128]{3,2,1,0:T(8,128)}, f32[2,8,32,128]{3,...) while((s32[]{:T(128)}, f32[2,8,32,128]{3,2,1,0:T(8,128)S(1)}, ...), condition=%wide.region_1.2_spmd.clone, body=%wide.region_0.1_spmd.sunk.clone.sunk | while | flops 252575744 | bytes 14467501 | solution.py:129
  1.6 20.9 %collective-permute-start = (f32[2,8,32,1]{2,1,0,3:T(8,128)S(1)}, f32[2,8,32,1]{2,1,0,3:T(8,128)S(1)}, u32[]{:S(2)}, u32[]{:S(2)}) collective-permute-start(f32[2,8,32,1]{2,1,0,3:T(8,128)S(1)} %get-tuple-element.304), channel_id=1, source_target_pairs={{1,0},{2,1},{3,2},{4,3},{5,4},{6,5},{7,6},{8,7},{9,8},{10,9},{11,1... | collective-permute-start | bytes 6152 | tf_op jit(solution)/shard_map/while/body/eval_jaxpr/ppermute | solution.py:29
  26.3 13.6 %collective-permute-done.1 = f32[2,8,32,1]{2,1,0,3:T(8,128)S(1)} collective-permute-done((f32[2,8,32,1]{2,1,0,3:T(8,128)S(1)}, f32[2,8,32,1]{2,1,0,3:T(8,128)S(1)}, u32[]{:S(2)}, u32[]{:S(2)}) %collective-permute-start.1) | collective-permute-done | bytes 2080 | tf_op jit(solution)/shard_map/while/body/eval_jaxpr/ppermute | solution.py:26
  55.9 18.1 %collective-permute-done.2 = f32[2,8,32,1]{3,2,1,0:T(8,128)S(1)} collective-permute-done((f32[2,8,32,1]{3,2,1,0:T(8,128)S(1)}, f32[2,8,32,1]{3,2,1,0:T(8,128)S(1)}, u32[]{:S(2)}, u32[]{:S(2)}) %collective-permute-start.2) | collective-permute-done | bytes 2080 | tf_op jit(solution)/shard_map/while/body/eval_jaxpr/ppermute | solution.py:29
  74.1 16.6 %collective-permute-done.3 = f32[2,8,32,1]{3,2,1,0:T(8,128)S(1)} collective-permute-done((f32[2,8,32,1]{3,2,1,0:T(8,128)S(1)}, f32[2,8,32,1]{3,2,1,0:T(8,128)S(1)}, u32[]{:S(2)}, u32[]{:S(2)}) %collective-permute-start.3) | collective-permute-done | bytes 2080 | tf_op jit(solution)/shard_map/while/body/eval_jaxpr/ppermute | solution.py:26
  153.0 16.7 %collective-permute-done.3 = f32[2,8,32,1]{3,2,1,0:T(8,128)S(1)} collective-permute-done((f32[2,8,32,1]{3,2,1,0:T(8,128)S(1)}, f32[2,8,32,1]{3,2,1,0:T(8,128)S(1)}, u32[]{:S(2)}, u32[]{:S(2)}) %collective-permute-start.3) | collective-permute-done | bytes 2080 | tf_op jit(solution)/shard_map/while/body/eval_jaxpr/ppermute | solution.py:26
  233.3 16.9 %collective-permute-done.3 = f32[2,8,32,1]{3,2,1,0:T(8,128)S(1)} collective-permute-done((f32[2,8,32,1]{3,2,1,0:T(8,128)S(1)}, f32[2,8,32,1]{3,2,1,0:T(8,128)S(1)}, u32[]{:S(2)}, u32[]{:S(2)}) %collective-permute-start.3) | collective-permute-done | bytes 2080 | tf_op jit(solution)/shard_map/while/body/eval_jaxpr/ppermute | solution.py:26
  259.8 13.0 %collective-permute-done.4 = f32[2,8,32,128]{3,2,1,0:T(8,128)S(1)} collective-permute-done((f32[2,8,32,128]{3,2,1,0:T(8,128)S(1)}, f32[2,8,32,128]{3,2,1,0:T(8,128)S(1)}, u32[]{:S(2)}, u32[]{:S(2)}) %collective-permute-start.4) | collective-permute-done | bytes 262176 | tf_op jit(solution)/shard_map/while/body/eval_jaxpr/ppermute | solution.py:37
  320.3 16.7 %collective-permute-done.3 = f32[2,8,32,1]{3,2,1,0:T(8,128)S(1)} collective-permute-done((f32[2,8,32,1]{3,2,1,0:T(8,128)S(1)}, f32[2,8,32,1]{3,2,1,0:T(8,128)S(1)}, u32[]{:S(2)}, u32[]{:S(2)}) %collective-permute-start.3) | collective-permute-done | bytes 2080 | tf_op jit(solution)/shard_map/while/body/eval_jaxpr/ppermute | solution.py:26
  398.8 16.6 %collective-permute-done.3 = f32[2,8,32,1]{3,2,1,0:T(8,128)S(1)} collective-permute-done((f32[2,8,32,1]{3,2,1,0:T(8,128)S(1)}, f32[2,8,32,1]{3,2,1,0:T(8,128)S(1)}, u32[]{:S(2)}, u32[]{:S(2)}) %collective-permute-start.3) | collective-permute-done | bytes 2080 | tf_op jit(solution)/shard_map/while/body/eval_jaxpr/ppermute | solution.py:26
  438.7 12.2 %collective-permute-done.1 = f32[2,8,32,1]{2,1,0,3:T(8,128)S(1)} collective-permute-done((f32[2,8,32,1]{2,1,0,3:T(8,128)S(1)}, f32[2,8,32,1]{2,1,0,3:T(8,128)S(1)}, u32[]{:S(2)}, u32[]{:S(2)}) %collective-permute-start.1) | collective-permute-done | bytes 2080 | tf_op jit(solution)/shard_map/while/body/eval_jaxpr/ppermute | solution.py:26
  477.0 16.9 %collective-permute-done.3 = f32[2,8,32,1]{3,2,1,0:T(8,128)S(1)} collective-permute-done((f32[2,8,32,1]{3,2,1,0:T(8,128)S(1)}, f32[2,8,32,1]{3,2,1,0:T(8,128)S(1)}, u32[]{:S(2)}, u32[]{:S(2)}) %collective-permute-start.3) | collective-permute-done | bytes 2080 | tf_op jit(solution)/shard_map/while/body/eval_jaxpr/ppermute | solution.py:26
  545.1 13.7 %collective-permute-done.2 = f32[2,8,32,1]{3,2,1,0:T(8,128)S(1)} collective-permute-done((f32[2,8,32,1]{3,2,1,0:T(8,128)S(1)}, f32[2,8,32,1]{3,2,1,0:T(8,128)S(1)}, u32[]{:S(2)}, u32[]{:S(2)}) %collective-permute-start.2) | collective-permute-done | bytes 2080 | tf_op jit(solution)/shard_map/while/body/eval_jaxpr/ppermute | solution.py:29
  559.0 17.0 %collective-permute-done.3 = f32[2,8,32,1]{3,2,1,0:T(8,128)S(1)} collective-permute-done((f32[2,8,32,1]{3,2,1,0:T(8,128)S(1)}, f32[2,8,32,1]{3,2,1,0:T(8,128)S(1)}, u32[]{:S(2)}, u32[]{:S(2)}) %collective-permute-start.3) | collective-permute-done | bytes 2080 | tf_op jit(solution)/shard_map/while/body/eval_jaxpr/ppermute | solution.py:26
  636.3 16.5 %collective-permute-done.3 = f32[2,8,32,1]{3,2,1,0:T(8,128)S(1)} collective-permute-done((f32[2,8,32,1]{3,2,1,0:T(8,128)S(1)}, f32[2,8,32,1]{3,2,1,0:T(8,128)S(1)}, u32[]{:S(2)}, u32[]{:S(2)}) %collective-permute-start.3) | collective-permute-done | bytes 2080 | tf_op jit(solution)/shard_map/while/body/eval_jaxpr/ppermute | solution.py:26
  711.0 17.2 %collective-permute-done.3 = f32[2,8,32,1]{3,2,1,0:T(8,128)S(1)} collective-permute-done((f32[2,8,32,1]{3,2,1,0:T(8,128)S(1)}, f32[2,8,32,1]{3,2,1,0:T(8,128)S(1)}, u32[]{:S(2)}, u32[]{:S(2)}) %collective-permute-start.3) | collective-permute-done | bytes 2080 | tf_op jit(solution)/shard_map/while/body/eval_jaxpr/ppermute | solution.py:26
  785.0 17.2 %collective-permute-done.3 = f32[2,8,32,1]{3,2,1,0:T(8,128)S(1)} collective-permute-done((f32[2,8,32,1]{3,2,1,0:T(8,128)S(1)}, f32[2,8,32,1]{3,2,1,0:T(8,128)S(1)}, u32[]{:S(2)}, u32[]{:S(2)}) %collective-permute-start.3) | collective-permute-done | bytes 2080 | tf_op jit(solution)/shard_map/while/body/eval_jaxpr/ppermute | solution.py:26
  859.4 17.1 %collective-permute-done.3 = f32[2,8,32,1]{3,2,1,0:T(8,128)S(1)} collective-permute-done((f32[2,8,32,1]{3,2,1,0:T(8,128)S(1)}, f32[2,8,32,1]{3,2,1,0:T(8,128)S(1)}, u32[]{:S(2)}, u32[]{:S(2)}) %collective-permute-start.3) | collective-permute-done | bytes 2080 | tf_op jit(solution)/shard_map/while/body/eval_jaxpr/ppermute | solution.py:26
  886.3 16.6 %collective-permute-done.4 = f32[2,8,32,128]{3,2,1,0:T(8,128)S(1)} collective-permute-done((f32[2,8,32,128]{3,2,1,0:T(8,128)S(1)}, f32[2,8,32,128]{3,2,1,0:T(8,128)S(1)}, u32[]{:S(2)}, u32[]{:S(2)}) %collective-permute-start.4) | collective-permute-done | bytes 262176 | tf_op jit(solution)/shard_map/while/body/eval_jaxpr/ppermute | solution.py:37
  943.8 16.7 %collective-permute-done.3 = f32[2,8,32,1]{3,2,1,0:T(8,128)S(1)} collective-permute-done((f32[2,8,32,1]{3,2,1,0:T(8,128)S(1)}, f32[2,8,32,1]{3,2,1,0:T(8,128)S(1)}, u32[]{:S(2)}, u32[]{:S(2)}) %collective-permute-start.3) | collective-permute-done | bytes 2080 | tf_op jit(solution)/shard_map/while/body/eval_jaxpr/ppermute | solution.py:26
  986.0 13.6 %collective-permute-done.1 = f32[2,8,32,1]{2,1,0,3:T(8,128)S(1)} collective-permute-done((f32[2,8,32,1]{2,1,0,3:T(8,128)S(1)}, f32[2,8,32,1]{2,1,0,3:T(8,128)S(1)}, u32[]{:S(2)}, u32[]{:S(2)}) %collective-permute-start.1) | collective-permute-done | bytes 2080 | tf_op jit(solution)/shard_map/while/body/eval_jaxpr/ppermute | solution.py:26
  1021.3 16.8 %collective-permute-done.3 = f32[2,8,32,1]{3,2,1,0:T(8,128)S(1)} collective-permute-done((f32[2,8,32,1]{3,2,1,0:T(8,128)S(1)}, f32[2,8,32,1]{3,2,1,0:T(8,128)S(1)}, u32[]{:S(2)}, u32[]{:S(2)}) %collective-permute-start.3) | collective-permute-done | bytes 2080 | tf_op jit(solution)/shard_map/while/body/eval_jaxpr/ppermute | solution.py:26
  1100.9 17.0 %collective-permute-done.3 = f32[2,8,32,1]{3,2,1,0:T(8,128)S(1)} collective-permute-done((f32[2,8,32,1]{3,2,1,0:T(8,128)S(1)}, f32[2,8,32,1]{3,2,1,0:T(8,128)S(1)}, u32[]{:S(2)}, u32[]{:S(2)}) %collective-permute-start.3) | collective-permute-done | bytes 2080 | tf_op jit(solution)/shard_map/while/body/eval_jaxpr/ppermute | solution.py:26
  1177.6 16.8 %collective-permute-done.3 = f32[2,8,32,1]{3,2,1,0:T(8,128)S(1)} collective-permute-done((f32[2,8,32,1]{3,2,1,0:T(8,128)S(1)}, f32[2,8,32,1]{3,2,1,0:T(8,128)S(1)}, u32[]{:S(2)}, u32[]{:S(2)}) %collective-permute-start.3) | collective-permute-done | bytes 2080 | tf_op jit(solution)/shard_map/while/body/eval_jaxpr/ppermute | solution.py:26
  (1019 shorter events, 831.5 us)
Async XLA Ops:
  1.6 24.7 %collective-permute-start = (f32[2,8,32,1]{2,1,0,3:T(8,128)S(1)}, f32[2,8,32,1]{2,1,0,3:T(8,128)S(1)}, u32[]{:S(2)}, u32[]{:S(2)}) collective-permute-start(f32[2,8,32,1]{2,1,0,3:T(8,128)S(1)} %get-tuple-element.304), channel_id=1, source_target_pairs={{1,0},{2,1},{3,2},{4,3},{5,4},{6,5},{7,6},{8,7},{9,8},{10,9},{11,1... | collective-permute-start | bytes 6152 | tf_op jit(solution)/shard_map/while/body/eval_jaxpr/ppermute | solution.py:29
  50.3 23.7 %collective-permute-start.2 = (f32[2,8,32,1]{3,2,1,0:T(8,128)S(1)}, f32[2,8,32,1]{3,2,1,0:T(8,128)S(1)}, u32[]{:S(2)}, u32[]{:S(2)}) collective-permute-start(f32[2,8,32,1]{3,2,1,0:T(8,128)S(1)} %get-tuple-element.316), channel_id=1, source_target_pairs={{1,0},{2,1},{3,2},{4,3},{5,4},{6,5},{7,6},{8,7},{9,8},{10,9},{11,1... | collective-permute-start | bytes 6152 | tf_op jit(solution)/shard_map/while/body/eval_jaxpr/ppermute | solution.py:29
  53.0 37.7 %collective-permute-start.3 = (f32[2,8,32,1]{3,2,1,0:T(8,128)S(1)}, f32[2,8,32,1]{3,2,1,0:T(8,128)S(1)}, u32[]{:S(2)}, u32[]{:S(2)}) collective-permute-start(f32[2,8,32,1]{3,2,1,0:T(8,128)S(1)} %get-tuple-element.319), channel_id=1, source_target_pairs={{0,1},{1,2},{2,3},{3,4},{4,5},{5,6},{6,7},{7,8},{8,9},{9,10},{10,1... | collective-permute-start | bytes 6152 | tf_op jit(solution)/shard_map/while/body/eval_jaxpr/ppermute | solution.py:26
  141.2 28.5 %collective-permute-start.3 = (f32[2,8,32,1]{3,2,1,0:T(8,128)S(1)}, f32[2,8,32,1]{3,2,1,0:T(8,128)S(1)}, u32[]{:S(2)}, u32[]{:S(2)}) collective-permute-start(f32[2,8,32,1]{3,2,1,0:T(8,128)S(1)} %get-tuple-element.319), channel_id=1, source_target_pairs={{0,1},{1,2},{2,3},{3,4},{4,5},{5,6},{6,7},{7,8},{8,9},{9,10},{10,1... | collective-permute-start | bytes 6152 | tf_op jit(solution)/shard_map/while/body/eval_jaxpr/ppermute | solution.py:26
  223.6 26.5 %collective-permute-start.3 = (f32[2,8,32,1]{3,2,1,0:T(8,128)S(1)}, f32[2,8,32,1]{3,2,1,0:T(8,128)S(1)}, u32[]{:S(2)}, u32[]{:S(2)}) collective-permute-start(f32[2,8,32,1]{3,2,1,0:T(8,128)S(1)} %get-tuple-element.319), channel_id=1, source_target_pairs={{0,1},{1,2},{2,3},{3,4},{4,5},{5,6},{6,7},{7,8},{8,9},{9,10},{10,1... | collective-permute-start | bytes 6152 | tf_op jit(solution)/shard_map/while/body/eval_jaxpr/ppermute | solution.py:26
  275.4 17.3 %collective-permute-start.1 = (f32[2,8,32,1]{2,1,0,3:T(8,128)S(1)}, f32[2,8,32,1]{2,1,0,3:T(8,128)S(1)}, u32[]{:S(2)}, u32[]{:S(2)}) collective-permute-start(f32[2,8,32,1]{2,1,0,3:T(8,128)S(1)} %get-tuple-element.307), channel_id=1, source_target_pairs={{0,1},{1,2},{2,3},{3,4},{4,5},{5,6},{6,7},{7,8},{8,9},{9,10},{10,1... | collective-permute-start | bytes 6152 | tf_op jit(solution)/shard_map/while/body/eval_jaxpr/ppermute | solution.py:26
  305.8 31.1 %collective-permute-start.3 = (f32[2,8,32,1]{3,2,1,0:T(8,128)S(1)}, f32[2,8,32,1]{3,2,1,0:T(8,128)S(1)}, u32[]{:S(2)}, u32[]{:S(2)}) collective-permute-start(f32[2,8,32,1]{3,2,1,0:T(8,128)S(1)} %get-tuple-element.319), channel_id=1, source_target_pairs={{0,1},{1,2},{2,3},{3,4},{4,5},{5,6},{6,7},{7,8},{8,9},{9,10},{10,1... | collective-permute-start | bytes 6152 | tf_op jit(solution)/shard_map/while/body/eval_jaxpr/ppermute | solution.py:26
  355.0 17.3 %collective-permute-start.1 = (f32[2,8,32,1]{2,1,0,3:T(8,128)S(1)}, f32[2,8,32,1]{2,1,0,3:T(8,128)S(1)}, u32[]{:S(2)}, u32[]{:S(2)}) collective-permute-start(f32[2,8,32,1]{2,1,0,3:T(8,128)S(1)} %get-tuple-element.307), channel_id=1, source_target_pairs={{0,1},{1,2},{2,3},{3,4},{4,5},{5,6},{6,7},{7,8},{8,9},{9,10},{10,1... | collective-permute-start | bytes 6152 | tf_op jit(solution)/shard_map/while/body/eval_jaxpr/ppermute | solution.py:26
  385.4 30.0 %collective-permute-start.3 = (f32[2,8,32,1]{3,2,1,0:T(8,128)S(1)}, f32[2,8,32,1]{3,2,1,0:T(8,128)S(1)}, u32[]{:S(2)}, u32[]{:S(2)}) collective-permute-start(f32[2,8,32,1]{3,2,1,0:T(8,128)S(1)} %get-tuple-element.319), channel_id=1, source_target_pairs={{0,1},{1,2},{2,3},{3,4},{4,5},{5,6},{6,7},{7,8},{8,9},{9,10},{10,1... | collective-permute-start | bytes 6152 | tf_op jit(solution)/shard_map/while/body/eval_jaxpr/ppermute | solution.py:26
  433.5 17.3 %collective-permute-start.1 = (f32[2,8,32,1]{2,1,0,3:T(8,128)S(1)}, f32[2,8,32,1]{2,1,0,3:T(8,128)S(1)}, u32[]{:S(2)}, u32[]{:S(2)}) collective-permute-start(f32[2,8,32,1]{2,1,0,3:T(8,128)S(1)} %get-tuple-element.307), channel_id=1, source_target_pairs={{0,1},{1,2},{2,3},{3,4},{4,5},{5,6},{6,7},{7,8},{8,9},{9,10},{10,1... | collective-permute-start | bytes 6152 | tf_op jit(solution)/shard_map/while/body/eval_jaxpr/ppermute | solution.py:26
  463.9 29.9 %collective-permute-start.3 = (f32[2,8,32,1]{3,2,1,0:T(8,128)S(1)}, f32[2,8,32,1]{3,2,1,0:T(8,128)S(1)}, u32[]{:S(2)}, u32[]{:S(2)}) collective-permute-start(f32[2,8,32,1]{3,2,1,0:T(8,128)S(1)} %get-tuple-element.319), channel_id=1, source_target_pairs={{0,1},{1,2},{2,3},{3,4},{4,5},{5,6},{6,7},{7,8},{8,9},{9,10},{10,1... | collective-permute-start | bytes 6152 | tf_op jit(solution)/shard_map/while/body/eval_jaxpr/ppermute | solution.py:26
  511.8 17.3 %collective-permute-start.1 = (f32[2,8,32,1]{2,1,0,3:T(8,128)S(1)}, f32[2,8,32,1]{2,1,0,3:T(8,128)S(1)}, u32[]{:S(2)}, u32[]{:S(2)}) collective-permute-start(f32[2,8,32,1]{2,1,0,3:T(8,128)S(1)} %get-tuple-element.307), channel_id=1, source_target_pairs={{0,1},{1,2},{2,3},{3,4},{4,5},{5,6},{6,7},{7,8},{8,9},{9,10},{10,1... | collective-permute-start | bytes 6152 | tf_op jit(solution)/shard_map/while/body/eval_jaxpr/ppermute | solution.py:26
  539.6 19.3 %collective-permute-start.2 = (f32[2,8,32,1]{3,2,1,0:T(8,128)S(1)}, f32[2,8,32,1]{3,2,1,0:T(8,128)S(1)}, u32[]{:S(2)}, u32[]{:S(2)}) collective-permute-start(f32[2,8,32,1]{3,2,1,0:T(8,128)S(1)} %get-tuple-element.316), channel_id=1, source_target_pairs={{1,0},{2,1},{3,2},{4,3},{5,4},{6,5},{7,6},{8,7},{9,8},{10,9},{11,1... | collective-permute-start | bytes 6152 | tf_op jit(solution)/shard_map/while/body/eval_jaxpr/ppermute | solution.py:29
  542.3 33.7 %collective-permute-start.3 = (f32[2,8,32,1]{3,2,1,0:T(8,128)S(1)}, f32[2,8,32,1]{3,2,1,0:T(8,128)S(1)}, u32[]{:S(2)}, u32[]{:S(2)}) collective-permute-start(f32[2,8,32,1]{3,2,1,0:T(8,128)S(1)} %get-tuple-element.319), channel_id=1, source_target_pairs={{0,1},{1,2},{2,3},{3,4},{4,5},{5,6},{6,7},{7,8},{8,9},{9,10},{10,1... | collective-permute-start | bytes 6152 | tf_op jit(solution)/shard_map/while/body/eval_jaxpr/ppermute | solution.py:26
  594.2 17.3 %collective-permute-start.1 = (f32[2,8,32,1]{2,1,0,3:T(8,128)S(1)}, f32[2,8,32,1]{2,1,0,3:T(8,128)S(1)}, u32[]{:S(2)}, u32[]{:S(2)}) collective-permute-start(f32[2,8,32,1]{2,1,0,3:T(8,128)S(1)} %get-tuple-element.307), channel_id=1, source_target_pairs={{0,1},{1,2},{2,3},{3,4},{4,5},{5,6},{6,7},{7,8},{8,9},{9,10},{10,1... | collective-permute-start | bytes 6152 | tf_op jit(solution)/shard_map/while/body/eval_jaxpr/ppermute | solution.py:26
  624.7 28.0 %collective-permute-start.3 = (f32[2,8,32,1]{3,2,1,0:T(8,128)S(1)}, f32[2,8,32,1]{3,2,1,0:T(8,128)S(1)}, u32[]{:S(2)}, u32[]{:S(2)}) collective-permute-start(f32[2,8,32,1]{3,2,1,0:T(8,128)S(1)} %get-tuple-element.319), channel_id=1, source_target_pairs={{0,1},{1,2},{2,3},{3,4},{4,5},{5,6},{6,7},{7,8},{8,9},{9,10},{10,1... | collective-permute-start | bytes 6152 | tf_op jit(solution)/shard_map/while/body/eval_jaxpr/ppermute | solution.py:26
  701.1 27.1 %collective-permute-start.3 = (f32[2,8,32,1]{3,2,1,0:T(8,128)S(1)}, f32[2,8,32,1]{3,2,1,0:T(8,128)S(1)}, u32[]{:S(2)}, u32[]{:S(2)}) collective-permute-start(f32[2,8,32,1]{3,2,1,0:T(8,128)S(1)} %get-tuple-element.319), channel_id=1, source_target_pairs={{0,1},{1,2},{2,3},{3,4},{4,5},{5,6},{6,7},{7,8},{8,9},{9,10},{10,1... | collective-permute-start | bytes 6152 | tf_op jit(solution)/shard_map/while/body/eval_jaxpr/ppermute | solution.py:26
  776.7 25.5 %collective-permute-start.3 = (f32[2,8,32,1]{3,2,1,0:T(8,128)S(1)}, f32[2,8,32,1]{3,2,1,0:T(8,128)S(1)}, u32[]{:S(2)}, u32[]{:S(2)}) collective-permute-start(f32[2,8,32,1]{3,2,1,0:T(8,128)S(1)} %get-tuple-element.319), channel_id=1, source_target_pairs={{0,1},{1,2},{2,3},{3,4},{4,5},{5,6},{6,7},{7,8},{8,9},{9,10},{10,1... | collective-permute-start | bytes 6152 | tf_op jit(solution)/shard_map/while/body/eval_jaxpr/ppermute | solution.py:26
  854.2 22.4 %collective-permute-start.3 = (f32[2,8,32,1]{3,2,1,0:T(8,128)S(1)}, f32[2,8,32,1]{3,2,1,0:T(8,128)S(1)}, u32[]{:S(2)}, u32[]{:S(2)}) collective-permute-start(f32[2,8,32,1]{3,2,1,0:T(8,128)S(1)} %get-tuple-element.319), channel_id=1, source_target_pairs={{0,1},{1,2},{2,3},{3,4},{4,5},{5,6},{6,7},{7,8},{8,9},{9,10},{10,1... | collective-permute-start | bytes 6152 | tf_op jit(solution)/shard_map/while/body/eval_jaxpr/ppermute | solution.py:26
  884.4 18.5 %collective-permute-start.4 = (f32[2,8,32,128]{3,2,1,0:T(8,128)S(1)}, f32[2,8,32,128]{3,2,1,0:T(8,128)S(1)}, u32[]{:S(2)}, u32[]{:S(2)}) collective-permute-start(f32[2,8,32,128]{3,2,1,0:T(8,128)S(1)} %fusion.62), channel_id=1, source_target_pairs={{32,0},{64,32},{96,64},{128,96},{160,128},{192,160},{224,192},{256... | collective-permute-start | bytes 786440 | tf_op jit(solution)/shard_map/while/body/eval_jaxpr/ppermute | solution.py:37
  935.8 24.7 %collective-permute-start.3 = (f32[2,8,32,1]{3,2,1,0:T(8,128)S(1)}, f32[2,8,32,1]{3,2,1,0:T(8,128)S(1)}, u32[]{:S(2)}, u32[]{:S(2)}) collective-permute-start(f32[2,8,32,1]{3,2,1,0:T(8,128)S(1)} %get-tuple-element.319), channel_id=1, source_target_pairs={{0,1},{1,2},{2,3},{3,4},{4,5},{5,6},{6,7},{7,8},{8,9},{9,10},{10,1... | collective-permute-start | bytes 6152 | tf_op jit(solution)/shard_map/while/body/eval_jaxpr/ppermute | solution.py:26
  1012.7 25.4 %collective-permute-start.3 = (f32[2,8,32,1]{3,2,1,0:T(8,128)S(1)}, f32[2,8,32,1]{3,2,1,0:T(8,128)S(1)}, u32[]{:S(2)}, u32[]{:S(2)}) collective-permute-start(f32[2,8,32,1]{3,2,1,0:T(8,128)S(1)} %get-tuple-element.319), channel_id=1, source_target_pairs={{0,1},{1,2},{2,3},{3,4},{4,5},{5,6},{6,7},{7,8},{8,9},{9,10},{10,1... | collective-permute-start | bytes 6152 | tf_op jit(solution)/shard_map/while/body/eval_jaxpr/ppermute | solution.py:26
  1091.8 26.0 %collective-permute-start.3 = (f32[2,8,32,1]{3,2,1,0:T(8,128)S(1)}, f32[2,8,32,1]{3,2,1,0:T(8,128)S(1)}, u32[]{:S(2)}, u32[]{:S(2)}) collective-permute-start(f32[2,8,32,1]{3,2,1,0:T(8,128)S(1)} %get-tuple-element.319), channel_id=1, source_target_pairs={{0,1},{1,2},{2,3},{3,4},{4,5},{5,6},{6,7},{7,8},{8,9},{9,10},{10,1... | collective-permute-start | bytes 6152 | tf_op jit(solution)/shard_map/while/body/eval_jaxpr/ppermute | solution.py:26
  1170.5 23.9 %collective-permute-start.3 = (f32[2,8,32,1]{3,2,1,0:T(8,128)S(1)}, f32[2,8,32,1]{3,2,1,0:T(8,128)S(1)}, u32[]{:S(2)}, u32[]{:S(2)}) collective-permute-start(f32[2,8,32,1]{3,2,1,0:T(8,128)S(1)} %get-tuple-element.319), channel_id=1, source_target_pairs={{0,1},{1,2},{2,3},{3,4},{4,5},{5,6},{6,7},{7,8},{8,9},{9,10},{10,1... | collective-permute-start | bytes 6152 | tf_op jit(solution)/shard_map/while/body/eval_jaxpr/ppermute | solution.py:26
  (99 other events, 617.2 us)
where the time goes:
time: 1230 us; the launch traced here: 1210 us
  waiting for transfers between devices  687 us (56%)
  local copies, waits for them, and re-layouts  270 us (22%)
  starting transfers between devices  209 us (17%)
  matrix products  21.9 us (2%)
  other arithmetic  18 us (1%)
    ppermute x30, waiting for transfers between devices, with_halo(): lax.ppermute(lax.slice_in_dim(block, block.shape[dim] - width, None, axis...  438 us
    ppermute x15, waiting for transfers between devices, shifted(): return lax.ppermute(block, axis, route)  126 us
    ppermute x30, waiting for transfers between devices, with_halo(): lax.ppermute(lax.slice_in_dim(block, 0, width, axis=dim), axis, backward)  123 us
    ppermute x30, starting transfers between devices, with_halo(): lax.ppermute(lax.slice_in_dim(block, 0, width, axis=dim), axis, backward)  90.8 us
    ppermute x30, starting transfers between devices, with_halo(): lax.ppermute(lax.slice_in_dim(block, block.shape[dim] - width, None, axis...  86.1 us
    scatter x60, local copies, waits for them, and re-layouts, average_pairs(): shaped = shaped.at[..., :, 7].set(0.5 * (lasts + after))  86 us
    scatter x60, local copies, waits for them, and re-layouts, average_pairs(): shaped = shaped.at[..., :, 0].set(0.5 * (firsts + before))  84.6 us
    while x135, local copies, waits for them, and re-layouts  41.9 us
  transfers between devices with their start and end apart: 75, of which 60 were waited for; matrix products, arithmetic and copies ran while one was open for 2% of the time, Pallas kernels for 0%

commit v1 on v0

v1 whole, which is shorter than its diff:
```python
import functools

import jax
import jax.numpy as jnp
import numpy as np
from jax import lax
from jax.experimental import pallas as pl
from jax.experimental.pallas import tpu as pltpu
from jax.sharding import PartitionSpec as P

time_step = 0.01
lobatto_points = [
    -1.0,
    -0.8717401485096066,
    -0.5917001814331423,
    -0.20929921790247888,
    0.20929921790247888,
    0.5917001814331423,
    0.8717401485096066,
    1.0,
]


def legendre_seven(point):
    before = 1.0
    current = point
    for order in range(1, 7):
        before, current = (
            current,
            ((2 * order + 1) * point * current - order * before) / (order + 1),
        )
    return current


def lobatto_table():
    values = [legendre_seven(point) for point in lobatto_points]
    table = np.zeros((8, 8))
    for row_index in range(8):
        for col_index in range(8):
            if row_index != col_index:
                table[row_index, col_index] = values[row_index] / (
                    values[col_index] * (lobatto_points[row_index] - lobatto_points[col_index])
                )
    table[0, 0] = -14.0
    table[7, 7] = 14.0
    return table.astype(np.float32)


def adjoint_steps(own_ref, west_ref, east_ref, dx_ref, dy_ref, start, windows, emit, last_moves):
    members = 2
    rows = own_ref.shape[2]
    width = own_ref.shape[3]
    shape = (members * rows, 3 * width)
    row = lax.broadcasted_iota(jnp.int32, shape, 0)
    col = lax.broadcasted_iota(jnp.int32, shape, 1)
    from_west = (col % 8) == 0
    from_east = (col % 8) == 7
    from_above = ((row % 8) == 0) & ((row % rows) != 0)
    from_below = ((row % 8) == 7) & ((row % rows) != rows - 1)
    high = lax.Precision.HIGHEST

    def wide(window, index):
        return jnp.concatenate(
            [west_ref[window, index], own_ref[window, index], east_ref[window, index]], axis=1
        )

    moved = start
    for window in range(windows - 1, -1, -1):
        field = jnp.concatenate([wide(window, 4), wide(window, 5)], axis=0)
        if moved is not None:
            field = field + moved
        emit(window, field[:, width : 2 * width])
        if window == 0 and not last_moves:
            return None
        for substep in (1, 0):
            wx = wide(window, substep)
            wy = wide(window, 2 + substep)
            wx = jnp.concatenate([wx, wx], axis=0)
            wy = jnp.concatenate([wy, wy], axis=0)
            partner = jnp.where(
                from_west,
                pltpu.roll(field, 1, 1),
                jnp.where(from_east, pltpu.roll(field, 3 * width - 1, 1), field),
            )
            q = 0.5 * (field + partner)
            partner = jnp.where(
                from_above,
                pltpu.roll(q, 1, 0),
                jnp.where(from_below, pltpu.roll(q, members * rows - 1, 0), q),
            )
            q = 0.5 * (q + partner)
            u = wx * q
            stacked = jnp.concatenate(
                [u[:, :width], u[:, width : 2 * width], u[:, 2 * width :]], axis=0
            )
            gx = jnp.dot(
                stacked, dx_ref[...], precision=high, preferred_element_type=jnp.float32
            )
            n = members * rows
            gx = jnp.concatenate([gx[:n], gx[n : 2 * n], gx[2 * n :]], axis=1)
            gy = jnp.dot(
                dy_ref[...], wy * q, precision=high, preferred_element_type=jnp.float32
            )
            field = q - (gx + gy)
        moved = field
    return moved


def first_kernel(own_ref, west_ref, east_ref, dx_ref, dy_ref, out_ref):
    width = own_ref.shape[3]
    moved = adjoint_steps(
        own_ref, west_ref, east_ref, dx_ref, dy_ref, None, own_ref.shape[0], lambda w, v: None, True
    )
    out_ref[...] = moved[:, width : 2 * width]


def second_kernel(own_ref, west_ref, east_ref, dx_ref, dy_ref, pw_ref, pc_ref, pe_ref, out_ref):
    rows = own_ref.shape[2]

    def emit(window, field):
        out_ref[window, 0] = field[:rows]
        out_ref[window, 1] = field[rows:]

    start = jnp.concatenate([pw_ref[...], pc_ref[...], pe_ref[...]], axis=1)
    adjoint_steps(
        own_ref, west_ref, east_ref, dx_ref, dy_ref, start, own_ref.shape[0], emit, False
    )


def local_call(kernel, out_shape, count):
    return pl.pallas_call(
        kernel,
        out_shape=out_shape,
        in_specs=[pl.BlockSpec(memory_space=pltpu.VMEM)] * count,
        out_specs=pl.BlockSpec(memory_space=pltpu.VMEM),
        compiler_params=pltpu.CompilerParams(vmem_limit_bytes=32 * 1024 * 1024),
    )


def on_device(forcing, wind_x, wind_y):
    members, _, levels, rows, width = forcing.shape
    steps = wind_x.shape[1]
    tm = lax.axis_size("tm")
    space = lax.axis_size("space")
    group = levels
    groups = [list(range(i, i + group)) for i in range(0, tm, group)]

    def flat(t, s):
        return t * space + s % space

    def moved_by(block, dt, ds):
        pairs = [
            (flat(t, s), flat(t + dt, s + ds))
            for t in range(tm)
            for s in range(space)
            if 0 <= t + dt < tm
        ]
        return lax.ppermute(block, ("tm", "space"), pairs)

    packed = jnp.concatenate([wind_x[0], wind_y[0], forcing[:, 0]], axis=0)
    packed = jnp.swapaxes(packed, 0, 1)
    own = lax.all_to_all(packed, "tm", 0, 0, axis_index_groups=groups, tiled=True)
    west = moved_by(own, 0, 1)
    east = moved_by(own, 0, -1)

    table = lobatto_table() * np.float32(time_step)
    dx = jnp.asarray(np.kron(np.eye(width // 8, dtype=np.float32), table))
    dy = jnp.asarray(np.kron(np.eye(members * rows // 8, dtype=np.float32), table.T))

    flat_field = jax.ShapeDtypeStruct((members * rows, width), jnp.float32)
    sent = local_call(first_kernel, flat_field, 5)(own, west, east, dx, dy)
    below = moved_by(sent, -group, 0)
    below_west = moved_by(sent, -group, 1)
    below_east = moved_by(sent, -group, -1)
    result = local_call(
        second_kernel, jax.ShapeDtypeStruct((group, members, rows, width), jnp.float32), 8
    )(own, west, east, dx, dy, below_west, below, below_east)
    result = lax.all_to_all(result, "tm", 0, 0, axis_index_groups=groups, tiled=True)
    return jnp.swapaxes(result, 0, 1)[:, None]


def solution(mesh):
    placed = (
        P(None, "tm", None, None, "space"),
        P("tm", None, None, None, "space"),
        P("tm", None, None, None, "space"),
    )
    return jax.shard_map(
        on_device,
        mesh=mesh,
        in_specs=placed,
        out_specs=P(None, "tm", None, None, "space"),
        check_vma=False,
    )
```

time: 1230 us -> 175 us (0.14); the launches traced: 1210 us -> 175 us
  waiting for transfers between devices: 687 us -> 85.4 us
  local copies, waits for them, and re-layouts: 270 us -> 1.86 us
  starting transfers between devices: 209 us -> 21.1 us
  blocking collectives: 0 us -> 52.4 us
  matrix products: 21.9 us -> 0 us
  other arithmetic: 18 us -> 0.05 us
  Pallas kernels: 0 us -> 13.6 us
    ppermute x75 -> x5, waiting for transfers between devices: 687 us -> 85.4 us  [moved_by(): return lax.ppermute(block, ('tm', 'space'), pairs)]
    ppermute x75 -> x5, starting transfers between devices: 209 us -> 21.1 us  [moved_by(): return lax.ppermute(block, ('tm', 'space'), pairs)]
    scatter x120 -> x0, local copies, waits for them, and re-layouts: 171 us -> none  [the longest x60 86 us: average_pairs(): shaped = shaped.at[..., :, 7].set(0.5 * (lasts + after))]
    all_to_all x0 -> x2, blocking collectives: none -> 52.4 us  [the longest x1 29.4 us: on_device(): lax.all_to_all(packed, 'tm', 0, 0, axis_index_groups=groups, tiled=True)]
    while x135 -> x0, local copies, waits for them, and re-layouts: 41.9 us -> none
    dot_general x60 -> x0, matrix products: 21.9 us -> none  [the longest x30 11.1 us: local_step(): jnp.dot(winds_x * field, column_matrix, precision=lax.Precision.HIGHEST,...]
    slice x90 -> x0, local copies, waits for them, and re-layouts: 21.1 us -> none  [the longest x15 13.6 us: local_step(): swapped = average_pairs(swapped, swapped[..., 0], swapped[..., -1])]
    reshape x45 -> x0, local copies, waits for them, and re-layouts: 14.7 us -> none  [the longest x30 9.76 us: average_pairs(): shaped = values.reshape(values.shape[:-1] + (-1, 8))]
  transfers between devices with their start and end apart: 75 -> 5, of which waited for: 60 -> 4; matrix products, arithmetic and copies ran while one was open for 2% -> 0% of each run, Pallas kernels for 0% -> 0%
where the time goes in v1:
time: 175 us
  waiting for transfers between devices  85.4 us (49%)
  blocking collectives  52.4 us (30%)
  starting transfers between devices  21.1 us (12%)
  Pallas kernels  13.6 us (8%)
  local copies, waits for them, and re-layouts  1.86 us (1%)
    ppermute x5, waiting for transfers between devices, moved_by(): return lax.ppermute(block, ('tm', 'space'), pairs)  85.4 us
    all_to_all x1, blocking collectives, on_device(): lax.all_to_all(packed, 'tm', 0, 0, axis_index_groups=groups, tiled=True)  29.4 us
    all_to_all x1, blocking collectives, on_device(): lax.all_to_all(result, 'tm', 0, 0, axis_index_groups=groups, tiled=True)  23.1 us
    ppermute x5, starting transfers between devices, moved_by(): return lax.ppermute(block, ('tm', 'space'), pairs)  21.1 us
    pallas_call x1, Pallas kernels, on_device(): sent = local_call(first_kernel, flat_field, 5)(own, west, east, dx, dy)  7.17 us
    pallas_call x1, Pallas kernels, on_device(): local_call(second_kernel, jax.ShapeDtypeStruct((group, members, rows, wid...  6.38 us
  transfers between devices with their start and end apart: 5, of which 4 were waited for; matrix products, arithmetic and copies ran while one was open for 0% of the time, Pallas kernels for 0%

profile of v1, /device:TPU:1, one launch (start us, length us, event | category | flops | bytes accessed | tf_op | source)
XLA Modules:
  0.0 174.5 jit_solution(14232316727859280511)
XLA Ops:
  0.0 0.0 copy-start.2
  0.0 1.0 copy.13
  1.0 0.0 copy-done.2
  1.0 0.1 copy-done.3
  1.2 0.1 maximum_bitcast_fusion
  1.2 0.0 copy-start
  1.2 0.0 copy-start.1
  1.2 29.4 %all_to_all.10.own_ref = f32[8,6,32,128]{3,2,1,0:T(8,128)S(1)} all-to-all(f32[8,6,32,128]{3,2,1,0:T(8,128)S(1)} %maximum_bitcast_fusion), channel_id=1, replica_groups={{0,32,64,96,128,160,192,224},{256,288,320,352,384,416,448,480},{1,33,65..., dimensions={0} | all-to-all | bytes 1572864 | tf_op jit(solution)/shard_map/all_to_all | solution.py:162
  30.6 15.3 %collective-permute-start.1 = (f32[8,6,32,128]{3,2,1,0:T(8,128)S(1)}, f32[8,6,32,128]{3,2,1,0:T(8,128)S(1)}, u32[]{:S(2)}, u32[]{:S(2)}) collective-permute-start(f32[8,6,32,128]{3,2,1,0:T(8,128)S(1)} %all_to_all.10.own_ref), channel_id=1, source_target_pairs={{0,31},{1,0},{2,1},{3,2},{4,3},{5,4},{6,5},{7,6},{8,7},{9,8},{10,9... | collective-permute-start | bytes 2359304 | tf_op jit(solution)/shard_map/ppermute | solution.py:158
  45.9 1.9 %collective-permute-start = (f32[8,6,32,128]{3,2,1,0:T(8,128)S(1)}, f32[8,6,32,128]{3,2,1,0:T(8,128)S(1)}, u32[]{:S(2)}, u32[]{:S(2)}) collective-permute-start(f32[8,6,32,128]{3,2,1,0:T(8,128)S(1)} %all_to_all.10.own_ref), channel_id=1, source_target_pairs={{0,1},{1,2},{2,3},{3,4},{4,5},{5,6},{6,7},{7,8},{8,9},{9,10},{10,1... | collective-permute-start | bytes 2359304 | tf_op jit(solution)/shard_map/ppermute | solution.py:158
  47.8 32.2 %collective-permute-done.1.east_ref = f32[8,6,32,128]{3,2,1,0:T(8,128)S(1)} collective-permute-done((f32[8,6,32,128]{3,2,1,0:T(8,128)S(1)}, f32[8,6,32,128]{3,2,1,0:T(8,128)S(1)}, u32[]{:S(2)}, u32[]{:S(2)}) %collective-permute-start.1) | collective-permute-done | bytes 786464 | tf_op jit(solution)/shard_map/ppermute | solution.py:158
  80.0 16.8 %collective-permute-done.west_ref = f32[8,6,32,128]{3,2,1,0:T(8,128)S(1)} collective-permute-done((f32[8,6,32,128]{3,2,1,0:T(8,128)S(1)}, f32[8,6,32,128]{3,2,1,0:T(8,128)S(1)}, u32[]{:S(2)}, u32[]{:S(2)}) %collective-permute-start) | collective-permute-done | bytes 786464 | tf_op jit(solution)/shard_map/ppermute | solution.py:158
  96.8 0.0 copy-done
  96.8 0.0 copy-done.1
  96.8 7.2 %shard_map.55 = f32[64,128]{1,0:T(8,128)S(1)} custom-call(f32[8,6,32,128]{3,2,1,0:T(8,128)S(1)} %all_to_all.10.own_ref, f32[8,6,32,128]{3,2,1,0:T(8,128)S(1)} %collective-permute-done.west_ref, f32[8,6,32,128]{3,2,1,0:T(8,128)S(1)} %collective-permute-done.1.east_ref, f32[128,128]{1,0:T(8,128)S(1)} %copy-done, f32[64,64]{1,0:T(8,128)S(1)} %copy-done.1), custom_call_target="tpu_custom_call" | custom-call | tf_op jit(solution)/shard_map/pallas_call | solution.py:171
  104.0 1.3 collective-permute-start.4
  105.3 1.3 collective-permute-start.3
  106.6 1.3 collective-permute-start.2
  107.9 5.9 %collective-permute-done.4.pe_ref = f32[64,128]{1,0:T(8,128)S(1)} collective-permute-done((f32[64,128]{1,0:T(8,128)S(1)}, f32[64,128]{1,0:T(8,128)S(1)}, u32[]{:S(2)}, u32[]{:S(2)}) %collective-permute-start.4) | collective-permute-done | bytes 32800 | tf_op jit(solution)/shard_map/ppermute | solution.py:158
  113.8 30.6 %collective-permute-done.3.pc_ref = f32[64,128]{1,0:T(8,128)S(1)} collective-permute-done((f32[64,128]{1,0:T(8,128)S(1)}, f32[64,128]{1,0:T(8,128)S(1)}, u32[]{:S(2)}, u32[]{:S(2)}) %collective-permute-start.3) | collective-permute-done | bytes 32800 | tf_op jit(solution)/shard_map/ppermute | solution.py:158
  144.3 0.0 collective-permute-done.2.pw_ref
  144.3 6.4 %shard_map.56 = f32[8,2,32,128]{3,2,1,0:T(8,128)S(1)} custom-call(f32[8,6,32,128]{3,2,1,0:T(8,128)S(1)} %all_to_all.10.own_ref, f32[8,6,32,128]{3,2,1,0:T(8,128)S(1)} %collective-permute-done.west_ref, f32[8,6,32,128]{3,2,1,0:T(8,128)S(1)} %collective-permute-done.1.east_ref, f32[128,128]{1,0:T(8,128)S(1)} %copy-done, f32[64,64]{1,0:T(8,128)S(1)} %copy-done.1, ...), custom_call_target="tpu_custom_call" | custom-call | tf_op jit(solution)/shard_map/pallas_call | solution.py:175
  150.7 23.1 %all_to_all.11 = f32[8,2,32,128]{3,2,1,0:T(8,128)S(1)} all-to-all(f32[8,2,32,128]{3,2,1,0:T(8,128)S(1)} %shard_map.56), channel_id=1, replica_groups={{0,32,64,96,128,160,192,224},{256,288,320,352,384,416,448,480},{1,33,65..., dimensions={0} | all-to-all | bytes 524288 | tf_op jit(solution)/shard_map/all_to_all | solution.py:178
  173.8 0.7 copy.9
  (2 shorter events, 0.0 us)
Async XLA Ops:
  0.0 1.0 copy-start.2
  0.0 1.1 copy-start.3
  1.2 95.6 %copy-start = (f32[128,128]{1,0:T(8,128)S(1)}, f32[128,128]{1,0:T(8,128)}, u32[]{:S(2)}) copy-start(f32[128,128]{1,0:T(8,128)} %constant.4.clone.dx_ref) | copy-start | bytes 196612
  1.2 95.6 %copy-start.1 = (f32[64,64]{1,0:T(8,128)S(1)}, f32[64,64]{1,0:T(8,128)}, u32[]{:S(2)}) copy-start(f32[64,64]{1,0:T(8,128)} %constant.5.clone.dy_ref) | copy-start | bytes 49156
  30.6 49.4 %collective-permute-start.1 = (f32[8,6,32,128]{3,2,1,0:T(8,128)S(1)}, f32[8,6,32,128]{3,2,1,0:T(8,128)S(1)}, u32[]{:S(2)}, u32[]{:S(2)}) collective-permute-start(f32[8,6,32,128]{3,2,1,0:T(8,128)S(1)} %all_to_all.10.own_ref), channel_id=1, source_target_pairs={{0,31},{1,0},{2,1},{3,2},{4,3},{5,4},{6,5},{7,6},{8,7},{9,8},{10,9... | collective-permute-start | bytes 2359304 | tf_op jit(solution)/shard_map/ppermute | solution.py:158
  45.9 50.9 %collective-permute-start = (f32[8,6,32,128]{3,2,1,0:T(8,128)S(1)}, f32[8,6,32,128]{3,2,1,0:T(8,128)S(1)}, u32[]{:S(2)}, u32[]{:S(2)}) collective-permute-start(f32[8,6,32,128]{3,2,1,0:T(8,128)S(1)} %all_to_all.10.own_ref), channel_id=1, source_target_pairs={{0,1},{1,2},{2,3},{3,4},{4,5},{5,6},{6,7},{7,8},{8,9},{9,10},{10,1... | collective-permute-start | bytes 2359304 | tf_op jit(solution)/shard_map/ppermute | solution.py:158
  104.0 9.8 %collective-permute-start.4 = (f32[64,128]{1,0:T(8,128)S(1)}, f32[64,128]{1,0:T(8,128)S(1)}, u32[]{:S(2)}, u32[]{:S(2)}) collective-permute-start(f32[64,128]{1,0:T(8,128)S(1)} %shard_map.55), channel_id=1, source_target_pairs={{256,31},{257,0},{258,1},{259,2},{260,3},{261,4},{262,5},{263,6},{... | collective-permute-start | bytes 98312 | tf_op jit(solution)/shard_map/ppermute | solution.py:158
  105.3 39.0 %collective-permute-start.3 = (f32[64,128]{1,0:T(8,128)S(1)}, f32[64,128]{1,0:T(8,128)S(1)}, u32[]{:S(2)}, u32[]{:S(2)}) collective-permute-start(f32[64,128]{1,0:T(8,128)S(1)} %shard_map.55), channel_id=1, source_target_pairs={{256,0},{257,1},{258,2},{259,3},{260,4},{261,5},{262,6},{263,7},{2... | collective-permute-start | bytes 98312 | tf_op jit(solution)/shard_map/ppermute | solution.py:158
  106.6 37.7 %collective-permute-start.2 = (f32[64,128]{1,0:T(8,128)S(1)}, f32[64,128]{1,0:T(8,128)S(1)}, u32[]{:S(2)}, u32[]{:S(2)}) collective-permute-start(f32[64,128]{1,0:T(8,128)S(1)} %shard_map.55), channel_id=1, source_target_pairs={{256,1},{257,2},{258,3},{259,4},{260,5},{261,6},{262,7},{263,8},{2... | collective-permute-start | bytes 98312 | tf_op jit(solution)/shard_map/ppermute | solution.py:158

commit v2 on v1

--- a/solution.py
+++ b/solution.py
@@ -1,5 +1,3 @@
-import functools
-
 import jax
 import jax.numpy as jnp
 import numpy as np
@@ -46,10 +44,67 @@
     return table.astype(np.float32)
 
 
-def adjoint_steps(own_ref, west_ref, east_ref, dx_ref, dy_ref, start, windows, emit, last_moves):
+def pair_tiles(windows):
+    last = 2 * windows
+    tiles = []
+
+    def block(step, kind):
+        return (windows - 1 - (step - 1) // 2, 2 * kind + (step % 2))
+
+    for step in range(1, windows + 1):
+        for kind in (0, 1):
+            tiles.append((block(step, kind), block(last + 1 - step, kind), 8 * (last - step)))
+    tiles.append(((windows - 1, 4), None, 16 * windows))
+    tiles.append(((windows - 1, 5), None, 16 * windows))
+    for window in range(windows - 2, windows // 2 - 1, -1):
+        for member in (4, 5):
+            tiles.append(
+                ((window, member), (windows - 2 - window, member), 16 * (window + 1))
+            )
+    middle = windows // 2 - 1
+    tiles.append(((middle, 4), (middle, 5), 16 * (middle + 1)))
+    return tiles
+
+
+def places(windows):
+    found = {}
+    for index, (first, second, columns) in enumerate(pair_tiles(windows)):
+        found[first] = (index, 0)
+        if second is not None:
+            found[second] = (index, columns)
+    return found
+
+
+def pack_kernel(own_ref, even_ref, odd_ref):
+    windows, _, rows, width = own_ref.shape
+    col = lax.broadcasted_iota(jnp.int32, (rows, width), 1)
+    odd_place = lax.axis_index("space") % 2
+
+    def write(low_ref, high_ref):
+        for index, (first, second, columns) in enumerate(pair_tiles(windows)):
+            one = own_ref[first[0], first[1]]
+            if second is None:
+                low_ref[index] = one
+                high_ref[index] = one
+                continue
+            other = own_ref[second[0], second[1]]
+            low_ref[index] = jnp.where(col < columns, one, pltpu.roll(other, columns, 1))
+            high_ref[index] = jnp.where(
+                col >= width - columns, one, pltpu.roll(other, width - columns, 1)
+            )
+
+    @pl.when(odd_place == 0)
+    def _():
+        write(odd_ref, even_ref)
+
+    @pl.when(odd_place == 1)
+    def _():
+        write(even_ref, odd_ref)
+
+
+def adjoint_steps(own_ref, halo, dx_ref, dy_ref, start, emit, last_moves):
+    windows, _, rows, width = own_ref.shape
     members = 2
-    rows = own_ref.shape[2]
-    width = own_ref.shape[3]
     shape = (members * rows, 3 * width)
     row = lax.broadcasted_iota(jnp.int32, shape, 0)
     col = lax.broadcasted_iota(jnp.int32, shape, 1)
@@ -60,9 +115,8 @@
     high = lax.Precision.HIGHEST
 
     def wide(window, index):
-        return jnp.concatenate(
-            [west_ref[window, index], own_ref[window, index], east_ref[window, index]], axis=1
-        )
+        west, east = halo(window, index)
+        return jnp.concatenate([west, own_ref[window, index], east], axis=1)
 
     moved = start
     for window in range(windows - 1, -1, -1):
@@ -106,75 +160,128 @@
     return moved
 
 
-def first_kernel(own_ref, west_ref, east_ref, dx_ref, dy_ref, out_ref):
-    width = own_ref.shape[3]
-    moved = adjoint_steps(
-        own_ref, west_ref, east_ref, dx_ref, dy_ref, None, own_ref.shape[0], lambda w, v: None, True
-    )
-    out_ref[...] = moved[:, width : 2 * width]
-
-
-def second_kernel(own_ref, west_ref, east_ref, dx_ref, dy_ref, pw_ref, pc_ref, pe_ref, out_ref):
-    rows = own_ref.shape[2]
+def halo_reader(windows, width, even_ref, odd_ref, far_ref):
+    found = places(windows)
+    odd_place = lax.axis_index("space") % 2 == 1
+
+    def read(window, index):
+        tile, shift = found[(window, index)]
+        by_even = even_ref[tile]
+        by_odd = odd_ref[tile] + far_ref[tile]
+        west = jnp.where(odd_place, by_even, by_odd)
+        east = jnp.where(odd_place, by_odd, by_even)
+        if shift:
+            west = pltpu.roll(west, shift, 1)
+            east = pltpu.roll(east, width - shift, 1)
+        return west, east
+
+    return read
+
+
+def emit_to(out_ref):
+    rows = out_ref.shape[2]
 
     def emit(window, field):
         out_ref[window, 0] = field[:rows]
         out_ref[window, 1] = field[rows:]
 
-    start = jnp.concatenate([pw_ref[...], pc_ref[...], pe_ref[...]], axis=1)
-    adjoint_steps(
-        own_ref, west_ref, east_ref, dx_ref, dy_ref, start, own_ref.shape[0], emit, False
-    )
-
-
-def local_call(kernel, out_shape, count):
+    return emit
+
+
+def upper_kernel(own_ref, even_ref, odd_ref, far_ref, dx_ref, dy_ref, out_ref, sent_ref):
+    windows, _, _, width = own_ref.shape
+
+    @pl.when(lax.axis_index("tm") >= windows)
+    def _():
+        halo = halo_reader(windows, width, even_ref, odd_ref, far_ref)
+        moved = adjoint_steps(own_ref, halo, dx_ref, dy_ref, None, emit_to(out_ref), True)
+        sent_ref[...] = moved[:, width : 2 * width]
+
+
+def lower_kernel(
+    done_ref, own_ref, even_ref, odd_ref, far_ref, dx_ref, dy_ref, here_ref, pe_ref, po_ref, out_ref
+):
+    windows, _, _, width = own_ref.shape
+
+    @pl.when(lax.axis_index("tm") < windows)
+    def _():
+        halo = halo_reader(windows, width, even_ref, odd_ref, far_ref)
+        odd_place = lax.axis_index("space") % 2 == 1
+        by_even = pe_ref[...]
+        by_odd = po_ref[...]
+        west = jnp.where(odd_place, by_even, by_odd)
+        east = jnp.where(odd_place, by_odd, by_even)
+        start = jnp.concatenate([west, here_ref[...], east], axis=1)
+        adjoint_steps(own_ref, halo, dx_ref, dy_ref, start, emit_to(out_ref), False)
+
+
+def local_call(kernel, out_shape, count, aliases=None):
+    whole = pl.BlockSpec(memory_space=pltpu.VMEM)
     return pl.pallas_call(
         kernel,
         out_shape=out_shape,
-        in_specs=[pl.BlockSpec(memory_space=pltpu.VMEM)] * count,
-        out_specs=pl.BlockSpec(memory_space=pltpu.VMEM),
+        in_specs=[whole] * count,
+        out_specs=jax.tree.map(lambda _: whole, out_shape),
+        input_output_aliases=aliases or {},
         compiler_params=pltpu.CompilerParams(vmem_limit_bytes=32 * 1024 * 1024),
     )
 
 
 def on_device(forcing, wind_x, wind_y):
     members, _, levels, rows, width = forcing.shape
-    steps = wind_x.shape[1]
     tm = lax.axis_size("tm")
     space = lax.axis_size("space")
     group = levels
     groups = [list(range(i, i + group)) for i in range(0, tm, group)]
-
-    def flat(t, s):
-        return t * space + s % space
-
-    def moved_by(block, dt, ds):
+    layer = space // 2
+
+    def even_mate(s):
+        return s ^ 1
+
+    def odd_mate(s):
+        return (s + 1) % space if s % 2 else (s - 1) % space
+
+    def is_far(s):
+        return s % layer in (0, layer - 1)
+
+    def exchange(block, mate, times=range(tm), places_of=range(space), dt=0):
         pairs = [
-            (flat(t, s), flat(t + dt, s + ds))
-            for t in range(tm)
-            for s in range(space)
-            if 0 <= t + dt < tm
+            (t * space + s, (t + dt) * space + mate(s)) for t in times for s in places_of
         ]
         return lax.ppermute(block, ("tm", "space"), pairs)
+
+    near = [s for s in range(space) if not is_far(s)]
+    far = [s for s in range(space) if is_far(s)]
+    upper = range(group, tm)
+    lower = range(group)
 
     packed = jnp.concatenate([wind_x[0], wind_y[0], forcing[:, 0]], axis=0)
     packed = jnp.swapaxes(packed, 0, 1)
     own = lax.all_to_all(packed, "tm", 0, 0, axis_index_groups=groups, tiled=True)
-    west = moved_by(own, 0, 1)
-    east = moved_by(own, 0, -1)
+
+    tiles = jax.ShapeDtypeStruct((len(pair_tiles(group)), rows, width), jnp.float32)
+    to_even, to_odd = local_call(pack_kernel, (tiles, tiles), 1)(own)
+    far_upper = exchange(to_odd, odd_mate, upper, far)
+    even = exchange(to_even, even_mate)
+    odd = exchange(to_odd, odd_mate, places_of=near)
+    to_odd_later = to_odd + 0.0 * (even[0, 0, 0] + odd[0, 0, 0])
+    far_lower = exchange(to_odd_later, odd_mate, lower, far)
 
     table = lobatto_table() * np.float32(time_step)
     dx = jnp.asarray(np.kron(np.eye(width // 8, dtype=np.float32), table))
     dy = jnp.asarray(np.kron(np.eye(members * rows // 8, dtype=np.float32), table.T))
 
+    result_shape = jax.ShapeDtypeStruct((group, members, rows, width), jnp.float32)
     flat_field = jax.ShapeDtypeStruct((members * rows, width), jnp.float32)
-    sent = local_call(first_kernel, flat_field, 5)(own, west, east, dx, dy)
-    below = moved_by(sent, -group, 0)
-    below_west = moved_by(sent, -group, 1)
-    below_east = moved_by(sent, -group, -1)
-    result = local_call(
-        second_kernel, jax.ShapeDtypeStruct((group, members, rows, width), jnp.float32), 8
-    )(own, west, east, dx, dy, below_west, below, below_east)
+    done, sent = local_call(upper_kernel, (result_shape, flat_field), 6)(
+        own, even, odd, far_upper, dx, dy
+    )
+    from_here = exchange(sent, lambda s: s, upper, dt=-group)
+    from_even = exchange(sent, even_mate, upper, dt=-group)
+    from_odd = exchange(sent, odd_mate, upper, dt=-group)
+    result = local_call(lower_kernel, result_shape, 10, {0: 0})(
+        done, own, even, odd, far_lower, dx, dy, from_here, from_even, from_odd
+    )
     result = lax.all_to_all(result, "tm", 0, 0, axis_index_groups=groups, tiled=True)
     return jnp.swapaxes(result, 0, 1)[:, None]
 

time: 175 us -> 115 us (0.66)
  waiting for transfers between devices: 85.4 us -> 39.9 us
  blocking collectives: 52.4 us -> 40.9 us
  Pallas kernels: 13.6 us -> 6.68 us
    ppermute x5 -> x7, waiting for transfers between devices: 85.4 us -> 39.9 us  [exchange(): return lax.ppermute(block, ('tm', 'space'), pairs)]
    all_to_all x1, blocking collectives: 23.1 us -> 11.7 us  [on_device(): lax.all_to_all(result, 'tm', 0, 0, axis_index_groups=groups, tiled=True)]
    pallas_call x2 -> x3, Pallas kernels: 13.6 us -> 6.68 us  [the longest x1 6.41 us: on_device(): local_call(lower_kernel, result_shape, 10, {0: 0})]
    ppermute x5 -> x7, starting transfers between devices: 21.1 us -> 22.5 us  [exchange(): return lax.ppermute(block, ('tm', 'space'), pairs)]
  transfers between devices with their start and end apart: 5 -> 7, of which waited for: 4 -> 2; matrix products, arithmetic and copies ran while one was open for 0% -> 1% of each run, Pallas kernels for 0% -> 0%
where the time goes in v2:
time: 115 us; the launch traced here: 114 us
  blocking collectives  40.9 us (36%)
  waiting for transfers between devices  39.9 us (35%)
  starting transfers between devices  22.5 us (20%)
  Pallas kernels  6.68 us (6%)
  local copies, waits for them, and re-layouts  2.89 us (3%)
  between operations  1.38 us (1%)
    ppermute x7, waiting for transfers between devices, exchange(): return lax.ppermute(block, ('tm', 'space'), pairs)  39.9 us
    all_to_all x1, blocking collectives, on_device(): lax.all_to_all(packed, 'tm', 0, 0, axis_index_groups=groups, tiled=True)  29.2 us
    ppermute x7, starting transfers between devices, exchange(): return lax.ppermute(block, ('tm', 'space'), pairs)  22.5 us
    all_to_all x1, blocking collectives, on_device(): lax.all_to_all(result, 'tm', 0, 0, axis_index_groups=groups, tiled=True)  11.7 us
    pallas_call x1, Pallas kernels, on_device(): local_call(lower_kernel, result_shape, 10, {0: 0})  6.41 us
  transfers between devices with their start and end apart: 7, of which 2 were waited for; matrix products, arithmetic and copies ran while one was open for 1% of the time, Pallas kernels for 0%

profile of v2, /device:TPU:1, one launch (start us, length us, event | category | flops | bytes accessed | tf_op | source)
XLA Modules:
  0.0 114.3 jit_solution(8673588161401355393)
XLA Ops:
  0.0 1.0 copy.14
  1.0 0.1 copy-done.3
  1.2 0.1 maximum_bitcast_fusion
  1.2 29.2 %all_to_all.10.own_ref = f32[8,6,32,128]{3,2,1,0:T(8,128)S(1)} all-to-all(f32[8,6,32,128]{3,2,1,0:T(8,128)S(1)} %maximum_bitcast_fusion), channel_id=1, replica_groups={{0,32,64,96,128,160,192,224},{256,288,320,352,384,416,448,480},{1,33,65..., dimensions={0} | all-to-all | bytes 1572864 | tf_op jit(solution)/shard_map/all_to_all | solution.py:260
  30.4 0.3 shard_map.55
  30.7 1.9 %collective-permute-start = (f32[25,32,128]{2,1,0:T(8,128)S(1)}, f32[25,32,128]{2,1,0:T(8,128)S(1)}, u32[]{:S(2)}, u32[]{:S(2)}) collective-permute-start(f32[25,32,128]{2,1,0:T(8,128)S(1)} %get-tuple-element.9), channel_id=1, source_target_pairs={{0,1},{1,0},{2,3},{3,2},{4,5},{5,4},{6,7},{7,6},{8,9},{9,8},{10,11... | collective-permute-start | bytes 1228808 | tf_op jit(solution)/shard_map/ppermute | solution.py:251
  32.6 0.7 collective-permute-start.1
  33.3 0.7 collective-permute-start.2
  34.0 8.5 %collective-permute-done.even_ref = f32[25,32,128]{2,1,0:T(8,128)S(1)} collective-permute-done((f32[25,32,128]{2,1,0:T(8,128)S(1)}, f32[25,32,128]{2,1,0:T(8,128)S(1)}, u32[]{:S(2)}, u32[]{:S(2)}) %collective-permute-start) | collective-permute-done | bytes 409632 | tf_op jit(solution)/shard_map/ppermute | solution.py:251
  42.5 0.5 slice.8
  43.0 0.0 collective-permute-done.1.odd_ref
  43.0 0.5 slice.9
  44.8 0.0 copy-start
  44.8 0.0 copy-start.1
  44.8 15.3 %collective-permute-start.3 = (f32[25,32,128]{2,1,0:T(8,128)S(1)}, f32[25,32,128]{2,1,0:T(8,128)S(1)}, u32[]{:S(2)}, u32[]{:S(2)}) collective-permute-start(f32[25,32,128]{2,1,0:T(8,128)S(1)} %broadcast_add_fusion), channel_id=1, source_target_pairs={{0,31},{15,16},{16,15},{31,0},{32,63},{47,48},{48,47},{63,32},{64,... | collective-permute-start | bytes 1228808 | tf_op jit(solution)/shard_map/ppermute | solution.py:251
  60.1 0.0 collective-permute-done.2.far_ref
  60.2 1.3 %collective-permute-start.4 = (f32[64,128]{1,0:T(8,128)S(1)}, f32[64,128]{1,0:T(8,128)S(1)}, u32[]{:S(2)}, u32[]{:S(2)}) collective-permute-start(f32[64,128]{1,0:T(8,128)S(1)} %get-tuple-element.12), channel_id=1, source_target_pairs={{256,0},{257,1},{258,2},{259,3},{260,4},{261,5},{262,6},{263,7},{2... | collective-permute-start | bytes 98312 | tf_op jit(solution)/shard_map/ppermute | solution.py:251
  61.5 1.3 %collective-permute-start.5 = (f32[64,128]{1,0:T(8,128)S(1)}, f32[64,128]{1,0:T(8,128)S(1)}, u32[]{:S(2)}, u32[]{:S(2)}) collective-permute-start(f32[64,128]{1,0:T(8,128)S(1)} %get-tuple-element.12), channel_id=1, source_target_pairs={{256,1},{257,0},{258,3},{259,2},{260,5},{261,4},{262,7},{263,6},{2... | collective-permute-start | bytes 98312 | tf_op jit(solution)/shard_map/ppermute | solution.py:251
  62.8 1.3 %collective-permute-start.6 = (f32[64,128]{1,0:T(8,128)S(1)}, f32[64,128]{1,0:T(8,128)S(1)}, u32[]{:S(2)}, u32[]{:S(2)}) collective-permute-start(f32[64,128]{1,0:T(8,128)S(1)} %get-tuple-element.12), channel_id=1, source_target_pairs={{256,31},{257,2},{258,1},{259,4},{260,3},{261,6},{262,5},{263,8},{... | collective-permute-start | bytes 98312 | tf_op jit(solution)/shard_map/ppermute | solution.py:251
  64.1 31.3 %collective-permute-done.4.here_ref = f32[64,128]{1,0:T(8,128)S(1)} collective-permute-done((f32[64,128]{1,0:T(8,128)S(1)}, f32[64,128]{1,0:T(8,128)S(1)}, u32[]{:S(2)}, u32[]{:S(2)}) %collective-permute-start.4) | collective-permute-done | bytes 32800 | tf_op jit(solution)/shard_map/ppermute | solution.py:251
  95.4 0.0 collective-permute-done.5.pe_ref
  95.4 6.4 %shard_map.57 = f32[8,2,32,128]{3,2,1,0:T(8,128)S(1)} custom-call(f32[8,2,32,128]{3,2,1,0:T(8,128)S(1)} %get-tuple-element.11.done_ref, f32[8,6,32,128]{3,2,1,0:T(8,128)S(1)} %all_to_all.10.own_ref, f32[25,32,128]{2,1,0:T(8,128)S(1)} %collective-permute-done.even_ref, ...), custom_call_target="tpu_custom_call", output_to_operand_aliasing={{}: (0, {})} | custom-call | tf_op jit(solution)/shard_map/pallas_call | solution.py:282
  101.9 11.7 %all_to_all.11 = f32[8,2,32,128]{3,2,1,0:T(8,128)S(1)} all-to-all(f32[8,2,32,128]{3,2,1,0:T(8,128)S(1)} %shard_map.57), channel_id=1, replica_groups={{0,32,64,96,128,160,192,224},{256,288,320,352,384,416,448,480},{1,33,65..., dimensions={0} | all-to-all | bytes 524288 | tf_op jit(solution)/shard_map/all_to_all | solution.py:285
  113.6 0.7 copy.10
  (10 shorter events, 0.1 us)
Async XLA Ops:
  0.0 1.0 copy-start.2
  0.0 1.1 copy-start.3
  30.7 11.8 %collective-permute-start = (f32[25,32,128]{2,1,0:T(8,128)S(1)}, f32[25,32,128]{2,1,0:T(8,128)S(1)}, u32[]{:S(2)}, u32[]{:S(2)}) collective-permute-start(f32[25,32,128]{2,1,0:T(8,128)S(1)} %get-tuple-element.9), channel_id=1, source_target_pairs={{0,1},{1,0},{2,3},{3,2},{4,5},{5,4},{6,7},{7,6},{8,9},{9,8},{10,11... | collective-permute-start | bytes 1228808 | tf_op jit(solution)/shard_map/ppermute | solution.py:251
  32.6 10.4 %collective-permute-start.1 = (f32[25,32,128]{2,1,0:T(8,128)S(1)}, f32[25,32,128]{2,1,0:T(8,128)S(1)}, u32[]{:S(2)}, u32[]{:S(2)}) collective-permute-start(f32[25,32,128]{2,1,0:T(8,128)S(1)} %get-tuple-element.10), channel_id=1, source_target_pairs={{1,2},{2,1},{3,4},{4,3},{5,6},{6,5},{7,8},{8,7},{9,10},{10,9},{11,... | collective-permute-start | bytes 1228808 | tf_op jit(solution)/shard_map/ppermute | solution.py:251
  33.3 26.8 %collective-permute-start.2 = (f32[25,32,128]{2,1,0:T(8,128)S(1)}, f32[25,32,128]{2,1,0:T(8,128)S(1)}, u32[]{:S(2)}, u32[]{:S(2)}) collective-permute-start(f32[25,32,128]{2,1,0:T(8,128)S(1)} %get-tuple-element.10), channel_id=1, source_target_pairs={{256,287},{271,272},{272,271},{287,256},{288,319},{303,304},{304,3... | collective-permute-start | bytes 1228808 | tf_op jit(solution)/shard_map/ppermute | solution.py:251
  44.8 15.4 %copy-start = (f32[128,128]{1,0:T(8,128)S(1)}, f32[128,128]{1,0:T(8,128)}, u32[]{:S(2)}) copy-start(f32[128,128]{1,0:T(8,128)} %constant.7.clone.dx_ref) | copy-start | bytes 196612
  44.8 15.4 %copy-start.1 = (f32[64,64]{1,0:T(8,128)S(1)}, f32[64,64]{1,0:T(8,128)}, u32[]{:S(2)}) copy-start(f32[64,64]{1,0:T(8,128)} %constant.8.clone.dy_ref) | copy-start | bytes 49156
  44.8 50.6 %collective-permute-start.3 = (f32[25,32,128]{2,1,0:T(8,128)S(1)}, f32[25,32,128]{2,1,0:T(8,128)S(1)}, u32[]{:S(2)}, u32[]{:S(2)}) collective-permute-start(f32[25,32,128]{2,1,0:T(8,128)S(1)} %broadcast_add_fusion), channel_id=1, source_target_pairs={{0,31},{15,16},{16,15},{31,0},{32,63},{47,48},{48,47},{63,32},{64,... | collective-permute-start | bytes 1228808 | tf_op jit(solution)/shard_map/ppermute | solution.py:251
  60.2 35.2 %collective-permute-start.4 = (f32[64,128]{1,0:T(8,128)S(1)}, f32[64,128]{1,0:T(8,128)S(1)}, u32[]{:S(2)}, u32[]{:S(2)}) collective-permute-start(f32[64,128]{1,0:T(8,128)S(1)} %get-tuple-element.12), channel_id=1, source_target_pairs={{256,0},{257,1},{258,2},{259,3},{260,4},{261,5},{262,6},{263,7},{2... | collective-permute-start | bytes 98312 | tf_op jit(solution)/shard_map/ppermute | solution.py:251
  61.5 34.0 %collective-permute-start.5 = (f32[64,128]{1,0:T(8,128)S(1)}, f32[64,128]{1,0:T(8,128)S(1)}, u32[]{:S(2)}, u32[]{:S(2)}) collective-permute-start(f32[64,128]{1,0:T(8,128)S(1)} %get-tuple-element.12), channel_id=1, source_target_pairs={{256,1},{257,0},{258,3},{259,2},{260,5},{261,4},{262,7},{263,6},{2... | collective-permute-start | bytes 98312 | tf_op jit(solution)/shard_map/ppermute | solution.py:251
  62.8 32.7 %collective-permute-start.6 = (f32[64,128]{1,0:T(8,128)S(1)}, f32[64,128]{1,0:T(8,128)S(1)}, u32[]{:S(2)}, u32[]{:S(2)}) collective-permute-start(f32[64,128]{1,0:T(8,128)S(1)} %get-tuple-element.12), channel_id=1, source_target_pairs={{256,31},{257,2},{258,1},{259,4},{260,3},{261,6},{262,5},{263,8},{... | collective-permute-start | bytes 98312 | tf_op jit(solution)/shard_map/ppermute | solution.py:251

commit v3 on v2

v3 whole, which is shorter than its diff:
```python
import jax
import jax.numpy as jnp
import numpy as np
from jax import lax
from jax.experimental import pallas as pl
from jax.experimental.pallas import tpu as pltpu
from jax.sharding import PartitionSpec as P

time_step = 0.01
lobatto_points = [
    -1.0,
    -0.8717401485096066,
    -0.5917001814331423,
    -0.20929921790247888,
    0.20929921790247888,
    0.5917001814331423,
    0.8717401485096066,
    1.0,
]


def legendre_seven(point):
    before = 1.0
    current = point
    for order in range(1, 7):
        before, current = (
            current,
            ((2 * order + 1) * point * current - order * before) / (order + 1),
        )
    return current


def lobatto_table():
    values = [legendre_seven(point) for point in lobatto_points]
    table = np.zeros((8, 8))
    for row_index in range(8):
        for col_index in range(8):
            if row_index != col_index:
                table[row_index, col_index] = values[row_index] / (
                    values[col_index] * (lobatto_points[row_index] - lobatto_points[col_index])
                )
    table[0, 0] = -14.0
    table[7, 7] = 14.0
    return table.astype(np.float32)


def split_bf16(value):
    high = value.astype(jnp.bfloat16)
    return high, (value - high.astype(jnp.float32)).astype(jnp.bfloat16)


def derivative_tables(width):
    table = lobatto_table() * np.float32(time_step)
    along_x = np.kron(np.eye(width // 8, dtype=np.float32), table)
    high = along_x.astype(jnp.bfloat16)
    low = (along_x - high.astype(np.float32)).astype(jnp.bfloat16)
    product = np.zeros((2 * width, 2 * width), jnp.bfloat16)
    product[:width, :width] = high
    product[width:, :width] = high
    product[:width, width:] = low
    along_y = np.zeros((8, 8, width), np.float32)
    for shift in range(8):
        for node in range(8):
            along_y[shift, node, :] = table[(node - shift) % 8, node]
    return jnp.asarray(product), jnp.asarray(along_y)


def pair_tiles(windows):
    last = 2 * windows
    tiles = []

    def block(step, kind):
        return (windows - 1 - (step - 1) // 2, 2 * kind + (step % 2))

    for step in range(1, windows + 1):
        for kind in (0, 1):
            tiles.append((block(step, kind), block(last + 1 - step, kind), 8 * (last - step)))
    tiles.append(((windows - 1, 4), None, 16 * windows))
    tiles.append(((windows - 1, 5), None, 16 * windows))
    for window in range(windows - 2, windows // 2 - 1, -1):
        for member in (4, 5):
            tiles.append(
                ((window, member), (windows - 2 - window, member), 16 * (window + 1))
            )
    middle = windows // 2 - 1
    tiles.append(((middle, 4), (middle, 5), 16 * (middle + 1)))
    return tiles


def places(windows):
    found = {}
    for index, (first, second, columns) in enumerate(pair_tiles(windows)):
        found[first] = (index, 0)
        if second is not None:
            found[second] = (index, columns)
    return found


def layer_here():
    return lax.axis_index("space") // (lax.axis_size("space") // 2)


def gather_kernel(wind_x_ref, wind_y_ref, forcing_ref, out_ref, sems):
    levels = out_ref.shape[0]
    half = levels // 2
    layer = layer_here()
    copies = []
    for part in (0, 1):
        here = pl.ds(half * part, half)
        there = pl.ds(half * jnp.bitwise_xor(layer, part), half)
        for index in (0, 1):
            copies.append((wind_x_ref.at[0, index, here], out_ref.at[there, index]))
            copies.append((wind_y_ref.at[0, index, here], out_ref.at[there, 2 + index]))
            copies.append((forcing_ref.at[index, 0, here], out_ref.at[there, 4 + index]))
    copies = [
        pltpu.make_async_copy(source, target, sems.at[index])
        for index, (source, target) in enumerate(copies)
    ]
    for copy in copies:
        copy.start()
    for copy in copies:
        copy.wait()


def scatter_kernel(in_ref, out_ref, sems):
    levels = in_ref.shape[0]
    half = levels // 2
    layer = layer_here()
    copies = []
    for part in (0, 1):
        here = pl.ds(half * part, half)
        there = pl.ds(half * jnp.bitwise_xor(layer, part), half)
        for member in (0, 1):
            copies.append(
                pltpu.make_async_copy(
                    in_ref.at[there, member],
                    out_ref.at[member, 0, here],
                    sems.at[2 * part + member],
                )
            )
    for copy in copies:
        copy.start()
    for copy in copies:
        copy.wait()


def pack_kernel(own_ref, even_ref, odd_ref):
    windows, _, rows, width = own_ref.shape
    col = lax.broadcasted_iota(jnp.int32, (rows, width), 1)
    odd_place = lax.axis_index("space") % 2

    def write(low_ref, high_ref):
        for index, (first, second, columns) in enumerate(pair_tiles(windows)):
            one = own_ref[first[0], first[1]]
            if second is None:
                low_ref[index] = one
                high_ref[index] = one
                continue
            other = own_ref[second[0], second[1]]
            low_ref[index] = jnp.where(col < columns, one, pltpu.roll(other, columns, 1))
            high_ref[index] = jnp.where(
                col >= width - columns, one, pltpu.roll(other, width - columns, 1)
            )

    @pl.when(odd_place == 0)
    def _():
        write(odd_ref, even_ref)

    @pl.when(odd_place == 1)
    def _():
        write(even_ref, odd_ref)


def shift_tiles(tiles, distance):
    distance %= tiles.shape[0]
    return jnp.concatenate([tiles[-distance:], tiles[:-distance]], axis=0)


def roll_columns(value, distance):
    width = value.shape[-1]
    return pltpu.roll(value.reshape(-1, width), distance % width, 1).reshape(value.shape)


def roll_nodes(value, distance):
    width = value.shape[-1]
    return pltpu.roll(value.reshape(-1, 8, width), distance % 8, 1).reshape(value.shape)


def adjoint_step(field, wind_x, wind_y, along_x, along_y):
    count, blocks, _, width = field.shape
    elements = blocks // 2
    col = lax.broadcasted_iota(jnp.int32, (1, 1, 8, width), 3)
    node = lax.broadcasted_iota(jnp.int32, (1, 1, 8, width), 2)

    from_west = roll_columns(field, 1)
    from_east = roll_columns(field, -1)
    west = jnp.where(col == 0, shift_tiles(from_west, 1), from_west)
    east = jnp.where(col == width - 1, shift_tiles(from_east, -1), from_east)
    q = 0.5 * (field + jnp.where(col % 8 == 0, west, jnp.where(col % 8 == 7, east, field)))

    down = roll_nodes(q, 1)
    up = roll_nodes(q, -1)
    before = []
    after = []
    for first in range(0, blocks, elements):
        end = first + elements
        before += [q[:, first : first + 1], down[:, first : end - 1]]
        after += [up[:, first + 1 : end], q[:, end - 1 : end]]
    before = jnp.concatenate(before, axis=1)
    after = jnp.concatenate(after, axis=1)
    q = 0.5 * (q + jnp.where(node == 0, before, jnp.where(node == 7, after, q)))

    flux_x = (jnp.concatenate([wind_x, wind_x], axis=1) * q).reshape(-1, width)
    high, low = split_bf16(flux_x)
    grad_x = jnp.dot(
        jnp.concatenate([high, low], axis=1), along_x, preferred_element_type=jnp.float32
    )
    grad_x = (grad_x[:, :width] + grad_x[:, width:]).reshape(q.shape)

    flux_y = (jnp.concatenate([wind_y, wind_y], axis=1) * q).reshape(-1, 8, width)
    grad_y = along_y[0] * flux_y
    for shift in range(1, 8):
        grad_y = grad_y + along_y[shift] * pltpu.roll(flux_y, shift, 1)
    return q - (grad_x + grad_y.reshape(q.shape))


def sweep(own_ref, even_ref, odd_ref, far_refs, along_x_ref, along_y_ref, start, out_ref, last_moves):
    windows, _, rows, width = own_ref.shape
    found = places(windows)
    odd_place = lax.axis_index("space") % 2 == 1
    along_x = along_x_ref[...]
    along_y = [along_y_ref[shift] for shift in range(8)]
    col = lax.broadcasted_iota(jnp.int32, (rows, width), 1)
    col_tile = lax.broadcasted_iota(jnp.int32, (1, 1, 8, width), 3)

    def tiles(window, index, merged):
        tile, shift = found[(window, index)]
        by_even = even_ref[tile]
        by_odd = odd_ref[tile]
        for far_ref in far_refs:
            by_odd = by_odd + far_ref[tile]
        west = jnp.where(odd_place, by_even, by_odd)
        east = jnp.where(odd_place, by_odd, by_even)
        if shift:
            west = pltpu.roll(west, shift, 1)
            east = pltpu.roll(east, width - shift, 1)
        own = own_ref[window, index]
        if merged:
            parts = [own, jnp.where(col < width // 2, east, west)]
        else:
            parts = [own, east, west]
        return jnp.stack(parts).reshape(len(parts), rows // 8, 8, width)

    moved = start
    for window in range(windows - 1, -1, -1):
        merged = window < windows // 2
        field = jnp.concatenate([tiles(window, 4, merged), tiles(window, 5, merged)], axis=1)
        if moved is not None:
            if moved.shape[0] > field.shape[0]:
                side = jnp.where(col_tile < width // 2, moved[1:2], moved[2:3])
                moved = jnp.concatenate([moved[0:1], side], axis=0)
            field = field + moved
        here = field[0].reshape(2 * rows, width)
        out_ref[window, 0] = here[:rows]
        out_ref[window, 1] = here[rows:]
        if window == 0 and not last_moves:
            return None
        for substep in (1, 0):
            field = adjoint_step(
                field,
                tiles(window, substep, merged),
                tiles(window, 2 + substep, merged),
                along_x,
                along_y,
            )
        moved = field
    return moved[0].reshape(2 * rows, width)


def upper_kernel(
    own_ref, odd_ref, even_ref, to_odd_ref, along_x_ref, along_y_ref, out_ref, sent_ref, later_ref
):
    windows = own_ref.shape[0]

    @pl.when(lax.axis_index("tm") < windows)
    def _():
        later_ref[...] = to_odd_ref[...]

    @pl.when(lax.axis_index("tm") >= windows)
    def _():
        sent_ref[...] = sweep(
            own_ref, even_ref, odd_ref, (), along_x_ref, along_y_ref, None, out_ref, True
        )


def lower_kernel(
    done_ref, own_ref, even_ref, odd_ref, far_ref, along_x_ref, along_y_ref, here_ref, pe_ref, po_ref, out_ref
):
    windows, _, rows, width = own_ref.shape

    @pl.when(lax.axis_index("tm") < windows)
    def _():
        odd_place = lax.axis_index("space") % 2 == 1
        by_even = pe_ref[...]
        by_odd = po_ref[...]
        west = jnp.where(odd_place, by_even, by_odd)
        east = jnp.where(odd_place, by_odd, by_even)
        start = jnp.stack([here_ref[...], east, west]).reshape(3, 2 * rows // 8, 8, width)
        sweep(
            own_ref, even_ref, odd_ref, (far_ref,), along_x_ref, along_y_ref, start, out_ref, False
        )


def local_call(kernel, out_shape, in_specs, out_specs=None, vmem=32, **options):
    whole = pl.BlockSpec(memory_space=pltpu.VMEM)
    if isinstance(in_specs, int):
        in_specs = [whole] * in_specs
    return pl.pallas_call(
        kernel,
        out_shape=out_shape,
        in_specs=in_specs,
        out_specs=out_specs or jax.tree.map(lambda _: whole, out_shape),
        compiler_params=pltpu.CompilerParams(vmem_limit_bytes=vmem * 1024 * 1024),
        **options,
    )


def on_device(forcing, wind_x, wind_y):
    members, _, levels, rows, width = forcing.shape
    tm = lax.axis_size("tm")
    space = lax.axis_size("space")
    group = levels
    groups = [list(range(i, i + group)) for i in range(0, tm, group)]
    layer = space // 2
    anywhere = pl.BlockSpec(memory_space=pltpu.HBM)

    def same(t, s):
        return t, s

    def even_mate(t, s):
        return t, s ^ 1

    def is_far(s):
        return s % layer in (0, layer - 1)

    def odd_mate(t, s):
        mate = (s + 1) % space if s % 2 else (s - 1) % space
        return (t ^ (group // 2) if is_far(s) else t), mate

    def exchange(block, mate, chosen, dt=0):
        pairs = []
        for t in range(tm):
            for s in range(space):
                if chosen(t, s):
                    to_t, to_s = mate(t, s)
                    pairs.append((t * space + s, (to_t + dt) * space + to_s))
        return lax.ppermute(block, ("tm", "space"), pairs)

    def upper(t, s):
        return t >= group

    packed = local_call(
        gather_kernel,
        jax.ShapeDtypeStruct((levels, 6, rows, width), jnp.float32),
        [anywhere] * 3,
        vmem=61,
        scratch_shapes=[pltpu.SemaphoreType.DMA((12,))],
    )(wind_x, wind_y, forcing)
    own = lax.all_to_all(packed, "tm", 0, 0, axis_index_groups=groups, tiled=True)

    tiles = jax.ShapeDtypeStruct((len(pair_tiles(group)), rows, width), jnp.float32)
    to_even, to_odd = local_call(pack_kernel, (tiles, tiles), 1)(own)
    odd = exchange(to_odd, odd_mate, lambda t, s: upper(t, s) or not is_far(s))
    even = exchange(to_even, even_mate, lambda t, s: True)
    along_x, along_y = derivative_tables(width)
    result_shape = jax.ShapeDtypeStruct((group, members, rows, width), jnp.float32)
    flat_field = jax.ShapeDtypeStruct((members * rows, width), jnp.float32)
    done, sent, later = local_call(upper_kernel, (result_shape, flat_field, tiles), 6)(
        own, odd, even, to_odd, along_x, along_y
    )
    far = exchange(later, odd_mate, lambda t, s: is_far(s) and not upper(t, s))
    from_here = exchange(sent, same, upper, -group)
    from_even = exchange(sent, even_mate, upper, -group)
    from_odd = exchange(sent, odd_mate, upper, -group)
    result = local_call(lower_kernel, result_shape, 10, input_output_aliases={0: 0})(
        done, own, even, odd, far, along_x, along_y, from_here, from_even, from_odd
    )
    result = lax.all_to_all(result, "tm", 0, 0, axis_index_groups=groups, tiled=True)
    return local_call(
        scatter_kernel,
        jax.ShapeDtypeStruct(forcing.shape, jnp.float32),
        [pl.BlockSpec(memory_space=pltpu.VMEM)],
        anywhere,
        scratch_shapes=[pltpu.SemaphoreType.DMA((4,))],
    )(result)


def solution(mesh):
    placed = (
        P(None, "tm", None, None, "space"),
        P("tm", None, None, None, "space"),
        P("tm", None, None, None, "space"),
    )
    return jax.shard_map(
        on_device,
        mesh=mesh,
        in_specs=placed,
        out_specs=P(None, "tm", None, None, "space"),
        check_vma=False,
    )
```

time: 115 us -> 108 us (0.939)
  local copies, waits for them, and re-layouts: 2.89 us -> 0.01 us
  starting transfers between devices: 22.5 us -> 20.1 us
  between operations: 1.38 us -> 0.1 us
    ppermute x7 -> x6, starting transfers between devices: 22.5 us -> 20.1 us  [exchange(): return lax.ppermute(block, ('tm', 'space'), pairs)]
    ppermute x7 -> x6, waiting for transfers between devices: 39.9 us -> 38.8 us  [exchange(): return lax.ppermute(block, ('tm', 'space'), pairs)]
    pallas_call x2 -> x4, Pallas kernels: 6.43 us -> 6.29 us  [the longest x1 3.4 us: on_device(): local_call(lower_kernel, result_shape, 10, input_output_aliases={0: 0})]
  transfers between devices with their start and end apart: 7 -> 6, of which waited for: 2 -> 2; matrix products, arithmetic and copies ran while one was open for 1% -> 0% of each run, Pallas kernels for 0% -> 0%
where the time goes in v3:
time: 108 us
  blocking collectives  42 us (39%)
  waiting for transfers between devices  38.8 us (36%)
  starting transfers between devices  20.1 us (19%)
  Pallas kernels  6.54 us (6%)
    ppermute x6, waiting for transfers between devices, exchange(): return lax.ppermute(block, ('tm', 'space'), pairs)  38.8 us
    all_to_all x1, blocking collectives, on_device(): lax.all_to_all(packed, 'tm', 0, 0, axis_index_groups=groups, tiled=True)  30.3 us
    ppermute x6, starting transfers between devices, exchange(): return lax.ppermute(block, ('tm', 'space'), pairs)  20.1 us
    all_to_all x1, blocking collectives, on_device(): lax.all_to_all(result, 'tm', 0, 0, axis_index_groups=groups, tiled=True)  11.7 us
    pallas_call x1, Pallas kernels, on_device(): local_call(lower_kernel, result_shape, 10, input_output_aliases={0: 0})  3.4 us
  transfers between devices with their start and end apart: 6, of which 2 were waited for; matrix products, arithmetic and copies ran while one was open for 0% of the time, Pallas kernels for 0%

profile of v3, /device:TPU:1, one launch (start us, length us, event | category | flops | bytes accessed | tf_op | source)
XLA Modules:
  0.0 107.6 jit_solution(14374578525566916729)
XLA Ops:
  0.0 2.1 %shard_map.55 = f32[8,6,32,128]{3,2,1,0:T(8,128)} custom-call(f32[1,2,8,32,128]{4,3,2,1,0:T(8,128)} %wind_x_ref.1, f32[1,2,8,32,128]{4,3,2,1,0:T(8,128)} %wind_y_ref.1, f32[2,1,8,32,128]{4,3,2,1,0:T(8,128)} %forcing_ref.1), custom_call_target="tpu_custom_call" | custom-call | tf_op jit(solution)/shard_map/pallas_call | solution.py:362
  2.1 30.3 %all_to_all.10.own_ref = f32[8,6,32,128]{3,2,1,0:T(8,128)S(1)} all-to-all(f32[8,6,32,128]{3,2,1,0:T(8,128)} %shard_map.55), channel_id=1, replica_groups={{0,32,64,96,128,160,192,224},{256,288,320,352,384,416,448,480},{1,33,65..., dimensions={0} | all-to-all | bytes 1572864 | tf_op jit(solution)/shard_map/all_to_all | solution.py:369
  32.4 0.0 copy-start
  32.4 0.0 copy-start.1
  32.4 0.3 shard_map.56
  32.7 0.7 collective-permute-start
  33.4 2.6 %collective-permute-start.1 = (f32[25,32,128]{2,1,0:T(8,128)S(1)}, f32[25,32,128]{2,1,0:T(8,128)S(1)}, u32[]{:S(2)}, u32[]{:S(2)}) collective-permute-start(f32[25,32,128]{2,1,0:T(8,128)S(1)} %get-tuple-element.11), channel_id=1, source_target_pairs={{0,1},{1,0},{2,3},{3,2},{4,5},{5,4},{6,7},{7,6},{8,9},{9,8},{10,11... | collective-permute-start | bytes 1228808 | tf_op jit(solution)/shard_map/ppermute | solution.py:357
  36.0 0.0 collective-permute-done.odd_ref
  36.0 9.2 %collective-permute-done.1.even_ref = f32[25,32,128]{2,1,0:T(8,128)S(1)} collective-permute-done((f32[25,32,128]{2,1,0:T(8,128)S(1)}, f32[25,32,128]{2,1,0:T(8,128)S(1)}, u32[]{:S(2)}, u32[]{:S(2)}) %collective-permute-start.1) | collective-permute-done | bytes 409632 | tf_op jit(solution)/shard_map/ppermute | solution.py:357
  45.2 0.0 copy-done
  45.2 0.0 copy-done.1
  45.2 12.9 %collective-permute-start.2 = (f32[25,32,128]{2,1,0:T(8,128)S(1)}, f32[25,32,128]{2,1,0:T(8,128)S(1)}, u32[]{:S(2)}, u32[]{:S(2)}) collective-permute-start(f32[25,32,128]{2,1,0:T(8,128)S(1)} %get-tuple-element.13), channel_id=1, source_target_pairs={{0,159},{15,144},{16,143},{31,128},{32,191},{47,176},{48,175},{63,... | collective-permute-start | bytes 1228808 | tf_op jit(solution)/shard_map/ppermute | solution.py:357
  58.2 1.3 %collective-permute-start.3 = (f32[64,128]{1,0:T(8,128)S(1)}, f32[64,128]{1,0:T(8,128)S(1)}, u32[]{:S(2)}, u32[]{:S(2)}) collective-permute-start(f32[64,128]{1,0:T(8,128)S(1)} %get-tuple-element.14), channel_id=1, source_target_pairs={{256,0},{257,1},{258,2},{259,3},{260,4},{261,5},{262,6},{263,7},{2... | collective-permute-start | bytes 98312 | tf_op jit(solution)/shard_map/ppermute | solution.py:357
  59.5 1.3 %collective-permute-start.4 = (f32[64,128]{1,0:T(8,128)S(1)}, f32[64,128]{1,0:T(8,128)S(1)}, u32[]{:S(2)}, u32[]{:S(2)}) collective-permute-start(f32[64,128]{1,0:T(8,128)S(1)} %get-tuple-element.14), channel_id=1, source_target_pairs={{256,1},{257,0},{258,3},{259,2},{260,5},{261,4},{262,7},{263,6},{2... | collective-permute-start | bytes 98312 | tf_op jit(solution)/shard_map/ppermute | solution.py:357
  60.8 1.3 %collective-permute-start.5 = (f32[64,128]{1,0:T(8,128)S(1)}, f32[64,128]{1,0:T(8,128)S(1)}, u32[]{:S(2)}, u32[]{:S(2)}) collective-permute-start(f32[64,128]{1,0:T(8,128)S(1)} %get-tuple-element.14), channel_id=1, source_target_pairs={{256,159},{257,2},{258,1},{259,4},{260,3},{261,6},{262,5},{263,8},... | collective-permute-start | bytes 98312 | tf_op jit(solution)/shard_map/ppermute | solution.py:357
  62.1 29.7 %collective-permute-done.3.here_ref = f32[64,128]{1,0:T(8,128)S(1)} collective-permute-done((f32[64,128]{1,0:T(8,128)S(1)}, f32[64,128]{1,0:T(8,128)S(1)}, u32[]{:S(2)}, u32[]{:S(2)}) %collective-permute-start.3) | collective-permute-done | bytes 32800 | tf_op jit(solution)/shard_map/ppermute | solution.py:357
  91.7 0.0 collective-permute-done.4.pe_ref
  91.7 0.0 collective-permute-done.5.po_ref
  91.7 0.0 collective-permute-done.2.far_ref
  91.7 3.4 %shard_map.58 = f32[8,2,32,128]{3,2,1,0:T(8,128)S(1)} custom-call(f32[8,2,32,128]{3,2,1,0:T(8,128)S(1)} %get-tuple-element.12.done_ref, f32[8,6,32,128]{3,2,1,0:T(8,128)S(1)} %all_to_all.10.own_ref, f32[25,32,128]{2,1,0:T(8,128)S(1)} %collective-permute-done.1.even_ref, ...), custom_call_target="tpu_custom_call", output_to_operand_aliasing={{}: (0, {})} | custom-call | tf_op jit(solution)/shard_map/pallas_call | solution.py:385
  95.1 11.7 %all_to_all.11.in_ref = f32[8,2,32,128]{3,2,1,0:T(8,128)S(1)} all-to-all(f32[8,2,32,128]{3,2,1,0:T(8,128)S(1)} %shard_map.58), channel_id=1, replica_groups={{0,32,64,96,128,160,192,224},{256,288,320,352,384,416,448,480},{1,33,65..., dimensions={0} | all-to-all | bytes 524288 | tf_op jit(solution)/shard_map/all_to_all | solution.py:388
  106.8 0.7 shard_map.59
  (1 shorter events, 0.0 us)
Async XLA Ops:
  32.4 12.8 %copy-start = (bf16[256,256]{1,0:T(8,128)(2,1)S(1)}, bf16[256,256]{1,0:T(8,128)(2,1)}, u32[]{:S(2)}) copy-start(bf16[256,256]{1,0:T(8,128)(2,1)} %constant.4.clone.along_x_ref) | copy-start | bytes 393220
  32.4 12.8 %copy-start.1 = (f32[8,8,128]{2,1,0:T(8,128)S(1)}, f32[8,8,128]{2,1,0:T(8,128)}, u32[]{:S(2)}) copy-start(f32[8,8,128]{2,1,0:T(8,128)} %constant.5.clone.along_y_ref) | copy-start | bytes 98308
  32.7 3.3 %collective-permute-start = (f32[25,32,128]{2,1,0:T(8,128)S(1)}, f32[25,32,128]{2,1,0:T(8,128)S(1)}, u32[]{:S(2)}, u32[]{:S(2)}) collective-permute-start(f32[25,32,128]{2,1,0:T(8,128)S(1)} %get-tuple-element.10.to_odd_ref), channel_id=1, source_target_pairs={{1,2},{2,1},{3,4},{4,3},{5,6},{6,5},{7,8},{8,7},{9,10},{10,9},{11,... | collective-permute-start | bytes 1228808 | tf_op jit(solution)/shard_map/ppermute | solution.py:357
  33.4 11.8 %collective-permute-start.1 = (f32[25,32,128]{2,1,0:T(8,128)S(1)}, f32[25,32,128]{2,1,0:T(8,128)S(1)}, u32[]{:S(2)}, u32[]{:S(2)}) collective-permute-start(f32[25,32,128]{2,1,0:T(8,128)S(1)} %get-tuple-element.11), channel_id=1, source_target_pairs={{0,1},{1,0},{2,3},{3,2},{4,5},{5,4},{6,7},{7,6},{8,9},{9,8},{10,11... | collective-permute-start | bytes 1228808 | tf_op jit(solution)/shard_map/ppermute | solution.py:357
  45.2 46.5 %collective-permute-start.2 = (f32[25,32,128]{2,1,0:T(8,128)S(1)}, f32[25,32,128]{2,1,0:T(8,128)S(1)}, u32[]{:S(2)}, u32[]{:S(2)}) collective-permute-start(f32[25,32,128]{2,1,0:T(8,128)S(1)} %get-tuple-element.13), channel_id=1, source_target_pairs={{0,159},{15,144},{16,143},{31,128},{32,191},{47,176},{48,175},{63,... | collective-permute-start | bytes 1228808 | tf_op jit(solution)/shard_map/ppermute | solution.py:357
  58.2 33.6 %collective-permute-start.3 = (f32[64,128]{1,0:T(8,128)S(1)}, f32[64,128]{1,0:T(8,128)S(1)}, u32[]{:S(2)}, u32[]{:S(2)}) collective-permute-start(f32[64,128]{1,0:T(8,128)S(1)} %get-tuple-element.14), channel_id=1, source_target_pairs={{256,0},{257,1},{258,2},{259,3},{260,4},{261,5},{262,6},{263,7},{2... | collective-permute-start | bytes 98312 | tf_op jit(solution)/shard_map/ppermute | solution.py:357
  59.5 32.3 %collective-permute-start.4 = (f32[64,128]{1,0:T(8,128)S(1)}, f32[64,128]{1,0:T(8,128)S(1)}, u32[]{:S(2)}, u32[]{:S(2)}) collective-permute-start(f32[64,128]{1,0:T(8,128)S(1)} %get-tuple-element.14), channel_id=1, source_target_pairs={{256,1},{257,0},{258,3},{259,2},{260,5},{261,4},{262,7},{263,6},{2... | collective-permute-start | bytes 98312 | tf_op jit(solution)/shard_map/ppermute | solution.py:357
  60.8 31.0 %collective-permute-start.5 = (f32[64,128]{1,0:T(8,128)S(1)}, f32[64,128]{1,0:T(8,128)S(1)}, u32[]{:S(2)}, u32[]{:S(2)}) collective-permute-start(f32[64,128]{1,0:T(8,128)S(1)} %get-tuple-element.14), channel_id=1, source_target_pairs={{256,159},{257,2},{258,1},{259,4},{260,3},{261,6},{262,5},{263,8},... | collective-permute-start | bytes 98312 | tf_op jit(solution)/shard_map/ppermute | solution.py:357

commit v4 on v3

--- a/solution.py
+++ b/solution.py
@@ -1,3 +1,5 @@
+import functools
+
 import jax
 import jax.numpy as jnp
 import numpy as np
@@ -144,31 +146,33 @@
         copy.wait()
 
 
-def pack_kernel(own_ref, even_ref, odd_ref):
+def pack_kernel(towards_even, own_ref, *refs):
+    out_ref = refs[-1]
     windows, _, rows, width = own_ref.shape
     col = lax.broadcasted_iota(jnp.int32, (rows, width), 1)
-    odd_place = lax.axis_index("space") % 2
-
-    def write(low_ref, high_ref):
+    to_east = (lax.axis_index("space") % 2 == 0) == towards_even
+
+    def write(high):
         for index, (first, second, columns) in enumerate(pair_tiles(windows)):
-            one = own_ref[first[0], first[1]]
-            if second is None:
-                low_ref[index] = one
-                high_ref[index] = one
-                continue
-            other = own_ref[second[0], second[1]]
-            low_ref[index] = jnp.where(col < columns, one, pltpu.roll(other, columns, 1))
-            high_ref[index] = jnp.where(
-                col >= width - columns, one, pltpu.roll(other, width - columns, 1)
-            )
-
-    @pl.when(odd_place == 0)
+            value = own_ref[first[0], first[1]]
+            if second is not None:
+                other = own_ref[second[0], second[1]]
+                if high:
+                    keep = col >= width - columns
+                    other = pltpu.roll(other, width - columns, 1)
+                else:
+                    keep = col < columns
+                    other = pltpu.roll(other, columns, 1)
+                value = jnp.where(keep, value, other)
+            out_ref[index] = value
+
+    @pl.when(to_east)
     def _():
-        write(odd_ref, even_ref)
-
-    @pl.when(odd_place == 1)
+        write(True)
+
+    @pl.when(jnp.logical_not(to_east))
     def _():
-        write(even_ref, odd_ref)
+        write(False)
 
 
 def shift_tiles(tiles, distance):
@@ -277,14 +281,8 @@
     return moved[0].reshape(2 * rows, width)
 
 
-def upper_kernel(
-    own_ref, odd_ref, even_ref, to_odd_ref, along_x_ref, along_y_ref, out_ref, sent_ref, later_ref
-):
+def upper_kernel(own_ref, odd_ref, even_ref, along_x_ref, along_y_ref, out_ref, sent_ref):
     windows = own_ref.shape[0]
-
-    @pl.when(lax.axis_index("tm") < windows)
-    def _():
-        later_ref[...] = to_odd_ref[...]
 
     @pl.when(lax.axis_index("tm") >= windows)
     def _():
@@ -332,6 +330,7 @@
     group = levels
     groups = [list(range(i, i + group)) for i in range(0, tm, group)]
     layer = space // 2
+    anything = pl.BlockSpec(memory_space=pl.ANY)
     anywhere = pl.BlockSpec(memory_space=pltpu.HBM)
 
     def same(t, s):
@@ -369,16 +368,22 @@
     own = lax.all_to_all(packed, "tm", 0, 0, axis_index_groups=groups, tiled=True)
 
     tiles = jax.ShapeDtypeStruct((len(pair_tiles(group)), rows, width), jnp.float32)
-    to_even, to_odd = local_call(pack_kernel, (tiles, tiles), 1)(own)
+    to_odd = local_call(functools.partial(pack_kernel, False), tiles, 1)(own)
     odd = exchange(to_odd, odd_mate, lambda t, s: upper(t, s) or not is_far(s))
+    relayed = exchange(to_odd, even_mate, lambda t, s: is_far(s) and not upper(t, s))
+    far = exchange(
+        relayed, lambda t, s: odd_mate(t, s ^ 1), lambda t, s: is_far(s ^ 1) and not upper(t, s)
+    )
+    to_even = local_call(
+        functools.partial(pack_kernel, True), tiles, [pl.BlockSpec(memory_space=pltpu.VMEM), anything]
+    )(own, relayed)
     even = exchange(to_even, even_mate, lambda t, s: True)
     along_x, along_y = derivative_tables(width)
     result_shape = jax.ShapeDtypeStruct((group, members, rows, width), jnp.float32)
     flat_field = jax.ShapeDtypeStruct((members * rows, width), jnp.float32)
-    done, sent, later = local_call(upper_kernel, (result_shape, flat_field, tiles), 6)(
-        own, odd, even, to_odd, along_x, along_y
-    )
-    far = exchange(later, odd_mate, lambda t, s: is_far(s) and not upper(t, s))
+    done, sent = local_call(upper_kernel, (result_shape, flat_field), 5)(
+        own, odd, even, along_x, along_y
+    )
     from_here = exchange(sent, same, upper, -group)
     from_even = exchange(sent, even_mate, upper, -group)
     from_odd = exchange(sent, odd_mate, upper, -group)

time: 108 us -> 102 us (0.944)
  starting transfers between devices: 20.1 us -> 11.4 us
  waiting for transfers between devices: 38.8 us -> 41.3 us
    ppermute x6 -> x7, starting transfers between devices: 20.1 us -> 11.4 us  [exchange(): return lax.ppermute(block, ('tm', 'space'), pairs)]
    ppermute x6 -> x7, waiting for transfers between devices: 38.8 us -> 41.3 us  [exchange(): return lax.ppermute(block, ('tm', 'space'), pairs)]
  transfers between devices with their start and end apart: 6 -> 7, of which waited for: 2 -> 5; matrix products, arithmetic and copies ran while one was open for 0% -> 0% of each run, Pallas kernels for 0% -> 0%
where the time goes in v4:
time: 102 us; the launch traced here: 101 us
  blocking collectives  42 us (41%)
  waiting for transfers between devices  41.3 us (40%)
  starting transfers between devices  11.4 us (11%)
  Pallas kernels  6.58 us (6%)
    ppermute x7, waiting for transfers between devices, exchange(): return lax.ppermute(block, ('tm', 'space'), pairs)  41.3 us
    all_to_all x1, blocking collectives, on_device(): lax.all_to_all(packed, 'tm', 0, 0, axis_index_groups=groups, tiled=True)  30.3 us
    all_to_all x1, blocking collectives, on_device(): lax.all_to_all(result, 'tm', 0, 0, axis_index_groups=groups, tiled=True)  11.7 us
    ppermute x7, starting transfers between devices, exchange(): return lax.ppermute(block, ('tm', 'space'), pairs)  11.4 us
    pallas_call x1, Pallas kernels, on_device(): local_call(lower_kernel, result_shape, 10, input_output_aliases={0: 0})  3.39 us
    pallas_call x1, Pallas kernels, on_device(): local_call(gather_kernel, jax.ShapeDtypeStruct((levels, 6, rows, width),...  2.14 us
  transfers between devices with their start and end apart: 7, of which 5 were waited for; matrix products, arithmetic and copies ran while one was open for 0% of the time, Pallas kernels for 0%

profile of v4, /device:TPU:1, one launch (start us, length us, event | category | flops | bytes accessed | tf_op | source)
XLA Modules:
  0.0 101.4 jit_solution(11555207925346276411)
XLA Ops:
  0.0 2.1 %shard_map.55 = f32[8,6,32,128]{3,2,1,0:T(8,128)} custom-call(f32[1,2,8,32,128]{4,3,2,1,0:T(8,128)} %wind_x_ref.1, f32[1,2,8,32,128]{4,3,2,1,0:T(8,128)} %wind_y_ref.1, f32[2,1,8,32,128]{4,3,2,1,0:T(8,128)} %forcing_ref.1), custom_call_target="tpu_custom_call" | custom-call | tf_op jit(solution)/shard_map/pallas_call | solution.py:361
  2.1 30.3 %all_to_all.10.own_ref = f32[8,6,32,128]{3,2,1,0:T(8,128)S(1)} all-to-all(f32[8,6,32,128]{3,2,1,0:T(8,128)} %shard_map.55), channel_id=1, replica_groups={{0,32,64,96,128,160,192,224},{256,288,320,352,384,416,448,480},{1,33,65..., dimensions={0} | all-to-all | bytes 1572864 | tf_op jit(solution)/shard_map/all_to_all | solution.py:368
  32.4 0.2 shard_map.56
  32.6 0.0 copy-start
  32.6 0.0 copy-start.1
  32.6 1.4 %collective-permute-start.1 = (f32[25,32,128]{2,1,0:T(8,128)S(1)}, f32[25,32,128]{2,1,0:T(8,128)S(1)}, u32[]{:S(2)}, u32[]{:S(2)}) collective-permute-start(f32[25,32,128]{2,1,0:T(8,128)S(1)} %shard_map.56), channel_id=1, source_target_pairs={{0,1},{15,14},{16,17},{31,30},{32,33},{47,46},{48,49},{63,62},{64,... | collective-permute-start | bytes 1228808 | tf_op jit(solution)/shard_map/ppermute | solution.py:356
  34.1 0.7 collective-permute-start
  34.8 7.3 %collective-permute-done.1.refs_0_ = f32[25,32,128]{2,1,0:T(8,128)S(1)} collective-permute-done((f32[25,32,128]{2,1,0:T(8,128)S(1)}, f32[25,32,128]{2,1,0:T(8,128)S(1)}, u32[]{:S(2)}, u32[]{:S(2)}) %collective-permute-start.1) | collective-permute-done | bytes 409632 | tf_op jit(solution)/shard_map/ppermute | solution.py:356
  42.1 0.2 shard_map.57
  42.2 4.1 %collective-permute-start.2 = (f32[25,32,128]{2,1,0:T(8,128)S(1)}, f32[25,32,128]{2,1,0:T(8,128)S(1)}, u32[]{:S(2)}, u32[]{:S(2)}) collective-permute-start(f32[25,32,128]{2,1,0:T(8,128)S(1)} %shard_map.57), channel_id=1, source_target_pairs={{0,1},{1,0},{2,3},{3,2},{4,5},{5,4},{6,7},{7,6},{8,9},{9,8},{10,11... | collective-permute-start | bytes 1228808 | tf_op jit(solution)/shard_map/ppermute | solution.py:356
  46.3 1.3 %collective-permute-start.3 = (f32[25,32,128]{2,1,0:T(8,128)S(1)}, f32[25,32,128]{2,1,0:T(8,128)S(1)}, u32[]{:S(2)}, u32[]{:S(2)}) collective-permute-start(f32[25,32,128]{2,1,0:T(8,128)S(1)} %collective-permute-done.1.refs_0_), channel_id=1, source_target_pairs={{1,159},{14,144},{17,143},{30,128},{33,191},{46,176},{49,175},{62,... | collective-permute-start | bytes 1228808 | tf_op jit(solution)/shard_map/ppermute | solution.py:356
  47.6 0.0 collective-permute-done.odd_ref
  47.7 6.8 %collective-permute-done.2.even_ref = f32[25,32,128]{2,1,0:T(8,128)S(1)} collective-permute-done((f32[25,32,128]{2,1,0:T(8,128)S(1)}, f32[25,32,128]{2,1,0:T(8,128)S(1)}, u32[]{:S(2)}, u32[]{:S(2)}) %collective-permute-start.2) | collective-permute-done | bytes 409632 | tf_op jit(solution)/shard_map/ppermute | solution.py:356
  54.5 0.0 copy-done
  54.5 1.3 %collective-permute-start.6 = (f32[64,128]{1,0:T(8,128)S(1)}, f32[64,128]{1,0:T(8,128)S(1)}, u32[]{:S(2)}, u32[]{:S(2)}) collective-permute-start(f32[64,128]{1,0:T(8,128)S(1)} %get-tuple-element.8), channel_id=1, source_target_pairs={{256,159},{257,2},{258,1},{259,4},{260,3},{261,6},{262,5},{263,8},... | collective-permute-start | bytes 98312 | tf_op jit(solution)/shard_map/ppermute | solution.py:356
  55.8 1.3 %collective-permute-start.5 = (f32[64,128]{1,0:T(8,128)S(1)}, f32[64,128]{1,0:T(8,128)S(1)}, u32[]{:S(2)}, u32[]{:S(2)}) collective-permute-start(f32[64,128]{1,0:T(8,128)S(1)} %get-tuple-element.8), channel_id=1, source_target_pairs={{256,1},{257,0},{258,3},{259,2},{260,5},{261,4},{262,7},{263,6},{2... | collective-permute-start | bytes 98312 | tf_op jit(solution)/shard_map/ppermute | solution.py:356
  57.1 1.3 %collective-permute-start.4 = (f32[64,128]{1,0:T(8,128)S(1)}, f32[64,128]{1,0:T(8,128)S(1)}, u32[]{:S(2)}, u32[]{:S(2)}) collective-permute-start(f32[64,128]{1,0:T(8,128)S(1)} %get-tuple-element.8), channel_id=1, source_target_pairs={{256,0},{257,1},{258,2},{259,3},{260,4},{261,5},{262,6},{263,7},{2... | collective-permute-start | bytes 98312 | tf_op jit(solution)/shard_map/ppermute | solution.py:356
  58.4 10.4 %collective-permute-done.3.far_ref = f32[25,32,128]{2,1,0:T(8,128)S(1)} collective-permute-done((f32[25,32,128]{2,1,0:T(8,128)S(1)}, f32[25,32,128]{2,1,0:T(8,128)S(1)}, u32[]{:S(2)}, u32[]{:S(2)}) %collective-permute-start.3) | collective-permute-done | bytes 409632 | tf_op jit(solution)/shard_map/ppermute | solution.py:356
  68.8 10.3 %collective-permute-done.6.po_ref = f32[64,128]{1,0:T(8,128)S(1)} collective-permute-done((f32[64,128]{1,0:T(8,128)S(1)}, f32[64,128]{1,0:T(8,128)S(1)}, u32[]{:S(2)}, u32[]{:S(2)}) %collective-permute-start.6) | collective-permute-done | bytes 32800 | tf_op jit(solution)/shard_map/ppermute | solution.py:356
  79.1 6.5 %collective-permute-done.5.pe_ref = f32[64,128]{1,0:T(8,128)S(1)} collective-permute-done((f32[64,128]{1,0:T(8,128)S(1)}, f32[64,128]{1,0:T(8,128)S(1)}, u32[]{:S(2)}, u32[]{:S(2)}) %collective-permute-start.5) | collective-permute-done | bytes 32800 | tf_op jit(solution)/shard_map/ppermute | solution.py:356
  85.5 0.0 collective-permute-done.4.here_ref
  85.5 3.4 %shard_map.59 = f32[8,2,32,128]{3,2,1,0:T(8,128)S(1)} custom-call(f32[8,2,32,128]{3,2,1,0:T(8,128)S(1)} %get-tuple-element.7.done_ref, f32[8,6,32,128]{3,2,1,0:T(8,128)S(1)} %all_to_all.10.own_ref, f32[25,32,128]{2,1,0:T(8,128)S(1)} %collective-permute-done.2.even_ref, ...), custom_call_target="tpu_custom_call", output_to_operand_aliasing={{}: (0, {})} | custom-call | tf_op jit(solution)/shard_map/pallas_call | solution.py:390
  88.9 11.7 %all_to_all.11.in_ref = f32[8,2,32,128]{3,2,1,0:T(8,128)S(1)} all-to-all(f32[8,2,32,128]{3,2,1,0:T(8,128)S(1)} %shard_map.59), channel_id=1, replica_groups={{0,32,64,96,128,160,192,224},{256,288,320,352,384,416,448,480},{1,33,65..., dimensions={0} | all-to-all | bytes 524288 | tf_op jit(solution)/shard_map/all_to_all | solution.py:393
  100.6 0.7 shard_map.60
  (2 shorter events, 0.0 us)
Async XLA Ops:
  32.6 21.9 %copy-start = (bf16[256,256]{1,0:T(8,128)(2,1)S(1)}, bf16[256,256]{1,0:T(8,128)(2,1)}, u32[]{:S(2)}) copy-start(bf16[256,256]{1,0:T(8,128)(2,1)} %constant.4.clone.along_x_ref) | copy-start | bytes 393220
  32.6 21.9 %copy-start.1 = (f32[8,8,128]{2,1,0:T(8,128)S(1)}, f32[8,8,128]{2,1,0:T(8,128)}, u32[]{:S(2)}) copy-start(f32[8,8,128]{2,1,0:T(8,128)} %constant.5.clone.along_y_ref) | copy-start | bytes 98308
  32.6 9.4 %collective-permute-start.1 = (f32[25,32,128]{2,1,0:T(8,128)S(1)}, f32[25,32,128]{2,1,0:T(8,128)S(1)}, u32[]{:S(2)}, u32[]{:S(2)}) collective-permute-start(f32[25,32,128]{2,1,0:T(8,128)S(1)} %shard_map.56), channel_id=1, source_target_pairs={{0,1},{15,14},{16,17},{31,30},{32,33},{47,46},{48,49},{63,62},{64,... | collective-permute-start | bytes 1228808 | tf_op jit(solution)/shard_map/ppermute | solution.py:356
  34.1 13.6 %collective-permute-start = (f32[25,32,128]{2,1,0:T(8,128)S(1)}, f32[25,32,128]{2,1,0:T(8,128)S(1)}, u32[]{:S(2)}, u32[]{:S(2)}) collective-permute-start(f32[25,32,128]{2,1,0:T(8,128)S(1)} %shard_map.56), channel_id=1, source_target_pairs={{1,2},{2,1},{3,4},{4,3},{5,6},{6,5},{7,8},{8,7},{9,10},{10,9},{11,... | collective-permute-start | bytes 1228808 | tf_op jit(solution)/shard_map/ppermute | solution.py:356
  42.2 12.2 %collective-permute-start.2 = (f32[25,32,128]{2,1,0:T(8,128)S(1)}, f32[25,32,128]{2,1,0:T(8,128)S(1)}, u32[]{:S(2)}, u32[]{:S(2)}) collective-permute-start(f32[25,32,128]{2,1,0:T(8,128)S(1)} %shard_map.57), channel_id=1, source_target_pairs={{0,1},{1,0},{2,3},{3,2},{4,5},{5,4},{6,7},{7,6},{8,9},{9,8},{10,11... | collective-permute-start | bytes 1228808 | tf_op jit(solution)/shard_map/ppermute | solution.py:356
  46.3 22.4 %collective-permute-start.3 = (f32[25,32,128]{2,1,0:T(8,128)S(1)}, f32[25,32,128]{2,1,0:T(8,128)S(1)}, u32[]{:S(2)}, u32[]{:S(2)}) collective-permute-start(f32[25,32,128]{2,1,0:T(8,128)S(1)} %collective-permute-done.1.refs_0_), channel_id=1, source_target_pairs={{1,159},{14,144},{17,143},{30,128},{33,191},{46,176},{49,175},{62,... | collective-permute-start | bytes 1228808 | tf_op jit(solution)/shard_map/ppermute | solution.py:356
  54.5 24.6 %collective-permute-start.6 = (f32[64,128]{1,0:T(8,128)S(1)}, f32[64,128]{1,0:T(8,128)S(1)}, u32[]{:S(2)}, u32[]{:S(2)}) collective-permute-start(f32[64,128]{1,0:T(8,128)S(1)} %get-tuple-element.8), channel_id=1, source_target_pairs={{256,159},{257,2},{258,1},{259,4},{260,3},{261,6},{262,5},{263,8},... | collective-permute-start | bytes 98312 | tf_op jit(solution)/shard_map/ppermute | solution.py:356
  55.8 29.8 %collective-permute-start.5 = (f32[64,128]{1,0:T(8,128)S(1)}, f32[64,128]{1,0:T(8,128)S(1)}, u32[]{:S(2)}, u32[]{:S(2)}) collective-permute-start(f32[64,128]{1,0:T(8,128)S(1)} %get-tuple-element.8), channel_id=1, source_target_pairs={{256,1},{257,0},{258,3},{259,2},{260,5},{261,4},{262,7},{263,6},{2... | collective-permute-start | bytes 98312 | tf_op jit(solution)/shard_map/ppermute | solution.py:356
  57.1 28.5 %collective-permute-start.4 = (f32[64,128]{1,0:T(8,128)S(1)}, f32[64,128]{1,0:T(8,128)S(1)}, u32[]{:S(2)}, u32[]{:S(2)}) collective-permute-start(f32[64,128]{1,0:T(8,128)S(1)} %get-tuple-element.8), channel_id=1, source_target_pairs={{256,0},{257,1},{258,2},{259,3},{260,4},{261,5},{262,6},{263,7},{2... | collective-permute-start | bytes 98312 | tf_op jit(solution)/shard_map/ppermute | solution.py:356

commit v5 on v3

--- a/solution.py
+++ b/solution.py
@@ -65,34 +65,71 @@
     return jnp.asarray(product), jnp.asarray(along_y)
 
 
-def pair_tiles(windows):
+def triangle_tiles(windows):
+    last = 2 * windows
+    width = 8 * last
+    tiles = []
+    for step in range(1, windows + 1):
+        for kind in (0, 1):
+            cut = 8 * (last - step)
+            tiles.append(
+                [
+                    (block_of(windows, step, kind), 0, cut),
+                    (block_of(windows, last + 1 - step, kind), cut, width - cut),
+                ]
+            )
+    tiles.append([((windows - 1, 4), 0, width)])
+    tiles.append([((windows - 1, 5), 0, width)])
+    for window in range(windows - 2, windows // 2 - 1, -1):
+        for member in (4, 5):
+            cut = 16 * (window + 1)
+            tiles.append(
+                [((window, member), 0, cut), ((windows - 2 - window, member), cut, width - cut)]
+            )
+    middle = windows // 2 - 1
+    cut = 16 * (middle + 1)
+    tiles.append([((middle, 4), 0, cut), ((middle, 5), cut, width - cut)])
+    return tiles
+
+
+def block_of(windows, step, kind):
+    return (windows - 1 - (step - 1) // 2, 2 * kind + (step % 2))
+
+
+def diamond_tiles(windows):
     last = 2 * windows
     tiles = []
 
-    def block(step, kind):
-        return (windows - 1 - (step - 1) // 2, 2 * kind + (step % 2))
-
-    for step in range(1, windows + 1):
-        for kind in (0, 1):
-            tiles.append((block(step, kind), block(last + 1 - step, kind), 8 * (last - step)))
-    tiles.append(((windows - 1, 4), None, 16 * windows))
-    tiles.append(((windows - 1, 5), None, 16 * windows))
-    for window in range(windows - 2, windows // 2 - 1, -1):
-        for member in (4, 5):
-            tiles.append(
-                ((window, member), (windows - 2 - window, member), 16 * (window + 1))
-            )
-    middle = windows // 2 - 1
-    tiles.append(((middle, 4), (middle, 5), 16 * (middle + 1)))
+    def fill(blocks):
+        offset = 0
+        tile = []
+        for block, elements in blocks:
+            tile.append((block, offset, 8 * elements))
+            offset += 8 * elements
+        tiles.append(tile)
+
+    for kind in (0, 1):
+        for step in range(1, windows // 2):
+            group = (step, windows - step, last - step, windows + step)
+            fill([(block_of(windows, n, kind), min(n, last - n)) for n in group])
+        group = (windows // 2, last - windows // 2, windows)
+        fill([(block_of(windows, n, kind), min(n, last - n)) for n in group])
+
+    def forcing_elements(window):
+        step = 2 * (windows - 1 - window) + 1
+        return min(step - 1, last + 1 - step)
+
+    for member in (4, 5):
+        for group in ((6, 4, 3), (5, 2, 1, 0)):
+            fill([((window, member), forcing_elements(window)) for window in group])
     return tiles
 
 
-def places(windows):
+def places(tiles):
     found = {}
-    for index, (first, second, columns) in enumerate(pair_tiles(windows)):
-        found[first] = (index, 0)
-        if second is not None:
-            found[second] = (index, columns)
+    for index, tile in enumerate(tiles):
+        for block, offset, _ in tile:
+            found[block] = (index, offset)
     return found
 
 
@@ -144,35 +181,119 @@
         copy.wait()
 
 
-def pack_kernel(own_ref, even_ref, odd_ref):
+def columns_at(col, offset, columns, high):
+    width = col.shape[-1]
+    if high:
+        offset = width - offset - columns
+    return (col >= offset) & (col < offset + columns)
+
+
+def pack_tiles(own_ref, layout, high, out_ref):
+    width = own_ref.shape[3]
+    col = lax.broadcasted_iota(jnp.int32, own_ref.shape[2:], 1)
+    for index, tile in enumerate(layout):
+        value = None
+        for block, offset, columns in tile:
+            one = own_ref[block[0], block[1]]
+            if offset:
+                one = pltpu.roll(one, width - offset if high else offset, 1)
+            if value is None:
+                value = one
+            else:
+                value = jnp.where(columns_at(col, offset, columns, high), one, value)
+        out_ref[index] = value
+
+
+def pack_sides(layout, own_ref, even_ref, odd_ref):
+    odd_place = lax.axis_index("space") % 2 == 1
+
+    @pl.when(odd_place)
+    def _():
+        pack_tiles(own_ref, layout, False, even_ref)
+        pack_tiles(own_ref, layout, True, odd_ref)
+
+    @pl.when(jnp.logical_not(odd_place))
+    def _():
+        pack_tiles(own_ref, layout, True, even_ref)
+        pack_tiles(own_ref, layout, False, odd_ref)
+
+
+def pack_relay_kernel(own_ref, first_ref, second_ref):
+    windows = own_ref.shape[0]
+    cut = first_ref.shape[0]
+    odd_place = lax.axis_index("space") % 2 == 1
+    in_lower = lax.axis_index("tm") < windows
+
+    def pack(high):
+        layout = triangle_tiles(windows)
+        pack_tiles(own_ref, layout[:cut], high, first_ref)
+        pack_tiles(own_ref, layout[cut:], high, second_ref)
+
+    @pl.when(jnp.logical_and(in_lower, odd_place))
+    def _():
+        pack(True)
+
+    @pl.when(jnp.logical_and(in_lower, jnp.logical_not(odd_place)))
+    def _():
+        pack(False)
+
+
+def pack_lower_kernel(own_ref, b1_ref, b2_ref, b3_ref, b4_ref, even_ref, odd_ref):
+    windows = own_ref.shape[0]
+
+    @pl.when(lax.axis_index("tm") < windows)
+    def _():
+        pack_sides(triangle_tiles(windows), own_ref, even_ref, odd_ref)
+
+
+def pack_upper_kernel(own_ref, along_x_ref, along_y_ref, even_ref, odd_ref):
     windows, _, rows, width = own_ref.shape
-    col = lax.broadcasted_iota(jnp.int32, (rows, width), 1)
-    odd_place = lax.axis_index("space") % 2
-
-    def write(low_ref, high_ref):
-        for index, (first, second, columns) in enumerate(pair_tiles(windows)):
-            one = own_ref[first[0], first[1]]
-            if second is None:
-                low_ref[index] = one
-                high_ref[index] = one
-                continue
-            other = own_ref[second[0], second[1]]
-            low_ref[index] = jnp.where(col < columns, one, pltpu.roll(other, columns, 1))
-            high_ref[index] = jnp.where(
-                col >= width - columns, one, pltpu.roll(other, width - columns, 1)
-            )
-
-    @pl.when(odd_place == 0)
-    def _():
-        write(odd_ref, even_ref)
-
-    @pl.when(odd_place == 1)
-    def _():
-        write(even_ref, odd_ref)
+    odd_place = lax.axis_index("space") % 2 == 1
+
+    @pl.when(lax.axis_index("tm") >= windows)
+    def _():
+        layout = diamond_tiles(windows)
+        pack_sides(layout, own_ref, even_ref, odd_ref)
+        along_x = along_x_ref[...]
+        along_y = [along_y_ref[shift] for shift in range(8)]
+        col = lax.broadcasted_iota(jnp.int32, (2 * rows, width), 1)
+
+        def tile(window, index):
+            return own_ref[window, index].reshape(1, rows // 8, 8, width)
+
+        field = None
+        low = high = None
+        for step in range(1, windows + 1):
+            window = windows - 1 - (step - 1) // 2
+            if step % 2:
+                forcing = jnp.concatenate([tile(window, 4), tile(window, 5)], axis=1)
+                field = forcing if field is None else field + forcing
+            here = field.reshape(2 * rows, width)
+            if step == 1:
+                low = high = here
+            else:
+                shift = 8 * (step - 1)
+                wanted = columns_at(col, 2 * shift, 16, False)
+                low = jnp.where(wanted, pltpu.roll(here, shift, 1), low)
+                wanted = columns_at(col, 2 * shift, 16, True)
+                high = jnp.where(wanted, pltpu.roll(here, width - shift, 1), high)
+            if step < windows:
+                field = adjoint_step(
+                    field, tile(window, step % 2), tile(window, 2 + step % 2), along_x, along_y
+                )
+        first = len(layout)
+        to_even = jnp.where(odd_place, low, high)
+        to_odd = jnp.where(odd_place, high, low)
+        even_ref[first] = to_even[:rows]
+        even_ref[first + 1] = to_even[rows:]
+        odd_ref[first] = to_odd[:rows]
+        odd_ref[first + 1] = to_odd[rows:]
 
 
 def shift_tiles(tiles, distance):
     distance %= tiles.shape[0]
+    if distance == 0:
+        return tiles
     return jnp.concatenate([tiles[-distance:], tiles[:-distance]], axis=0)
 
 
@@ -224,32 +345,53 @@
     return q - (grad_x + grad_y.reshape(q.shape))
 
 
-def sweep(own_ref, even_ref, odd_ref, far_refs, along_x_ref, along_y_ref, start, out_ref, last_moves):
+def sweep(
+    own_ref, even_ref, odd_ref, far_refs, along_x_ref, along_y_ref, start, out_ref, upper
+):
     windows, _, rows, width = own_ref.shape
-    found = places(windows)
+    layout = diamond_tiles(windows) if upper else triangle_tiles(windows)
+    found = places(layout)
     odd_place = lax.axis_index("space") % 2 == 1
     along_x = along_x_ref[...]
     along_y = [along_y_ref[shift] for shift in range(8)]
     col = lax.broadcasted_iota(jnp.int32, (rows, width), 1)
     col_tile = lax.broadcasted_iota(jnp.int32, (1, 1, 8, width), 3)
 
-    def tiles(window, index, merged):
-        tile, shift = found[(window, index)]
+    def sides(tile, shift):
         by_even = even_ref[tile]
         by_odd = odd_ref[tile]
+        first = 0
         for far_ref in far_refs:
-            by_odd = by_odd + far_ref[tile]
+            if first <= tile < first + far_ref.shape[0]:
+                by_odd = by_odd + far_ref[tile - first]
+            first += far_ref.shape[0]
         west = jnp.where(odd_place, by_even, by_odd)
         east = jnp.where(odd_place, by_odd, by_even)
         if shift:
             west = pltpu.roll(west, shift, 1)
             east = pltpu.roll(east, width - shift, 1)
+        return east, west
+
+    def tiles(window, index, merged):
         own = own_ref[window, index]
+        if (window, index) in found:
+            east, west = sides(*found[(window, index)])
+        else:
+            east = west = jnp.zeros_like(own)
         if merged:
             parts = [own, jnp.where(col < width // 2, east, west)]
         else:
             parts = [own, east, west]
         return jnp.stack(parts).reshape(len(parts), rows // 8, 8, width)
+
+    def with_finished(field, step):
+        shift = 8 * (step - 1)
+        pairs = [sides(len(layout) + member, shift) for member in (0, 1)]
+        east = jnp.stack([pair[0] for pair in pairs]).reshape(1, 2 * rows // 8, 8, width)
+        west = jnp.stack([pair[1] for pair in pairs]).reshape(1, 2 * rows // 8, 8, width)
+        east = jnp.where(columns_at(col_tile, shift, 16, False), east, field[1:2])
+        west = jnp.where(columns_at(col_tile, shift, 16, True), west, field[2:3])
+        return jnp.concatenate([field[0:1], east, west], axis=0)
 
     moved = start
     for window in range(windows - 1, -1, -1):
@@ -263,9 +405,12 @@
         here = field[0].reshape(2 * rows, width)
         out_ref[window, 0] = here[:rows]
         out_ref[window, 1] = here[rows:]
-        if window == 0 and not last_moves:
+        if window == 0 and not upper:
             return None
         for substep in (1, 0):
+            step = 2 * (windows - window) - substep
+            if upper and step <= windows:
+                field = with_finished(field, step)
             field = adjoint_step(
                 field,
                 tiles(window, substep, merged),
@@ -278,13 +423,17 @@
 
 
 def upper_kernel(
-    own_ref, odd_ref, even_ref, to_odd_ref, along_x_ref, along_y_ref, out_ref, sent_ref, later_ref
+    own_ref,
+    odd_ref,
+    even_ref,
+    b1_ref,
+    b2_ref,
+    along_x_ref,
+    along_y_ref,
+    out_ref,
+    sent_ref,
 ):
     windows = own_ref.shape[0]
-
-    @pl.when(lax.axis_index("tm") < windows)
-    def _():
-        later_ref[...] = to_odd_ref[...]
 
     @pl.when(lax.axis_index("tm") >= windows)
     def _():
@@ -294,7 +443,18 @@
 
 
 def lower_kernel(
-    done_ref, own_ref, even_ref, odd_ref, far_ref, along_x_ref, along_y_ref, here_ref, pe_ref, po_ref, out_ref
+    done_ref,
+    own_ref,
+    even_ref,
+    odd_ref,
+    far_x_ref,
+    far_y_ref,
+    along_x_ref,
+    along_y_ref,
+    here_ref,
+    pe_ref,
+    po_ref,
+    out_ref,
 ):
     windows, _, rows, width = own_ref.shape
 
@@ -305,9 +465,10 @@
         by_odd = po_ref[...]
         west = jnp.where(odd_place, by_even, by_odd)
         east = jnp.where(odd_place, by_odd, by_even)
+        far_refs = (far_x_ref, far_y_ref)
         start = jnp.stack([here_ref[...], east, west]).reshape(3, 2 * rows // 8, 8, width)
         sweep(
-            own_ref, even_ref, odd_ref, (far_ref,), along_x_ref, along_y_ref, start, out_ref, False
+            own_ref, even_ref, odd_ref, far_refs, along_x_ref, along_y_ref, start, out_ref, False
         )
 
 
@@ -332,6 +493,7 @@
     group = levels
     groups = [list(range(i, i + group)) for i in range(0, tm, group)]
     layer = space // 2
+    anything = pl.BlockSpec(memory_space=pl.ANY)
     anywhere = pl.BlockSpec(memory_space=pltpu.HBM)
 
     def same(t, s):
@@ -346,6 +508,10 @@
     def odd_mate(t, s):
         mate = (s + 1) % space if s % 2 else (s - 1) % space
         return (t ^ (group // 2) if is_far(s) else t), mate
+
+    def along_y_mate(t, s):
+        row = max(2, layer // 4)
+        return t, (s + row if s % layer == 0 else s - row)
 
     def exchange(block, mate, chosen, dt=0):
         pairs = []
@@ -368,22 +534,57 @@
     )(wind_x, wind_y, forcing)
     own = lax.all_to_all(packed, "tm", 0, 0, axis_index_groups=groups, tiled=True)
 
-    tiles = jax.ShapeDtypeStruct((len(pair_tiles(group)), rows, width), jnp.float32)
-    to_even, to_odd = local_call(pack_kernel, (tiles, tiles), 1)(own)
-    odd = exchange(to_odd, odd_mate, lambda t, s: upper(t, s) or not is_far(s))
-    even = exchange(to_even, even_mate, lambda t, s: True)
+    whole = pl.BlockSpec(memory_space=pltpu.VMEM)
+    anything = pl.BlockSpec(memory_space=pl.ANY)
     along_x, along_y = derivative_tables(width)
+
+    def tiles(number):
+        return jax.ShapeDtypeStruct((number, rows, width), jnp.float32)
+
+    def lower(t, s):
+        return not upper(t, s)
+
+    diamond = tiles(len(diamond_tiles(group)) + 2)
+    triangle = tiles(len(triangle_tiles(group)))
+    to_even, to_odd = local_call(pack_upper_kernel, (diamond, diamond), 3)(own, along_x, along_y)
+    upper_odd = exchange(to_odd, odd_mate, upper)
+    upper_even = exchange(to_even, even_mate, upper)
+
+    cut = (len(triangle_tiles(group)) + 1) // 2
+    halves = tiles(cut), tiles(len(triangle_tiles(group)) - cut)
+    first_half, second_half = local_call(pack_relay_kernel, halves, 1)(own)
+
+    def relay(block, neighbour):
+        there = exchange(block, neighbour, lambda t, s: is_far(s) and lower(t, s))
+        pairs = []
+        for t in range(group):
+            for s in range(space):
+                if is_far(s):
+                    from_t, from_s = neighbour(t, s)
+                    to_t, to_s = odd_mate(t, s)
+                    pairs.append((from_t * space + from_s, to_t * space + to_s))
+        return there, lax.ppermute(there, ("tm", "space"), pairs)
+
+    there_x, far_x = relay(first_half, even_mate)
+    there_y, far_y = relay(second_half, along_y_mate)
+    to_even, to_odd = local_call(
+        pack_lower_kernel, (triangle, triangle), [whole] + [anything] * 4
+    )(own, upper_odd, upper_even, there_x, there_y)
+    lower_odd = exchange(to_odd, odd_mate, lambda t, s: lower(t, s) and not is_far(s))
+    lower_even = exchange(to_even, even_mate, lower)
+
     result_shape = jax.ShapeDtypeStruct((group, members, rows, width), jnp.float32)
     flat_field = jax.ShapeDtypeStruct((members * rows, width), jnp.float32)
-    done, sent, later = local_call(upper_kernel, (result_shape, flat_field, tiles), 6)(
-        own, odd, even, to_odd, along_x, along_y
-    )
-    far = exchange(later, odd_mate, lambda t, s: is_far(s) and not upper(t, s))
+    done, sent = local_call(
+        upper_kernel,
+        (result_shape, flat_field),
+        [whole] * 3 + [anything] * 2 + [whole] * 2,
+    )(own, upper_odd, upper_even, lower_odd, lower_even, along_x, along_y)
     from_here = exchange(sent, same, upper, -group)
     from_even = exchange(sent, even_mate, upper, -group)
     from_odd = exchange(sent, odd_mate, upper, -group)
-    result = local_call(lower_kernel, result_shape, 10, input_output_aliases={0: 0})(
-        done, own, even, odd, far, along_x, along_y, from_here, from_even, from_odd
+    result = local_call(lower_kernel, result_shape, 11, input_output_aliases={0: 0})(
+        done, own, lower_even, lower_odd, far_x, far_y, along_x, along_y, from_here, from_even, from_odd
     )
     result = lax.all_to_all(result, "tm", 0, 0, axis_index_groups=groups, tiled=True)
     return local_call(

time: 108 us -> 96 us (0.89)
  waiting for transfers between devices: 38.8 us -> 26.7 us
  starting transfers between devices: 20.1 us -> 15.4 us
  blocking collectives: 42 us -> 46.6 us
    ppermute x6 -> x9, waiting for transfers between devices: 38.8 us -> 17 us  [exchange(): return lax.ppermute(block, ('tm', 'space'), pairs)]
    ppermute x0 -> x2, waiting for transfers between devices: none -> 9.73 us  [relay(): return (there, lax.ppermute(there, ('tm', 'space'), pairs))]
    ppermute x6 -> x9, starting transfers between devices: 20.1 us -> 12.9 us  [exchange(): return lax.ppermute(block, ('tm', 'space'), pairs)]
    all_to_all x1, blocking collectives: 11.7 us -> 16.1 us  [on_device(): lax.all_to_all(result, 'tm', 0, 0, axis_index_groups=groups, tiled=True)]
    ppermute x0 -> x2, starting transfers between devices: none -> 2.58 us  [relay(): return (there, lax.ppermute(there, ('tm', 'space'), pairs))]
    pallas_call x3 -> x5, Pallas kernels: 3.68 us -> 3.85 us  [the longest x1 3.39 us: on_device(): local_call(lower_kernel, result_shape, 11, input_output_aliases={0: 0})]
  transfers between devices with their start and end apart: 6 -> 11, of which waited for: 2 -> 5; matrix products, arithmetic and copies ran while one was open for 0% -> 0% of each run, Pallas kernels for 0% -> 0%
where the time goes in v5:
time: 96 us; the launch traced here: 95.6 us
  blocking collectives  46.6 us (49%)
  waiting for transfers between devices  26.7 us (28%)
  starting transfers between devices  15.4 us (16%)
  Pallas kernels  6.73 us (7%)
    all_to_all x1, blocking collectives, on_device(): lax.all_to_all(packed, 'tm', 0, 0, axis_index_groups=groups, tiled=True)  30.4 us
    ppermute x9, waiting for transfers between devices, exchange(): return lax.ppermute(block, ('tm', 'space'), pairs)  17 us
    all_to_all x1, blocking collectives, on_device(): lax.all_to_all(result, 'tm', 0, 0, axis_index_groups=groups, tiled=True)  16.1 us
    ppermute x9, starting transfers between devices, exchange(): return lax.ppermute(block, ('tm', 'space'), pairs)  12.9 us
    ppermute x2, waiting for transfers between devices, relay(): return (there, lax.ppermute(there, ('tm', 'space'), pairs))  9.73 us
    pallas_call x1, Pallas kernels, on_device(): local_call(lower_kernel, result_shape, 11, input_output_aliases={0: 0})  3.39 us
    ppermute x2, starting transfers between devices, relay(): return (there, lax.ppermute(there, ('tm', 'space'), pairs))  2.58 us
    pallas_call x1, Pallas kernels, on_device(): local_call(gather_kernel, jax.ShapeDtypeStruct((levels, 6, rows, width),...  2.16 us
  transfers between devices with their start and end apart: 11, of which 5 were waited for; matrix products, arithmetic and copies ran while one was open for 0% of the time, Pallas kernels for 0%

profile of v5, /device:TPU:1, one launch (start us, length us, event | category | flops | bytes accessed | tf_op | source)
XLA Modules:
  0.0 95.6 jit_solution(16254639545499417183)
XLA Ops:
  0.0 2.2 %shard_map.55 = f32[8,6,32,128]{3,2,1,0:T(8,128)} custom-call(f32[1,2,8,32,128]{4,3,2,1,0:T(8,128)} %wind_x_ref.1, f32[1,2,8,32,128]{4,3,2,1,0:T(8,128)} %wind_y_ref.1, f32[2,1,8,32,128]{4,3,2,1,0:T(8,128)} %forcing_ref.1), custom_call_target="tpu_custom_call" | custom-call | tf_op jit(solution)/shard_map/pallas_call | solution.py:528
  2.2 0.0 copy-start
  2.2 30.4 %all_to_all.10.own_ref = f32[8,6,32,128]{3,2,1,0:T(8,128)S(1)} all-to-all(f32[8,6,32,128]{3,2,1,0:T(8,128)} %shard_map.55), channel_id=1, replica_groups={{0,32,64,96,128,160,192,224},{256,288,320,352,384,416,448,480},{1,33,65..., dimensions={0} | all-to-all | bytes 1572864 | tf_op jit(solution)/shard_map/all_to_all | solution.py:535
  32.6 0.7 collective-permute-start
  33.3 0.7 collective-permute-start.1
  34.0 0.2 shard_map.57
  34.1 1.3 %collective-permute-start.2 = (f32[13,32,128]{2,1,0:T(8,128)S(1)}, f32[13,32,128]{2,1,0:T(8,128)S(1)}, u32[]{:S(2)}, u32[]{:S(2)}) collective-permute-start(f32[13,32,128]{2,1,0:T(8,128)S(1)} %get-tuple-element.15), channel_id=1, source_target_pairs={{0,1},{15,14},{16,17},{31,30},{32,33},{47,46},{48,49},{63,62},{64,... | collective-permute-start | bytes 638984 | tf_op jit(solution)/shard_map/ppermute | solution.py:523
  35.5 1.3 %collective-permute-start.3 = (f32[12,32,128]{2,1,0:T(8,128)S(1)}, f32[12,32,128]{2,1,0:T(8,128)S(1)}, u32[]{:S(2)}, u32[]{:S(2)}) collective-permute-start(f32[12,32,128]{2,1,0:T(8,128)S(1)} %get-tuple-element.16), channel_id=1, source_target_pairs={{0,4},{15,11},{16,20},{31,27},{32,36},{47,43},{48,52},{63,59},{64,... | collective-permute-start | bytes 589832 | tf_op jit(solution)/shard_map/ppermute | solution.py:523
  36.8 3.4 %collective-permute-done.3.b4_ref = f32[12,32,128]{2,1,0:T(8,128)S(1)} collective-permute-done((f32[12,32,128]{2,1,0:T(8,128)S(1)}, f32[12,32,128]{2,1,0:T(8,128)S(1)}, u32[]{:S(2)}, u32[]{:S(2)}) %collective-permute-start.3) | collective-permute-done | bytes 196640 | tf_op jit(solution)/shard_map/ppermute | solution.py:523
  40.2 0.3 shard_map.58
  40.5 0.7 collective-permute-start.4
  41.2 4.4 %collective-permute-start.5 = (f32[25,32,128]{2,1,0:T(8,128)S(1)}, f32[25,32,128]{2,1,0:T(8,128)S(1)}, u32[]{:S(2)}, u32[]{:S(2)}) collective-permute-start(f32[25,32,128]{2,1,0:T(8,128)S(1)} %get-tuple-element.18), channel_id=1, source_target_pairs={{0,1},{1,0},{2,3},{3,2},{4,5},{5,4},{6,7},{7,6},{8,9},{9,8},{10,11... | collective-permute-start | bytes 1228808 | tf_op jit(solution)/shard_map/ppermute | solution.py:523
  45.6 1.3 %collective-permute-start.6 = (f32[13,32,128]{2,1,0:T(8,128)S(1)}, f32[13,32,128]{2,1,0:T(8,128)S(1)}, u32[]{:S(2)}, u32[]{:S(2)}) collective-permute-start(f32[13,32,128]{2,1,0:T(8,128)S(1)} %collective-permute-done.2.b3_ref), channel_id=1, source_target_pairs={{1,159},{14,144},{17,143},{30,128},{33,191},{46,176},{49,175},{62,... | collective-permute-start | bytes 638984 | tf_op jit(solution)/shard_map/ppermute | solution.py:566
  46.9 1.3 %collective-permute-start.7 = (f32[12,32,128]{2,1,0:T(8,128)S(1)}, f32[12,32,128]{2,1,0:T(8,128)S(1)}, u32[]{:S(2)}, u32[]{:S(2)}) collective-permute-start(f32[12,32,128]{2,1,0:T(8,128)S(1)} %collective-permute-done.3.b4_ref), channel_id=1, source_target_pairs={{4,159},{11,144},{20,143},{27,128},{36,191},{43,176},{52,175},{59,... | collective-permute-start | bytes 589832 | tf_op jit(solution)/shard_map/ppermute | solution.py:566
  48.2 5.5 %collective-permute-done.5.b2_ref.even_ref = f32[25,32,128]{2,1,0:T(8,128)S(1)} collective-permute-done((f32[25,32,128]{2,1,0:T(8,128)S(1)}, f32[25,32,128]{2,1,0:T(8,128)S(1)}, u32[]{:S(2)}, u32[]{:S(2)}) %collective-permute-start.5) | collective-permute-done | bytes 409632 | tf_op jit(solution)/shard_map/ppermute | solution.py:523
  53.7 1.3 %collective-permute-start.10 = (f32[64,128]{1,0:T(8,128)S(1)}, f32[64,128]{1,0:T(8,128)S(1)}, u32[]{:S(2)}, u32[]{:S(2)}) collective-permute-start(f32[64,128]{1,0:T(8,128)S(1)} %get-tuple-element.20), channel_id=1, source_target_pairs={{256,159},{257,2},{258,1},{259,4},{260,3},{261,6},{262,5},{263,8},... | collective-permute-start | bytes 98312 | tf_op jit(solution)/shard_map/ppermute | solution.py:523
  55.0 1.3 %collective-permute-start.9 = (f32[64,128]{1,0:T(8,128)S(1)}, f32[64,128]{1,0:T(8,128)S(1)}, u32[]{:S(2)}, u32[]{:S(2)}) collective-permute-start(f32[64,128]{1,0:T(8,128)S(1)} %get-tuple-element.20), channel_id=1, source_target_pairs={{256,1},{257,0},{258,3},{259,2},{260,5},{261,4},{262,7},{263,6},{2... | collective-permute-start | bytes 98312 | tf_op jit(solution)/shard_map/ppermute | solution.py:523
  56.3 1.3 %collective-permute-start.8 = (f32[64,128]{1,0:T(8,128)S(1)}, f32[64,128]{1,0:T(8,128)S(1)}, u32[]{:S(2)}, u32[]{:S(2)}) collective-permute-start(f32[64,128]{1,0:T(8,128)S(1)} %get-tuple-element.20), channel_id=1, source_target_pairs={{256,0},{257,1},{258,2},{259,3},{260,4},{261,5},{262,6},{263,7},{2... | collective-permute-start | bytes 98312 | tf_op jit(solution)/shard_map/ppermute | solution.py:523
  57.6 9.7 %collective-permute-done.7.far_y_ref = f32[12,32,128]{2,1,0:T(8,128)S(1)} collective-permute-done((f32[12,32,128]{2,1,0:T(8,128)S(1)}, f32[12,32,128]{2,1,0:T(8,128)S(1)}, u32[]{:S(2)}, u32[]{:S(2)}) %collective-permute-start.7) | collective-permute-done | bytes 196640 | tf_op jit(solution)/shard_map/ppermute | solution.py:566
  67.3 7.9 %collective-permute-done.10.po_ref = f32[64,128]{1,0:T(8,128)S(1)} collective-permute-done((f32[64,128]{1,0:T(8,128)S(1)}, f32[64,128]{1,0:T(8,128)S(1)}, u32[]{:S(2)}, u32[]{:S(2)}) %collective-permute-start.10) | collective-permute-done | bytes 32800 | tf_op jit(solution)/shard_map/ppermute | solution.py:523
  75.2 0.2 collective-permute-done.9.pe_ref
  75.3 3.4 %shard_map.60 = f32[8,2,32,128]{3,2,1,0:T(8,128)S(1)} custom-call(f32[8,2,32,128]{3,2,1,0:T(8,128)S(1)} %get-tuple-element.19.done_ref, f32[8,6,32,128]{3,2,1,0:T(8,128)S(1)} %all_to_all.10.own_ref, f32[25,32,128]{2,1,0:T(8,128)S(1)} %collective-permute-done.5.b2_ref.even_ref, ...), custom_call_target="tpu_custom_call", output_to_operand_aliasing={{}: (0, {})} | custom-call | tf_op jit(solution)/shard_map/pallas_call | solution.py:586
  78.7 16.1 %all_to_all.11.in_ref = f32[8,2,32,128]{3,2,1,0:T(8,128)S(1)} all-to-all(f32[8,2,32,128]{3,2,1,0:T(8,128)S(1)} %shard_map.60), channel_id=1, replica_groups={{0,32,64,96,128,160,192,224},{256,288,320,352,384,416,448,480},{1,33,65..., dimensions={0} | all-to-all | bytes 524288 | tf_op jit(solution)/shard_map/all_to_all | solution.py:589
  94.9 0.7 shard_map.61
  (11 shorter events, 0.0 us)
Async XLA Ops:
  2.2 30.4 %copy-start = (bf16[256,256]{1,0:T(8,128)(2,1)S(1)}, bf16[256,256]{1,0:T(8,128)(2,1)}, u32[]{:S(2)}) copy-start(bf16[256,256]{1,0:T(8,128)(2,1)} %constant.4.clone.along_x_ref) | copy-start | bytes 393220
  2.2 30.4 %copy-start.1 = (f32[8,8,128]{2,1,0:T(8,128)S(1)}, f32[8,8,128]{2,1,0:T(8,128)}, u32[]{:S(2)}) copy-start(f32[8,8,128]{2,1,0:T(8,128)} %constant.5.clone.along_y_ref) | copy-start | bytes 98308
  32.6 7.6 %collective-permute-start = (f32[14,32,128]{2,1,0:T(8,128)S(1)}, f32[14,32,128]{2,1,0:T(8,128)S(1)}, u32[]{:S(2)}, u32[]{:S(2)}) collective-permute-start(f32[14,32,128]{2,1,0:T(8,128)S(1)} %get-tuple-element.13), channel_id=1, source_target_pairs={{256,415},{257,258},{258,257},{259,260},{260,259},{261,262},{262,2... | collective-permute-start | bytes 688136 | tf_op jit(solution)/shard_map/ppermute | solution.py:523
  33.3 6.9 %collective-permute-start.1 = (f32[14,32,128]{2,1,0:T(8,128)S(1)}, f32[14,32,128]{2,1,0:T(8,128)S(1)}, u32[]{:S(2)}, u32[]{:S(2)}) collective-permute-start(f32[14,32,128]{2,1,0:T(8,128)S(1)} %get-tuple-element.14), channel_id=1, source_target_pairs={{256,257},{257,256},{258,259},{259,258},{260,261},{261,260},{262,2... | collective-permute-start | bytes 688136 | tf_op jit(solution)/shard_map/ppermute | solution.py:523
  34.1 6.1 %collective-permute-start.2 = (f32[13,32,128]{2,1,0:T(8,128)S(1)}, f32[13,32,128]{2,1,0:T(8,128)S(1)}, u32[]{:S(2)}, u32[]{:S(2)}) collective-permute-start(f32[13,32,128]{2,1,0:T(8,128)S(1)} %get-tuple-element.15), channel_id=1, source_target_pairs={{0,1},{15,14},{16,17},{31,30},{32,33},{47,46},{48,49},{63,62},{64,... | collective-permute-start | bytes 638984 | tf_op jit(solution)/shard_map/ppermute | solution.py:523
  35.5 4.8 %collective-permute-start.3 = (f32[12,32,128]{2,1,0:T(8,128)S(1)}, f32[12,32,128]{2,1,0:T(8,128)S(1)}, u32[]{:S(2)}, u32[]{:S(2)}) collective-permute-start(f32[12,32,128]{2,1,0:T(8,128)S(1)} %get-tuple-element.16), channel_id=1, source_target_pairs={{0,4},{15,11},{16,20},{31,27},{32,36},{47,43},{48,52},{63,59},{64,... | collective-permute-start | bytes 589832 | tf_op jit(solution)/shard_map/ppermute | solution.py:523
  40.5 7.7 %collective-permute-start.4 = (f32[25,32,128]{2,1,0:T(8,128)S(1)}, f32[25,32,128]{2,1,0:T(8,128)S(1)}, u32[]{:S(2)}, u32[]{:S(2)}) collective-permute-start(f32[25,32,128]{2,1,0:T(8,128)S(1)} %get-tuple-element.17), channel_id=1, source_target_pairs={{1,2},{2,1},{3,4},{4,3},{5,6},{6,5},{7,8},{8,7},{9,10},{10,9},{11,... | collective-permute-start | bytes 1228808 | tf_op jit(solution)/shard_map/ppermute | solution.py:523
  41.2 12.5 %collective-permute-start.5 = (f32[25,32,128]{2,1,0:T(8,128)S(1)}, f32[25,32,128]{2,1,0:T(8,128)S(1)}, u32[]{:S(2)}, u32[]{:S(2)}) collective-permute-start(f32[25,32,128]{2,1,0:T(8,128)S(1)} %get-tuple-element.18), channel_id=1, source_target_pairs={{0,1},{1,0},{2,3},{3,2},{4,5},{5,4},{6,7},{7,6},{8,9},{9,8},{10,11... | collective-permute-start | bytes 1228808 | tf_op jit(solution)/shard_map/ppermute | solution.py:523
  45.6 21.7 %collective-permute-start.6 = (f32[13,32,128]{2,1,0:T(8,128)S(1)}, f32[13,32,128]{2,1,0:T(8,128)S(1)}, u32[]{:S(2)}, u32[]{:S(2)}) collective-permute-start(f32[13,32,128]{2,1,0:T(8,128)S(1)} %collective-permute-done.2.b3_ref), channel_id=1, source_target_pairs={{1,159},{14,144},{17,143},{30,128},{33,191},{46,176},{49,175},{62,... | collective-permute-start | bytes 638984 | tf_op jit(solution)/shard_map/ppermute | solution.py:566
  46.9 20.4 %collective-permute-start.7 = (f32[12,32,128]{2,1,0:T(8,128)S(1)}, f32[12,32,128]{2,1,0:T(8,128)S(1)}, u32[]{:S(2)}, u32[]{:S(2)}) collective-permute-start(f32[12,32,128]{2,1,0:T(8,128)S(1)} %collective-permute-done.3.b4_ref), channel_id=1, source_target_pairs={{4,159},{11,144},{20,143},{27,128},{36,191},{43,176},{52,175},{59,... | collective-permute-start | bytes 589832 | tf_op jit(solution)/shard_map/ppermute | solution.py:566
  53.7 21.5 %collective-permute-start.10 = (f32[64,128]{1,0:T(8,128)S(1)}, f32[64,128]{1,0:T(8,128)S(1)}, u32[]{:S(2)}, u32[]{:S(2)}) collective-permute-start(f32[64,128]{1,0:T(8,128)S(1)} %get-tuple-element.20), channel_id=1, source_target_pairs={{256,159},{257,2},{258,1},{259,4},{260,3},{261,6},{262,5},{263,8},... | collective-permute-start | bytes 98312 | tf_op jit(solution)/shard_map/ppermute | solution.py:523
  55.0 20.4 %collective-permute-start.9 = (f32[64,128]{1,0:T(8,128)S(1)}, f32[64,128]{1,0:T(8,128)S(1)}, u32[]{:S(2)}, u32[]{:S(2)}) collective-permute-start(f32[64,128]{1,0:T(8,128)S(1)} %get-tuple-element.20), channel_id=1, source_target_pairs={{256,1},{257,0},{258,3},{259,2},{260,5},{261,4},{262,7},{263,6},{2... | collective-permute-start | bytes 98312 | tf_op jit(solution)/shard_map/ppermute | solution.py:523
  56.3 19.1 %collective-permute-start.8 = (f32[64,128]{1,0:T(8,128)S(1)}, f32[64,128]{1,0:T(8,128)S(1)}, u32[]{:S(2)}, u32[]{:S(2)}) collective-permute-start(f32[64,128]{1,0:T(8,128)S(1)} %get-tuple-element.20), channel_id=1, source_target_pairs={{256,0},{257,1},{258,2},{259,3},{260,4},{261,5},{262,6},{263,7},{2... | collective-permute-start | bytes 98312 | tf_op jit(solution)/shard_map/ppermute | solution.py:523

commit v6 on v5

--- a/solution.py
+++ b/solution.py
@@ -137,48 +137,8 @@
     return lax.axis_index("space") // (lax.axis_size("space") // 2)
 
 
-def gather_kernel(wind_x_ref, wind_y_ref, forcing_ref, out_ref, sems):
-    levels = out_ref.shape[0]
-    half = levels // 2
-    layer = layer_here()
-    copies = []
-    for part in (0, 1):
-        here = pl.ds(half * part, half)
-        there = pl.ds(half * jnp.bitwise_xor(layer, part), half)
-        for index in (0, 1):
-            copies.append((wind_x_ref.at[0, index, here], out_ref.at[there, index]))
-            copies.append((wind_y_ref.at[0, index, here], out_ref.at[there, 2 + index]))
-            copies.append((forcing_ref.at[index, 0, here], out_ref.at[there, 4 + index]))
-    copies = [
-        pltpu.make_async_copy(source, target, sems.at[index])
-        for index, (source, target) in enumerate(copies)
-    ]
-    for copy in copies:
-        copy.start()
-    for copy in copies:
-        copy.wait()
-
-
-def scatter_kernel(in_ref, out_ref, sems):
-    levels = in_ref.shape[0]
-    half = levels // 2
-    layer = layer_here()
-    copies = []
-    for part in (0, 1):
-        here = pl.ds(half * part, half)
-        there = pl.ds(half * jnp.bitwise_xor(layer, part), half)
-        for member in (0, 1):
-            copies.append(
-                pltpu.make_async_copy(
-                    in_ref.at[there, member],
-                    out_ref.at[member, 0, here],
-                    sems.at[2 * part + member],
-                )
-            )
-    for copy in copies:
-        copy.start()
-    for copy in copies:
-        copy.wait()
+def slot_of(windows, window):
+    return jnp.bitwise_xor(window, layer_here() * (windows // 2))
 
 
 def columns_at(col, offset, columns, high):
@@ -194,7 +154,7 @@
     for index, tile in enumerate(layout):
         value = None
         for block, offset, columns in tile:
-            one = own_ref[block[0], block[1]]
+            one = own_ref[slot_of(own_ref.shape[0], block[0]), block[1]]
             if offset:
                 one = pltpu.roll(one, width - offset if high else offset, 1)
             if value is None:
@@ -259,7 +219,7 @@
         col = lax.broadcasted_iota(jnp.int32, (2 * rows, width), 1)
 
         def tile(window, index):
-            return own_ref[window, index].reshape(1, rows // 8, 8, width)
+            return own_ref[slot_of(windows, window), index].reshape(1, rows // 8, 8, width)
 
         field = None
         low = high = None
@@ -373,7 +333,7 @@
         return east, west
 
     def tiles(window, index, merged):
-        own = own_ref[window, index]
+        own = own_ref[slot_of(windows, window), index]
         if (window, index) in found:
             east, west = sides(*found[(window, index)])
         else:
@@ -403,8 +363,9 @@
                 moved = jnp.concatenate([moved[0:1], side], axis=0)
             field = field + moved
         here = field[0].reshape(2 * rows, width)
-        out_ref[window, 0] = here[:rows]
-        out_ref[window, 1] = here[rows:]
+        slot = slot_of(windows, window)
+        out_ref[slot, 0] = here[:rows]
+        out_ref[slot, 1] = here[rows:]
         if window == 0 and not upper:
             return None
         for substep in (1, 0):
@@ -472,7 +433,7 @@
         )
 
 
-def local_call(kernel, out_shape, in_specs, out_specs=None, vmem=32, **options):
+def local_call(kernel, out_shape, in_specs, out_specs=None, **options):
     whole = pl.BlockSpec(memory_space=pltpu.VMEM)
     if isinstance(in_specs, int):
         in_specs = [whole] * in_specs
@@ -481,7 +442,7 @@
         out_shape=out_shape,
         in_specs=in_specs,
         out_specs=out_specs or jax.tree.map(lambda _: whole, out_shape),
-        compiler_params=pltpu.CompilerParams(vmem_limit_bytes=vmem * 1024 * 1024),
+        compiler_params=pltpu.CompilerParams(vmem_limit_bytes=32 * 1024 * 1024),
         **options,
     )
 
@@ -491,10 +452,8 @@
     tm = lax.axis_size("tm")
     space = lax.axis_size("space")
     group = levels
-    groups = [list(range(i, i + group)) for i in range(0, tm, group)]
     layer = space // 2
     anything = pl.BlockSpec(memory_space=pl.ANY)
-    anywhere = pl.BlockSpec(memory_space=pltpu.HBM)
 
     def same(t, s):
         return t, s
@@ -525,14 +484,19 @@
     def upper(t, s):
         return t >= group
 
-    packed = local_call(
-        gather_kernel,
-        jax.ShapeDtypeStruct((levels, 6, rows, width), jnp.float32),
-        [anywhere] * 3,
-        vmem=61,
-        scratch_shapes=[pltpu.SemaphoreType.DMA((12,))],
-    )(wind_x, wind_y, forcing)
-    own = lax.all_to_all(packed, "tm", 0, 0, axis_index_groups=groups, tiled=True)
+    groups = []
+    for s in range(space):
+        flip = (s // layer) * (group // 2)
+        for first in range(0, tm, group):
+            groups.append([(first + (place ^ flip)) * space + s for place in range(group)])
+
+    def within_groups(block):
+        return lax.all_to_all(
+            block, ("tm", "space"), 0, 0, axis_index_groups=groups, tiled=True
+        )
+
+    packed = jnp.concatenate([wind_x[0], wind_y[0], forcing[:, 0]], axis=0)
+    own = within_groups(jnp.swapaxes(packed, 0, 1))
 
     whole = pl.BlockSpec(memory_space=pltpu.VMEM)
     anything = pl.BlockSpec(memory_space=pl.ANY)
@@ -586,14 +550,8 @@
     result = local_call(lower_kernel, result_shape, 11, input_output_aliases={0: 0})(
         done, own, lower_even, lower_odd, far_x, far_y, along_x, along_y, from_here, from_even, from_odd
     )
-    result = lax.all_to_all(result, "tm", 0, 0, axis_index_groups=groups, tiled=True)
-    return local_call(
-        scatter_kernel,
-        jax.ShapeDtypeStruct(forcing.shape, jnp.float32),
-        [pl.BlockSpec(memory_space=pltpu.VMEM)],
-        anywhere,
-        scratch_shapes=[pltpu.SemaphoreType.DMA((4,))],
-    )(result)
+    result = within_groups(result)
+    return jnp.swapaxes(result, 0, 1)[:, None]
 
 
 def solution(mesh):

time: 96 us -> 93.5 us (0.974)
  blocking collectives: 46.6 us -> 43.2 us
  Pallas kernels: 6.73 us -> 3.88 us
  local copies, waits for them, and re-layouts: 0.01 us -> 1.86 us
  waiting for transfers between devices: 26.7 us -> 28.5 us
    all_to_all x2, blocking collectives: 46.6 us -> 43.2 us  [within_groups(): lax.all_to_all(block, ('tm', 'space'), 0, 0, axis_index_groups=groups, ti...]
    pallas_call x2 -> x0, Pallas kernels: 2.88 us -> none  [the longest x1 2.16 us: on_device(): local_call(gather_kernel, jax.ShapeDtypeStruct((levels, 6, rows, width),...]
    ppermute x9, waiting for transfers between devices: 17 us -> 18.8 us  [exchange(): return lax.ppermute(block, ('tm', 'space'), pairs)]
    unnamed x4 -> x9, local copies, waits for them, and re-layouts: 0.01 us -> 1.11 us
where the time goes in v6:
time: 93.5 us; the launch traced here: 93.1 us
  blocking collectives  43.2 us (46%)
  waiting for transfers between devices  28.5 us (30%)
  starting transfers between devices  15.4 us (16%)
  Pallas kernels  3.88 us (4%)
  local copies, waits for them, and re-layouts  1.86 us (2%)
    all_to_all x2, blocking collectives, within_groups(): lax.all_to_all(block, ('tm', 'space'), 0, 0, axis_index_groups=groups, ti...  43.2 us
    ppermute x9, waiting for transfers between devices, exchange(): return lax.ppermute(block, ('tm', 'space'), pairs)  18.8 us
    ppermute x9, starting transfers between devices, exchange(): return lax.ppermute(block, ('tm', 'space'), pairs)  12.8 us
    ppermute x2, waiting for transfers between devices, relay(): return (there, lax.ppermute(there, ('tm', 'space'), pairs))  9.74 us
    pallas_call x1, Pallas kernels, on_device(): local_call(lower_kernel, result_shape, 11, input_output_aliases={0: 0})  3.4 us
    ppermute x2, starting transfers between devices, relay(): return (there, lax.ppermute(there, ('tm', 'space'), pairs))  2.58 us
  transfers between devices with their start and end apart: 11, of which 5 were waited for; matrix products, arithmetic and copies ran while one was open for 0% of the time, Pallas kernels for 0%

profile of v6, /device:TPU:1, one launch (start us, length us, event | category | flops | bytes accessed | tf_op | source)
XLA Modules:
  0.0 93.1 jit_solution(8970544814872176723)
XLA Ops:
  0.0 1.0 %copy.14 = f32[2,1,8,32,128]{4,3,0,2,1:T(8,128)S(1)} copy(f32[2,1,8,32,128]{4,3,2,1,0:T(8,128)} %param.5) | data formatting | bytes 524288 | tf_op args[0]
  1.2 0.1 maximum_bitcast_fusion
  1.3 29.4 %all_to_all.10.own_ref = f32[8,6,32,128]{3,2,1,0:T(8,128)S(1)} all-to-all(f32[8,6,32,128]{3,2,1,0:T(8,128)S(1)} %maximum_bitcast_fusion), channel_id=1, replica_groups={{0,32,64,96,128,160,192,224},{256,288,320,352,384,416,448,480},{1,33,65..., dimensions={0} | all-to-all | bytes 1572864 | tf_op jit(solution)/shard_map/all_to_all | solution.py:494
  30.6 0.7 collective-permute-start
  31.3 0.7 collective-permute-start.1
  32.0 0.2 shard_map.56
  32.2 1.3 %collective-permute-start.2 = (f32[13,32,128]{2,1,0:T(8,128)S(1)}, f32[13,32,128]{2,1,0:T(8,128)S(1)}, u32[]{:S(2)}, u32[]{:S(2)}) collective-permute-start(f32[13,32,128]{2,1,0:T(8,128)S(1)} %get-tuple-element.15), channel_id=1, source_target_pairs={{0,1},{15,14},{16,17},{31,30},{32,33},{47,46},{48,49},{63,62},{64,... | collective-permute-start | bytes 638984 | tf_op jit(solution)/shard_map/ppermute | solution.py:482
  33.5 1.3 %collective-permute-start.3 = (f32[12,32,128]{2,1,0:T(8,128)S(1)}, f32[12,32,128]{2,1,0:T(8,128)S(1)}, u32[]{:S(2)}, u32[]{:S(2)}) collective-permute-start(f32[12,32,128]{2,1,0:T(8,128)S(1)} %get-tuple-element.16), channel_id=1, source_target_pairs={{0,4},{15,11},{16,20},{31,27},{32,36},{47,43},{48,52},{63,59},{64,... | collective-permute-start | bytes 589832 | tf_op jit(solution)/shard_map/ppermute | solution.py:482
  34.8 3.4 %collective-permute-done.3.b4_ref = f32[12,32,128]{2,1,0:T(8,128)S(1)} collective-permute-done((f32[12,32,128]{2,1,0:T(8,128)S(1)}, f32[12,32,128]{2,1,0:T(8,128)S(1)}, u32[]{:S(2)}, u32[]{:S(2)}) %collective-permute-start.3) | collective-permute-done | bytes 196640 | tf_op jit(solution)/shard_map/ppermute | solution.py:482
  38.2 0.3 shard_map.57
  38.5 0.7 collective-permute-start.4
  39.2 4.4 %collective-permute-start.5 = (f32[25,32,128]{2,1,0:T(8,128)S(1)}, f32[25,32,128]{2,1,0:T(8,128)S(1)}, u32[]{:S(2)}, u32[]{:S(2)}) collective-permute-start(f32[25,32,128]{2,1,0:T(8,128)S(1)} %get-tuple-element.18), channel_id=1, source_target_pairs={{0,1},{1,0},{2,3},{3,2},{4,5},{5,4},{6,7},{7,6},{8,9},{9,8},{10,11... | collective-permute-start | bytes 1228808 | tf_op jit(solution)/shard_map/ppermute | solution.py:482
  43.6 1.3 %collective-permute-start.6 = (f32[13,32,128]{2,1,0:T(8,128)S(1)}, f32[13,32,128]{2,1,0:T(8,128)S(1)}, u32[]{:S(2)}, u32[]{:S(2)}) collective-permute-start(f32[13,32,128]{2,1,0:T(8,128)S(1)} %collective-permute-done.2.b3_ref), channel_id=1, source_target_pairs={{1,159},{14,144},{17,143},{30,128},{33,191},{46,176},{49,175},{62,... | collective-permute-start | bytes 638984 | tf_op jit(solution)/shard_map/ppermute | solution.py:530
  44.9 1.3 %collective-permute-start.7 = (f32[12,32,128]{2,1,0:T(8,128)S(1)}, f32[12,32,128]{2,1,0:T(8,128)S(1)}, u32[]{:S(2)}, u32[]{:S(2)}) collective-permute-start(f32[12,32,128]{2,1,0:T(8,128)S(1)} %collective-permute-done.3.b4_ref), channel_id=1, source_target_pairs={{4,159},{11,144},{20,143},{27,128},{36,191},{43,176},{52,175},{59,... | collective-permute-start | bytes 589832 | tf_op jit(solution)/shard_map/ppermute | solution.py:530
  46.2 5.5 %collective-permute-done.5.b2_ref.even_ref = f32[25,32,128]{2,1,0:T(8,128)S(1)} collective-permute-done((f32[25,32,128]{2,1,0:T(8,128)S(1)}, f32[25,32,128]{2,1,0:T(8,128)S(1)}, u32[]{:S(2)}, u32[]{:S(2)}) %collective-permute-start.5) | collective-permute-done | bytes 409632 | tf_op jit(solution)/shard_map/ppermute | solution.py:482
  51.7 1.3 %collective-permute-start.10 = (f32[64,128]{1,0:T(8,128)S(1)}, f32[64,128]{1,0:T(8,128)S(1)}, u32[]{:S(2)}, u32[]{:S(2)}) collective-permute-start(f32[64,128]{1,0:T(8,128)S(1)} %get-tuple-element.20), channel_id=1, source_target_pairs={{256,159},{257,2},{258,1},{259,4},{260,3},{261,6},{262,5},{263,8},... | collective-permute-start | bytes 98312 | tf_op jit(solution)/shard_map/ppermute | solution.py:482
  53.0 1.3 %collective-permute-start.9 = (f32[64,128]{1,0:T(8,128)S(1)}, f32[64,128]{1,0:T(8,128)S(1)}, u32[]{:S(2)}, u32[]{:S(2)}) collective-permute-start(f32[64,128]{1,0:T(8,128)S(1)} %get-tuple-element.20), channel_id=1, source_target_pairs={{256,1},{257,0},{258,3},{259,2},{260,5},{261,4},{262,7},{263,6},{2... | collective-permute-start | bytes 98312 | tf_op jit(solution)/shard_map/ppermute | solution.py:482
  54.3 1.3 %collective-permute-start.8 = (f32[64,128]{1,0:T(8,128)S(1)}, f32[64,128]{1,0:T(8,128)S(1)}, u32[]{:S(2)}, u32[]{:S(2)}) collective-permute-start(f32[64,128]{1,0:T(8,128)S(1)} %get-tuple-element.20), channel_id=1, source_target_pairs={{256,0},{257,1},{258,2},{259,3},{260,4},{261,5},{262,6},{263,7},{2... | collective-permute-start | bytes 98312 | tf_op jit(solution)/shard_map/ppermute | solution.py:482
  55.6 9.7 %collective-permute-done.7.far_y_ref = f32[12,32,128]{2,1,0:T(8,128)S(1)} collective-permute-done((f32[12,32,128]{2,1,0:T(8,128)S(1)}, f32[12,32,128]{2,1,0:T(8,128)S(1)}, u32[]{:S(2)}, u32[]{:S(2)}) %collective-permute-start.7) | collective-permute-done | bytes 196640 | tf_op jit(solution)/shard_map/ppermute | solution.py:530
  65.3 7.5 %collective-permute-done.10.po_ref = f32[64,128]{1,0:T(8,128)S(1)} collective-permute-done((f32[64,128]{1,0:T(8,128)S(1)}, f32[64,128]{1,0:T(8,128)S(1)}, u32[]{:S(2)}, u32[]{:S(2)}) %collective-permute-start.10) | collective-permute-done | bytes 32800 | tf_op jit(solution)/shard_map/ppermute | solution.py:482
  72.8 2.3 %collective-permute-done.9.pe_ref = f32[64,128]{1,0:T(8,128)S(1)} collective-permute-done((f32[64,128]{1,0:T(8,128)S(1)}, f32[64,128]{1,0:T(8,128)S(1)}, u32[]{:S(2)}, u32[]{:S(2)}) %collective-permute-start.9) | collective-permute-done | bytes 32800 | tf_op jit(solution)/shard_map/ppermute | solution.py:482
  75.1 3.4 %shard_map.59 = f32[8,2,32,128]{3,2,1,0:T(8,128)S(1)} custom-call(f32[8,2,32,128]{3,2,1,0:T(8,128)S(1)} %get-tuple-element.19.done_ref, f32[8,6,32,128]{3,2,1,0:T(8,128)S(1)} %all_to_all.10.own_ref, f32[25,32,128]{2,1,0:T(8,128)S(1)} %collective-permute-done.5.b2_ref.even_ref, ...), custom_call_target="tpu_custom_call", output_to_operand_aliasing={{}: (0, {})} | custom-call | tf_op jit(solution)/shard_map/pallas_call | solution.py:550
  78.5 13.8 %all_to_all.11 = f32[8,2,32,128]{3,2,1,0:T(8,128)S(1)} all-to-all(f32[8,2,32,128]{3,2,1,0:T(8,128)S(1)} %shard_map.59), channel_id=1, replica_groups={{0,32,64,96,128,160,192,224},{256,288,320,352,384,416,448,480},{1,33,65..., dimensions={0} | all-to-all | bytes 524288 | tf_op jit(solution)/shard_map/all_to_all | solution.py:494
  92.4 0.7 copy.10
  (17 shorter events, 0.1 us)
Async XLA Ops:
  0.0 1.0 %copy-start.2 = (f32[1,2,8,32,128]{4,3,2,1,0:T(8,128)S(1)}, f32[1,2,8,32,128]{4,3,2,1,0:T(8,128)}, u32[]{:S(2)}) copy-start(f32[1,2,8,32,128]{4,3,2,1,0:T(8,128)} %param.7) | copy-start | bytes 786436
  0.0 1.1 %copy-start.3 = (f32[1,2,8,32,128]{4,3,2,1,0:T(8,128)S(1)}, f32[1,2,8,32,128]{4,3,2,1,0:T(8,128)}, u32[]{:S(2)}) copy-start(f32[1,2,8,32,128]{4,3,2,1,0:T(8,128)} %param.6) | copy-start | bytes 786436
  1.2 29.4 %copy-start = (bf16[256,256]{1,0:T(8,128)(2,1)S(1)}, bf16[256,256]{1,0:T(8,128)(2,1)}, u32[]{:S(2)}) copy-start(bf16[256,256]{1,0:T(8,128)(2,1)} %constant.4.clone.along_x_ref) | copy-start | bytes 393220
  1.2 29.4 %copy-start.1 = (f32[8,8,128]{2,1,0:T(8,128)S(1)}, f32[8,8,128]{2,1,0:T(8,128)}, u32[]{:S(2)}) copy-start(f32[8,8,128]{2,1,0:T(8,128)} %constant.5.clone.along_y_ref) | copy-start | bytes 98308
  30.6 7.6 %collective-permute-start = (f32[14,32,128]{2,1,0:T(8,128)S(1)}, f32[14,32,128]{2,1,0:T(8,128)S(1)}, u32[]{:S(2)}, u32[]{:S(2)}) collective-permute-start(f32[14,32,128]{2,1,0:T(8,128)S(1)} %get-tuple-element.13), channel_id=1, source_target_pairs={{256,415},{257,258},{258,257},{259,260},{260,259},{261,262},{262,2... | collective-permute-start | bytes 688136 | tf_op jit(solution)/shard_map/ppermute | solution.py:482
  31.3 6.9 %collective-permute-start.1 = (f32[14,32,128]{2,1,0:T(8,128)S(1)}, f32[14,32,128]{2,1,0:T(8,128)S(1)}, u32[]{:S(2)}, u32[]{:S(2)}) collective-permute-start(f32[14,32,128]{2,1,0:T(8,128)S(1)} %get-tuple-element.14), channel_id=1, source_target_pairs={{256,257},{257,256},{258,259},{259,258},{260,261},{261,260},{262,2... | collective-permute-start | bytes 688136 | tf_op jit(solution)/shard_map/ppermute | solution.py:482
  32.2 6.0 %collective-permute-start.2 = (f32[13,32,128]{2,1,0:T(8,128)S(1)}, f32[13,32,128]{2,1,0:T(8,128)S(1)}, u32[]{:S(2)}, u32[]{:S(2)}) collective-permute-start(f32[13,32,128]{2,1,0:T(8,128)S(1)} %get-tuple-element.15), channel_id=1, source_target_pairs={{0,1},{15,14},{16,17},{31,30},{32,33},{47,46},{48,49},{63,62},{64,... | collective-permute-start | bytes 638984 | tf_op jit(solution)/shard_map/ppermute | solution.py:482
  33.5 4.7 %collective-permute-start.3 = (f32[12,32,128]{2,1,0:T(8,128)S(1)}, f32[12,32,128]{2,1,0:T(8,128)S(1)}, u32[]{:S(2)}, u32[]{:S(2)}) collective-permute-start(f32[12,32,128]{2,1,0:T(8,128)S(1)} %get-tuple-element.16), channel_id=1, source_target_pairs={{0,4},{15,11},{16,20},{31,27},{32,36},{47,43},{48,52},{63,59},{64,... | collective-permute-start | bytes 589832 | tf_op jit(solution)/shard_map/ppermute | solution.py:482
  38.5 7.7 %collective-permute-start.4 = (f32[25,32,128]{2,1,0:T(8,128)S(1)}, f32[25,32,128]{2,1,0:T(8,128)S(1)}, u32[]{:S(2)}, u32[]{:S(2)}) collective-permute-start(f32[25,32,128]{2,1,0:T(8,128)S(1)} %get-tuple-element.17), channel_id=1, source_target_pairs={{1,2},{2,1},{3,4},{4,3},{5,6},{6,5},{7,8},{8,7},{9,10},{10,9},{11,... | collective-permute-start | bytes 1228808 | tf_op jit(solution)/shard_map/ppermute | solution.py:482
  39.2 12.5 %collective-permute-start.5 = (f32[25,32,128]{2,1,0:T(8,128)S(1)}, f32[25,32,128]{2,1,0:T(8,128)S(1)}, u32[]{:S(2)}, u32[]{:S(2)}) collective-permute-start(f32[25,32,128]{2,1,0:T(8,128)S(1)} %get-tuple-element.18), channel_id=1, source_target_pairs={{0,1},{1,0},{2,3},{3,2},{4,5},{5,4},{6,7},{7,6},{8,9},{9,8},{10,11... | collective-permute-start | bytes 1228808 | tf_op jit(solution)/shard_map/ppermute | solution.py:482
  43.6 21.7 %collective-permute-start.6 = (f32[13,32,128]{2,1,0:T(8,128)S(1)}, f32[13,32,128]{2,1,0:T(8,128)S(1)}, u32[]{:S(2)}, u32[]{:S(2)}) collective-permute-start(f32[13,32,128]{2,1,0:T(8,128)S(1)} %collective-permute-done.2.b3_ref), channel_id=1, source_target_pairs={{1,159},{14,144},{17,143},{30,128},{33,191},{46,176},{49,175},{62,... | collective-permute-start | bytes 638984 | tf_op jit(solution)/shard_map/ppermute | solution.py:530
  44.9 20.4 %collective-permute-start.7 = (f32[12,32,128]{2,1,0:T(8,128)S(1)}, f32[12,32,128]{2,1,0:T(8,128)S(1)}, u32[]{:S(2)}, u32[]{:S(2)}) collective-permute-start(f32[12,32,128]{2,1,0:T(8,128)S(1)} %collective-permute-done.3.b4_ref), channel_id=1, source_target_pairs={{4,159},{11,144},{20,143},{27,128},{36,191},{43,176},{52,175},{59,... | collective-permute-start | bytes 589832 | tf_op jit(solution)/shard_map/ppermute | solution.py:530
  51.7 21.1 %collective-permute-start.10 = (f32[64,128]{1,0:T(8,128)S(1)}, f32[64,128]{1,0:T(8,128)S(1)}, u32[]{:S(2)}, u32[]{:S(2)}) collective-permute-start(f32[64,128]{1,0:T(8,128)S(1)} %get-tuple-element.20), channel_id=1, source_target_pairs={{256,159},{257,2},{258,1},{259,4},{260,3},{261,6},{262,5},{263,8},... | collective-permute-start | bytes 98312 | tf_op jit(solution)/shard_map/ppermute | solution.py:482
  53.0 22.2 %collective-permute-start.9 = (f32[64,128]{1,0:T(8,128)S(1)}, f32[64,128]{1,0:T(8,128)S(1)}, u32[]{:S(2)}, u32[]{:S(2)}) collective-permute-start(f32[64,128]{1,0:T(8,128)S(1)} %get-tuple-element.20), channel_id=1, source_target_pairs={{256,1},{257,0},{258,3},{259,2},{260,5},{261,4},{262,7},{263,6},{2... | collective-permute-start | bytes 98312 | tf_op jit(solution)/shard_map/ppermute | solution.py:482
  54.3 20.9 %collective-permute-start.8 = (f32[64,128]{1,0:T(8,128)S(1)}, f32[64,128]{1,0:T(8,128)S(1)}, u32[]{:S(2)}, u32[]{:S(2)}) collective-permute-start(f32[64,128]{1,0:T(8,128)S(1)} %get-tuple-element.20), channel_id=1, source_target_pairs={{256,0},{257,1},{258,2},{259,3},{260,4},{261,5},{262,6},{263,7},{2... | collective-permute-start | bytes 98312 | tf_op jit(solution)/shard_map/ppermute | solution.py:482

commit v7 on v6

--- a/solution.py
+++ b/solution.py
@@ -178,7 +178,7 @@
         pack_tiles(own_ref, layout, False, odd_ref)
 
 
-def pack_relay_kernel(own_ref, first_ref, second_ref):
+def pack_relay_kernel(own_ref, through_ref, first_ref, second_ref, out_ref):
     windows = own_ref.shape[0]
     cut = first_ref.shape[0]
     odd_place = lax.axis_index("space") % 2 == 1
@@ -198,7 +198,7 @@
         pack(False)
 
 
-def pack_lower_kernel(own_ref, b1_ref, b2_ref, b3_ref, b4_ref, even_ref, odd_ref):
+def pack_lower_kernel(own_ref, b1_ref, b2_ref, b3_ref, even_ref, odd_ref, x_ref, y_ref):
     windows = own_ref.shape[0]
 
     @pl.when(lax.axis_index("tm") < windows)
@@ -387,8 +387,6 @@
     own_ref,
     odd_ref,
     even_ref,
-    b1_ref,
-    b2_ref,
     along_x_ref,
     along_y_ref,
     out_ref,
@@ -401,6 +399,10 @@
         sent_ref[...] = sweep(
             own_ref, even_ref, odd_ref, (), along_x_ref, along_y_ref, None, out_ref, True
         )
+
+
+def pass_kernel(sent_ref, b1_ref, b2_ref, out_ref):
+    pass
 
 
 def lower_kernel(
@@ -512,14 +514,18 @@
     triangle = tiles(len(triangle_tiles(group)))
     to_even, to_odd = local_call(pack_upper_kernel, (diamond, diamond), 3)(own, along_x, along_y)
     upper_odd = exchange(to_odd, odd_mate, upper)
-    upper_even = exchange(to_even, even_mate, upper)
 
     cut = (len(triangle_tiles(group)) + 1) // 2
     halves = tiles(cut), tiles(len(triangle_tiles(group)) - cut)
-    first_half, second_half = local_call(pack_relay_kernel, halves, 1)(own)
+    first_half, second_half, to_even = local_call(
+        pack_relay_kernel, halves + (diamond,), 2, input_output_aliases={1: 2}
+    )(own, to_even)
+    upper_even = exchange(to_even, even_mate, upper)
 
     def relay(block, neighbour):
-        there = exchange(block, neighbour, lambda t, s: is_far(s) and lower(t, s))
+        return exchange(block, neighbour, lambda t, s: is_far(s) and lower(t, s))
+
+    def send_on(there, neighbour):
         pairs = []
         for t in range(group):
             for s in range(space):
@@ -527,13 +533,18 @@
                     from_t, from_s = neighbour(t, s)
                     to_t, to_s = odd_mate(t, s)
                     pairs.append((from_t * space + from_s, to_t * space + to_s))
-        return there, lax.ppermute(there, ("tm", "space"), pairs)
-
-    there_x, far_x = relay(first_half, even_mate)
-    there_y, far_y = relay(second_half, along_y_mate)
-    to_even, to_odd = local_call(
-        pack_lower_kernel, (triangle, triangle), [whole] + [anything] * 4
-    )(own, upper_odd, upper_even, there_x, there_y)
+        return lax.ppermute(there, ("tm", "space"), pairs)
+
+    there_x = relay(first_half, even_mate)
+    there_y = relay(second_half, along_y_mate)
+    to_even, to_odd, there_x, there_y = local_call(
+        pack_lower_kernel,
+        (triangle, triangle) + halves,
+        [whole, anything, whole, whole],
+        input_output_aliases={2: 2, 3: 3},
+    )(own, upper_even, there_x, there_y)
+    far_x = send_on(there_x, even_mate)
+    far_y = send_on(there_y, along_y_mate)
     lower_odd = exchange(to_odd, odd_mate, lambda t, s: lower(t, s) and not is_far(s))
     lower_even = exchange(to_even, even_mate, lower)
 
@@ -542,8 +553,14 @@
     done, sent = local_call(
         upper_kernel,
         (result_shape, flat_field),
-        [whole] * 3 + [anything] * 2 + [whole] * 2,
-    )(own, upper_odd, upper_even, lower_odd, lower_even, along_x, along_y)
+        5,
+        cost_estimate=pl.CostEstimate(
+            flops=10**10, bytes_accessed=10**6, transcendentals=0
+        ),
+    )(own, upper_odd, upper_even, along_x, along_y)
+    sent = local_call(
+        pass_kernel, flat_field, [whole, anything, anything], input_output_aliases={0: 0}
+    )(sent, lower_odd, lower_even)
     from_here = exchange(sent, same, upper, -group)
     from_even = exchange(sent, even_mate, upper, -group)
     from_odd = exchange(sent, odd_mate, upper, -group)

time: 93.5 us -> 93.2 us (level)
  starting transfers between devices: 15.4 us -> 14.2 us
    ppermute x9, starting transfers between devices: 12.8 us -> 11.7 us  [exchange(): return lax.ppermute(block, ('tm', 'space'), pairs)]
where the time goes in v7:
time: 93.2 us; the launch traced here: 92.9 us
  blocking collectives  43.5 us (47%)
  waiting for transfers between devices  29.2 us (31%)
  starting transfers between devices  14.2 us (15%)
  Pallas kernels  3.83 us (4%)
  local copies, waits for them, and re-layouts  1.86 us (2%)
    all_to_all x2, blocking collectives, within_groups(): lax.all_to_all(block, ('tm', 'space'), 0, 0, axis_index_groups=groups, ti...  43.5 us
    ppermute x9, waiting for transfers between devices, exchange(): return lax.ppermute(block, ('tm', 'space'), pairs)  18.7 us
    ppermute x9, starting transfers between devices, exchange(): return lax.ppermute(block, ('tm', 'space'), pairs)  11.7 us
    ppermute x2, waiting for transfers between devices, send_on(): return lax.ppermute(there, ('tm', 'space'), pairs)  10.5 us
    pallas_call x1, Pallas kernels, on_device(): local_call(lower_kernel, result_shape, 11, input_output_aliases={0: 0})  3.4 us
    ppermute x2, starting transfers between devices, send_on(): return lax.ppermute(there, ('tm', 'space'), pairs)  2.58 us
  transfers between devices with their start and end apart: 11, of which 5 were waited for; matrix products, arithmetic and copies ran while one was open for 0% of the time, Pallas kernels for 0%

profile of v7, /device:TPU:1, one launch (start us, length us, event | category | flops | bytes accessed | tf_op | source)
XLA Modules:
  0.0 92.9 jit_solution(16139233648729946855)
XLA Ops:
  0.0 1.0 %copy.18 = f32[2,1,8,32,128]{4,3,0,2,1:T(8,128)S(1)} copy(f32[2,1,8,32,128]{4,3,2,1,0:T(8,128)} %param.5) | data formatting | bytes 524288 | tf_op args[0]
  1.2 0.1 maximum_bitcast_fusion
  1.3 29.4 %all_to_all.10.own_ref = f32[8,6,32,128]{3,2,1,0:T(8,128)S(1)} all-to-all(f32[8,6,32,128]{3,2,1,0:T(8,128)S(1)} %maximum_bitcast_fusion), channel_id=1, replica_groups={{0,32,64,96,128,160,192,224},{256,288,320,352,384,416,448,480},{1,33,65..., dimensions={0} | all-to-all | bytes 1572864 | tf_op jit(solution)/shard_map/all_to_all | solution.py:496
  30.6 0.2 shard_map.56
  30.8 0.7 collective-permute-start.1
  31.5 0.7 collective-permute-start
  32.2 1.3 %collective-permute-start.2 = (f32[13,32,128]{2,1,0:T(8,128)S(1)}, f32[13,32,128]{2,1,0:T(8,128)S(1)}, u32[]{:S(2)}, u32[]{:S(2)}) collective-permute-start(f32[13,32,128]{2,1,0:T(8,128)S(1)} %get-tuple-element.20), channel_id=1, source_target_pairs={{0,1},{15,14},{16,17},{31,30},{32,33},{47,46},{48,49},{63,62},{64,... | collective-permute-start | bytes 638984 | tf_op jit(solution)/shard_map/ppermute | solution.py:484
  33.5 1.3 %collective-permute-start.3 = (f32[12,32,128]{2,1,0:T(8,128)S(1)}, f32[12,32,128]{2,1,0:T(8,128)S(1)}, u32[]{:S(2)}, u32[]{:S(2)}) collective-permute-start(f32[12,32,128]{2,1,0:T(8,128)S(1)} %get-tuple-element.21), channel_id=1, source_target_pairs={{0,4},{15,11},{16,20},{31,27},{32,36},{47,43},{48,52},{63,59},{64,... | collective-permute-start | bytes 589832 | tf_op jit(solution)/shard_map/ppermute | solution.py:484
  34.8 3.4 %collective-permute-done.3.b3_ref = f32[12,32,128]{2,1,0:T(8,128)S(1)} collective-permute-done((f32[12,32,128]{2,1,0:T(8,128)S(1)}, f32[12,32,128]{2,1,0:T(8,128)S(1)}, u32[]{:S(2)}, u32[]{:S(2)}) %collective-permute-start.3) | collective-permute-done | bytes 196640 | tf_op jit(solution)/shard_map/ppermute | solution.py:484
  38.2 0.3 shard_map.58
  38.5 3.1 %collective-permute-start.4 = (f32[25,32,128]{2,1,0:T(8,128)S(1)}, f32[25,32,128]{2,1,0:T(8,128)S(1)}, u32[]{:S(2)}, u32[]{:S(2)}) collective-permute-start(f32[25,32,128]{2,1,0:T(8,128)S(1)} %get-tuple-element.22), channel_id=1, source_target_pairs={{0,1},{1,0},{2,3},{3,2},{4,5},{5,4},{6,7},{7,6},{8,9},{9,8},{10,11... | collective-permute-start | bytes 1228808 | tf_op jit(solution)/shard_map/ppermute | solution.py:484
  41.6 0.7 collective-permute-start.5
  42.3 1.3 %collective-permute-start.6 = (f32[13,32,128]{2,1,0:T(8,128)S(1)}, f32[13,32,128]{2,1,0:T(8,128)S(1)}, u32[]{:S(2)}, u32[]{:S(2)}) collective-permute-start(f32[13,32,128]{2,1,0:T(8,128)S(1)} %get-tuple-element.24), channel_id=1, source_target_pairs={{1,159},{14,144},{17,143},{30,128},{33,191},{46,176},{49,175},{62,... | collective-permute-start | bytes 638984 | tf_op jit(solution)/shard_map/ppermute | solution.py:536
  43.6 1.3 %collective-permute-start.7 = (f32[12,32,128]{2,1,0:T(8,128)S(1)}, f32[12,32,128]{2,1,0:T(8,128)S(1)}, u32[]{:S(2)}, u32[]{:S(2)}) collective-permute-start(f32[12,32,128]{2,1,0:T(8,128)S(1)} %get-tuple-element.25), channel_id=1, source_target_pairs={{4,159},{11,144},{20,143},{27,128},{36,191},{43,176},{52,175},{59,... | collective-permute-start | bytes 589832 | tf_op jit(solution)/shard_map/ppermute | solution.py:536
  45.0 4.7 %collective-permute-done.4.b2_ref.even_ref = f32[25,32,128]{2,1,0:T(8,128)S(1)} collective-permute-done((f32[25,32,128]{2,1,0:T(8,128)S(1)}, f32[25,32,128]{2,1,0:T(8,128)S(1)}, u32[]{:S(2)}, u32[]{:S(2)}) %collective-permute-start.4) | collective-permute-done | bytes 409632 | tf_op jit(solution)/shard_map/ppermute | solution.py:484
  49.6 1.3 %collective-permute-start.10 = (f32[64,128]{1,0:T(8,128)S(1)}, f32[64,128]{1,0:T(8,128)S(1)}, u32[]{:S(2)}, u32[]{:S(2)}) collective-permute-start(f32[64,128]{1,0:T(8,128)S(1)} %shard_map.59), channel_id=1, source_target_pairs={{256,159},{257,2},{258,1},{259,4},{260,3},{261,6},{262,5},{263,8},... | collective-permute-start | bytes 98312 | tf_op jit(solution)/shard_map/ppermute | solution.py:484
  50.9 1.3 %collective-permute-start.8 = (f32[64,128]{1,0:T(8,128)S(1)}, f32[64,128]{1,0:T(8,128)S(1)}, u32[]{:S(2)}, u32[]{:S(2)}) collective-permute-start(f32[64,128]{1,0:T(8,128)S(1)} %shard_map.59), channel_id=1, source_target_pairs={{256,0},{257,1},{258,2},{259,3},{260,4},{261,5},{262,6},{263,7},{2... | collective-permute-start | bytes 98312 | tf_op jit(solution)/shard_map/ppermute | solution.py:484
  52.2 1.3 %collective-permute-start.9 = (f32[64,128]{1,0:T(8,128)S(1)}, f32[64,128]{1,0:T(8,128)S(1)}, u32[]{:S(2)}, u32[]{:S(2)}) collective-permute-start(f32[64,128]{1,0:T(8,128)S(1)} %shard_map.59), channel_id=1, source_target_pairs={{256,1},{257,0},{258,3},{259,2},{260,5},{261,4},{262,7},{263,6},{2... | collective-permute-start | bytes 98312 | tf_op jit(solution)/shard_map/ppermute | solution.py:484
  53.5 10.5 %collective-permute-done.7.far_y_ref = f32[12,32,128]{2,1,0:T(8,128)S(1)} collective-permute-done((f32[12,32,128]{2,1,0:T(8,128)S(1)}, f32[12,32,128]{2,1,0:T(8,128)S(1)}, u32[]{:S(2)}, u32[]{:S(2)}) %collective-permute-start.7) | collective-permute-done | bytes 196640 | tf_op jit(solution)/shard_map/ppermute | solution.py:536
  64.0 8.8 %collective-permute-done.10.po_ref = f32[64,128]{1,0:T(8,128)S(1)} collective-permute-done((f32[64,128]{1,0:T(8,128)S(1)}, f32[64,128]{1,0:T(8,128)S(1)}, u32[]{:S(2)}, u32[]{:S(2)}) %collective-permute-start.10) | collective-permute-done | bytes 32800 | tf_op jit(solution)/shard_map/ppermute | solution.py:484
  72.8 1.8 %collective-permute-done.9.pe_ref = f32[64,128]{1,0:T(8,128)S(1)} collective-permute-done((f32[64,128]{1,0:T(8,128)S(1)}, f32[64,128]{1,0:T(8,128)S(1)}, u32[]{:S(2)}, u32[]{:S(2)}) %collective-permute-start.9) | collective-permute-done | bytes 32800 | tf_op jit(solution)/shard_map/ppermute | solution.py:484
  74.6 3.4 %shard_map.60 = f32[8,2,32,128]{3,2,1,0:T(8,128)S(1)} custom-call(f32[8,2,32,128]{3,2,1,0:T(8,128)S(1)} %get-tuple-element.19.done_ref, f32[8,6,32,128]{3,2,1,0:T(8,128)S(1)} %all_to_all.10.own_ref, f32[25,32,128]{2,1,0:T(8,128)S(1)} %collective-permute-done.4.b2_ref.even_ref, ...), custom_call_target="tpu_custom_call", output_to_operand_aliasing={{}: (0, {})} | custom-call | tf_op jit(solution)/shard_map/pallas_call | solution.py:567
  78.0 14.2 %all_to_all.11 = f32[8,2,32,128]{3,2,1,0:T(8,128)S(1)} all-to-all(f32[8,2,32,128]{3,2,1,0:T(8,128)S(1)} %shard_map.60), channel_id=1, replica_groups={{0,32,64,96,128,160,192,224},{256,288,320,352,384,416,448,480},{1,33,65..., dimensions={0} | all-to-all | bytes 524288 | tf_op jit(solution)/shard_map/all_to_all | solution.py:496
  92.1 0.7 copy.14
  (18 shorter events, 0.2 us)
Async XLA Ops:
  0.0 1.0 %copy-start.3 = (f32[1,2,8,32,128]{4,3,2,1,0:T(8,128)S(1)}, f32[1,2,8,32,128]{4,3,2,1,0:T(8,128)}, u32[]{:S(2)}) copy-start(f32[1,2,8,32,128]{4,3,2,1,0:T(8,128)} %param.6) | copy-start | bytes 786436
  0.0 1.1 %copy-start.2 = (f32[1,2,8,32,128]{4,3,2,1,0:T(8,128)S(1)}, f32[1,2,8,32,128]{4,3,2,1,0:T(8,128)}, u32[]{:S(2)}) copy-start(f32[1,2,8,32,128]{4,3,2,1,0:T(8,128)} %param.7) | copy-start | bytes 786436
  1.2 29.4 %copy-start = (bf16[256,256]{1,0:T(8,128)(2,1)S(1)}, bf16[256,256]{1,0:T(8,128)(2,1)}, u32[]{:S(2)}) copy-start(bf16[256,256]{1,0:T(8,128)(2,1)} %constant.4.clone.along_x_ref) | copy-start | bytes 393220
  1.2 29.4 %copy-start.1 = (f32[8,8,128]{2,1,0:T(8,128)S(1)}, f32[8,8,128]{2,1,0:T(8,128)}, u32[]{:S(2)}) copy-start(f32[8,8,128]{2,1,0:T(8,128)} %constant.5.clone.along_y_ref) | copy-start | bytes 98308
  30.8 7.4 %collective-permute-start.1 = (f32[14,32,128]{2,1,0:T(8,128)S(1)}, f32[14,32,128]{2,1,0:T(8,128)S(1)}, u32[]{:S(2)}, u32[]{:S(2)}) collective-permute-start(f32[14,32,128]{2,1,0:T(8,128)S(1)} %get-tuple-element.18), channel_id=1, source_target_pairs={{256,257},{257,256},{258,259},{259,258},{260,261},{261,260},{262,2... | collective-permute-start | bytes 688136 | tf_op jit(solution)/shard_map/ppermute | solution.py:484
  31.5 13.4 %collective-permute-start = (f32[14,32,128]{2,1,0:T(8,128)S(1)}, f32[14,32,128]{2,1,0:T(8,128)S(1)}, u32[]{:S(2)}, u32[]{:S(2)}) collective-permute-start(f32[14,32,128]{2,1,0:T(8,128)S(1)} %get-tuple-element.16), channel_id=1, source_target_pairs={{256,415},{257,258},{258,257},{259,260},{260,259},{261,262},{262,2... | collective-permute-start | bytes 688136 | tf_op jit(solution)/shard_map/ppermute | solution.py:484
  32.2 6.0 %collective-permute-start.2 = (f32[13,32,128]{2,1,0:T(8,128)S(1)}, f32[13,32,128]{2,1,0:T(8,128)S(1)}, u32[]{:S(2)}, u32[]{:S(2)}) collective-permute-start(f32[13,32,128]{2,1,0:T(8,128)S(1)} %get-tuple-element.20), channel_id=1, source_target_pairs={{0,1},{15,14},{16,17},{31,30},{32,33},{47,46},{48,49},{63,62},{64,... | collective-permute-start | bytes 638984 | tf_op jit(solution)/shard_map/ppermute | solution.py:484
  33.5 4.7 %collective-permute-start.3 = (f32[12,32,128]{2,1,0:T(8,128)S(1)}, f32[12,32,128]{2,1,0:T(8,128)S(1)}, u32[]{:S(2)}, u32[]{:S(2)}) collective-permute-start(f32[12,32,128]{2,1,0:T(8,128)S(1)} %get-tuple-element.21), channel_id=1, source_target_pairs={{0,4},{15,11},{16,20},{31,27},{32,36},{47,43},{48,52},{63,59},{64,... | collective-permute-start | bytes 589832 | tf_op jit(solution)/shard_map/ppermute | solution.py:484
  38.5 11.2 %collective-permute-start.4 = (f32[25,32,128]{2,1,0:T(8,128)S(1)}, f32[25,32,128]{2,1,0:T(8,128)S(1)}, u32[]{:S(2)}, u32[]{:S(2)}) collective-permute-start(f32[25,32,128]{2,1,0:T(8,128)S(1)} %get-tuple-element.22), channel_id=1, source_target_pairs={{0,1},{1,0},{2,3},{3,2},{4,5},{5,4},{6,7},{7,6},{8,9},{9,8},{10,11... | collective-permute-start | bytes 1228808 | tf_op jit(solution)/shard_map/ppermute | solution.py:484
  41.6 8.0 %collective-permute-start.5 = (f32[25,32,128]{2,1,0:T(8,128)S(1)}, f32[25,32,128]{2,1,0:T(8,128)S(1)}, u32[]{:S(2)}, u32[]{:S(2)}) collective-permute-start(f32[25,32,128]{2,1,0:T(8,128)S(1)} %get-tuple-element.23), channel_id=1, source_target_pairs={{1,2},{2,1},{3,4},{4,3},{5,6},{6,5},{7,8},{8,7},{9,10},{10,9},{11,... | collective-permute-start | bytes 1228808 | tf_op jit(solution)/shard_map/ppermute | solution.py:484
  42.3 21.7 %collective-permute-start.6 = (f32[13,32,128]{2,1,0:T(8,128)S(1)}, f32[13,32,128]{2,1,0:T(8,128)S(1)}, u32[]{:S(2)}, u32[]{:S(2)}) collective-permute-start(f32[13,32,128]{2,1,0:T(8,128)S(1)} %get-tuple-element.24), channel_id=1, source_target_pairs={{1,159},{14,144},{17,143},{30,128},{33,191},{46,176},{49,175},{62,... | collective-permute-start | bytes 638984 | tf_op jit(solution)/shard_map/ppermute | solution.py:536
  43.6 20.4 %collective-permute-start.7 = (f32[12,32,128]{2,1,0:T(8,128)S(1)}, f32[12,32,128]{2,1,0:T(8,128)S(1)}, u32[]{:S(2)}, u32[]{:S(2)}) collective-permute-start(f32[12,32,128]{2,1,0:T(8,128)S(1)} %get-tuple-element.25), channel_id=1, source_target_pairs={{4,159},{11,144},{20,143},{27,128},{36,191},{43,176},{52,175},{59,... | collective-permute-start | bytes 589832 | tf_op jit(solution)/shard_map/ppermute | solution.py:536
  49.6 23.1 %collective-permute-start.10 = (f32[64,128]{1,0:T(8,128)S(1)}, f32[64,128]{1,0:T(8,128)S(1)}, u32[]{:S(2)}, u32[]{:S(2)}) collective-permute-start(f32[64,128]{1,0:T(8,128)S(1)} %shard_map.59), channel_id=1, source_target_pairs={{256,159},{257,2},{258,1},{259,4},{260,3},{261,6},{262,5},{263,8},... | collective-permute-start | bytes 98312 | tf_op jit(solution)/shard_map/ppermute | solution.py:484
  50.9 21.9 %collective-permute-start.8 = (f32[64,128]{1,0:T(8,128)S(1)}, f32[64,128]{1,0:T(8,128)S(1)}, u32[]{:S(2)}, u32[]{:S(2)}) collective-permute-start(f32[64,128]{1,0:T(8,128)S(1)} %shard_map.59), channel_id=1, source_target_pairs={{256,0},{257,1},{258,2},{259,3},{260,4},{261,5},{262,6},{263,7},{2... | collective-permute-start | bytes 98312 | tf_op jit(solution)/shard_map/ppermute | solution.py:484
  52.2 22.3 %collective-permute-start.9 = (f32[64,128]{1,0:T(8,128)S(1)}, f32[64,128]{1,0:T(8,128)S(1)}, u32[]{:S(2)}, u32[]{:S(2)}) collective-permute-start(f32[64,128]{1,0:T(8,128)S(1)} %shard_map.59), channel_id=1, source_target_pairs={{256,1},{257,0},{258,3},{259,2},{260,5},{261,4},{262,7},{263,6},{2... | collective-permute-start | bytes 98312 | tf_op jit(solution)/shard_map/ppermute | solution.py:484
